TPU v7x, 128 devices: a whole 4x4x4 slice. The times are simulated.
128 devices in a mesh: space: 16 (over z_hi, x, core), chan: 8 (over z_lo, y).
Axes of the slice: x: 4, y: 4, z: 4 (z_hi: 2, z_lo: 2; z = z_hi * 2 + z_lo), core: 2. Of those that a mesh axis runs over, the one named last changes fastest.
Arguments:
- activation: bfloat16 [96, 128, 1024], P('space', 'chan'), may hold values from -6 to 6
- cotangent: bfloat16 [96, 128, 1024], P('space', 'chan'), may hold values from -6 to 6
- kernel: bfloat16 [3, 3, 3, 128, 128], P(None, None, None, None, 'chan'), may hold values from -0.109375 to 0.109375
Outputs:
- output: bfloat16 [96, 128, 1024], P('space', 'chan')
- grad_input: bfloat16 [96, 128, 1024], P('space', 'chan')
- grad_kernel: float32 [3, 3, 3, 128, 128], P(None, None, None, None, 'chan')
All inputs are finite; a program needn't handle non-finite values.
Results may differ from a plain program's by a relative error of at most 0.0029.
Values may be sent and summed in bfloat16 or wider, within the bound.
No kernel may reach another device: no remote copies, remote signals or barrier semaphores. Data moves between devices by JAX's collectives and lax.ppermute only.
A program may use at most 64 MiB of HBM per device.

v0:
```python
import functools

import jax
import jax.numpy as jnp
from jax import lax
from jax.experimental import pallas as pl
from jax.experimental.pallas import tpu as pltpu
from jax.sharding import Mesh, PartitionSpec as P

NXY = 32
CELLS = NXY * NXY
C = 128
N = 6
SPACE = ("zh", "x", "core")
CHAN = ("zl", "y")
BF = jnp.bfloat16
F32 = jnp.float32
VMEM_LIMIT = 56 * 1024 * 1024
VM = pl.BlockSpec(memory_space=pltpu.VMEM)
KEYS = [(0, 0), (0, 1), (0, 2), (0, 3), (1, 0), (1, 1), (1, 2), (1, 3)]


def swap(v, axis, bits):
    return lax.ppermute(v, axis, [(i, i ^ bits) for i in range(lax.axis_size(axis))])


def outer_swap(v):
    pairs = []
    for i in range(1, 16, 2):
        j = (i + 1) % 16
        pairs += [(i, j), (j, i)]
    return lax.ppermute(v, SPACE, pairs)


def after(v, *deps):
    return lax.optimization_barrier((v,) + deps)[0]


def group(key):
    return (lax.axis_index("zl") ^ key[0]) * 4 + (lax.axis_index("y") ^ key[1])


def first_row(key):
    return pl.multiple_of(group(key) * 16, 16)


def lane_y():
    return lax.broadcasted_iota(jnp.int32, (16, CELLS), 1) % NXY


def from_y_before(v, y):
    return jnp.where(y == 0, pltpu.roll(v, CELLS - (NXY - 1), 1), pltpu.roll(v, 1, 1))


def from_y_after(v, y):
    return jnp.where(y == NXY - 1, pltpu.roll(v, NXY - 1, 1), pltpu.roll(v, CELLS - 1, 1))


def assemble(blocks, field, absolute, pair):
    for n, (key, (ref, start)) in enumerate(zip(KEYS, blocks)):
        row = first_row(key) if absolute else n * 16
        for z in (2 * pair, 2 * pair + 1):
            field[z, pl.ds(row, 16), :] = ref[start + z]


def pack_filter_body(k_ref, near, far, turned):
    turned[:, 0:432] = jnp.transpose(k_ref[...].astype(F32))
    turned[:, 432:512] = jnp.zeros((C, 80), F32)
    for ry in range(4):
        near[pl.ds(ry * 16, 16), :] = turned[pl.ds(first_row((0, ry)), 16), :].astype(BF)
        far[pl.ds(ry * 16, 16), :] = turned[pl.ds(first_row((1, ry)), 16), :].astype(BF)


def unpack_filter_body(near, far, got1, got3, w_ref):
    lane = lax.broadcasted_iota(jnp.int32, (16, C), 1) // 16
    pieces = {
        (0, 0): near[0:16],
        (1, 0): far[0:16],
        (0, 1): got1[0:16],
        (1, 1): got1[32:48],
        (0, 2): got3[0:16],
        (0, 3): got3[16:32],
        (1, 2): got3[32:48],
        (1, 3): got3[48:64],
    }
    pieces = {k: v.astype(F32) for k, v in pieces.items()}
    for tap in range(27):
        tile, spot = divmod(tap * 16, C)
        row = jnp.zeros((16, C), F32)
        for n, key in enumerate(KEYS):
            v = pieces[key][:, tile * C : (tile + 1) * C]
            move = (n * 16 - spot) % C
            v = v if move == 0 else pltpu.roll(v, move, 1)
            row = jnp.where(lane == n, v, row)
        w_ref[pl.ds((26 - tap) * 16, 16), :] = row.astype(BF)


def gk_body(*refs):
    units, (g, g_in, g_out), (out,), (field, g9) = refs[:8], refs[8:11], refs[11:12], refs[12:]
    core = lax.axis_index("core")
    y = lane_y()
    for p in range(N + 2):
        if p == 0:
            plane = jnp.where(core == 0, g_out[0].astype(F32), g_in[0].astype(F32))
        elif p == N + 1:
            plane = jnp.where(core == 0, g_in[0].astype(F32), g_out[0].astype(F32))
        else:
            plane = g[p - 1].astype(F32)
        slot = N + 1 - p
        for c, v in enumerate((from_y_after(plane, y), plane, from_y_before(plane, y))):
            for b, w in enumerate((pltpu.roll(v, CELLS - NXY, 1), v, pltpu.roll(v, NXY, 1))):
                g9[pl.ds(slot * 144 + (b * 3 + c) * 16, 16), :] = w.astype(BF)
    for pair in range(N // 2):
        assemble([(u, 0) for u in units], field, True, pair)
        z = 2 * pair
        lhs = g9[pl.ds((N - 2 - z) * 144, 576), :]
        rhs = field[pl.ds(z, 2)].reshape(2 * C, CELLS)
        term = lax.dot_general(lhs, rhs, (((1,), (1,)), ((), ())), preferred_element_type=F32)
        term = term[144:576, 0:C] + term[0:432, C : 2 * C]
        if pair == 0:
            out[...] = term
        else:
            out[...] += term


def conv_planes(blocks, absolute, field, w, carry, out_ref, edge):
    y = lane_y()
    w0, w1, w2 = (w[pl.ds(a * 144, 144), :] for a in range(3))
    none = jnp.zeros((144, C), BF)
    lhs = jnp.concatenate(
        [jnp.concatenate(row, axis=1) for row in ((w2, none), (w1, w2), (w0, w1), (none, w0))], axis=0
    )
    beyond = []
    for pair in range(N // 2):
        assemble(blocks, field, absolute, pair)
        rhs = field[pl.ds(2 * pair, 2)].reshape(2 * C, CELLS)
        terms = jnp.dot(lhs, rhs, preferred_element_type=F32)
        last = pair == N // 2 - 1
        for n in range(4):
            z = 2 * pair - 1 + n
            t = terms[n * 144 : n * 144 + 144]
            if n < 2 and pair > 0:
                t = t + carry[pl.ds(n * 144, 144), :]
            if n >= 2 and not last:
                carry[pl.ds((n - 2) * 144, 144), :] = t
                continue
            s = t[48:96] + pltpu.roll(t[0:48], NXY, 1) + pltpu.roll(t[96:144], CELLS - NXY, 1)
            out = s[16:32] + from_y_before(s[0:16], y) + from_y_after(s[32:48], y)
            if z in (-1, N):
                beyond.append(out)
            elif z in (0, N - 1):
                edge[0 if z == 0 else 1] = out
            else:
                out_ref[z] = out.astype(BF)
    out_ref[0] = jnp.zeros((16, CELLS), BF)
    out_ref[N - 1] = jnp.zeros((16, CELLS), BF)
    return beyond


def output_body(*refs):
    units, w, (out_ref, edge, inner, outer), (field, carry) = refs[:8], refs[8], refs[9:13], refs[13:]
    before, behind = conv_planes([(u, 0) for u in units], True, field, w, carry, out_ref, edge)
    first = lax.axis_index("core") == 0
    inner[...] = jnp.where(first, behind, before)
    outer[...] = jnp.where(first, before, behind)


def grad_input_body(*refs):
    units, (w, inner0, outer0), (out_ref, edge, inner, outer), (field, carry) = refs[:8], refs[8:11], refs[11:15], refs[15:]
    starts = [0 if key in ((0, 0), (1, 2)) else N for key in KEYS]
    inner[0] = inner0[...]
    outer[0] = outer0[...]
    before, behind = conv_planes(list(zip(units, starts)), False, field, w, carry, out_ref, edge)
    first = lax.axis_index("core") == 0
    inner[1] = jnp.where(first, behind, before)
    outer[1] = jnp.where(first, before, behind)


def finish_body(o_in, o_edge, g_in, g_edge, inner, outer, o_ref, g_ref):
    first = lax.axis_index("core") == 0
    for n, (src, edge, dst) in enumerate(((o_in, o_edge, o_ref), (g_in, g_edge, g_ref))):
        dst[pl.ds(1, N - 2)] = src[pl.ds(1, N - 2)]
        low = jnp.where(first, outer[n], inner[n])
        high = jnp.where(first, inner[n], outer[n])
        dst[0] = (edge[0] + low).astype(BF)
        dst[N - 1] = (edge[1] + high).astype(BF)


def call(body, name, args, specs, outs, scratch=(), flops=0, size=1 << 20):
    return pl.pallas_call(
        body,
        out_shape=[jax.ShapeDtypeStruct(s, d) for s, d in outs],
        in_specs=specs,
        out_specs=[VM] * len(outs),
        scratch_shapes=list(scratch),
        compiler_params=pltpu.CompilerParams(vmem_limit_bytes=VMEM_LIMIT),
        cost_estimate=pl.CostEstimate(flops=flops, bytes_accessed=size, transcendentals=0),
        name=name,
    )(*args)


CONV_FLOPS = 2 * 432 * C * CELLS * N
FIELD = [pltpu.VMEM((N, C, CELLS), BF)]


def on_device(activation, cotangent, kernel):
    core = lax.axis_index("core")
    kt = jnp.swapaxes(kernel, 3, 4).reshape(432, C)

    own = jnp.concatenate([activation, cotangent], axis=0)
    k1 = swap(own, "y", 1)
    z0 = swap(own, "zl", 1)
    k3 = swap(own, "y", 3)
    g_in = swap(jnp.where(core == 0, cotangent[N - 1 :], cotangent[:1]), "core", 1)
    g_out = outer_swap(jnp.where(core == 0, cotangent[:1], cotangent[N - 1 :]))
    k2 = swap(k1, "y", 3)
    z1 = swap(z0, "y", 1)
    z3 = swap(k3, "zl", 1)
    z2a = swap(k2[:N], "zl", 1)
    z2g = swap(z3[N:], "y", 1)

    near, far = call(
        pack_filter_body, "pack_filter", [kt], [VM], [((64, 512), BF)] * 2, [pltpu.VMEM((C, 512), F32)]
    )
    far = swap(after(far, k1, z0, k3, g_out), "zl", 1)
    got1 = swap(jnp.concatenate([near[16:48], far[16:48]]), "y", 1)
    got3 = swap(after(jnp.concatenate([got1[16:32], near[48:64], got1[48:64], far[48:64]]), k2), "y", 3)
    w_in = call(
        unpack_filter_body,
        "unpack_filter",
        [near, far, got1, got3],
        [VM] * 4,
        [((432, C), BF)],
    )[0]

    activation = after(activation, got3)
    a_units = [activation, k1, k2, k3, z0, z1, z2a, z3]
    g_units = [cotangent, k1, k2, k3, z0, z1, z2g, z3]
    terms = call(
        gk_body,
        "grad_kernel_terms",
        [*a_units, cotangent, g_in, g_out],
        [VM] * 8 + [VM] * 3,
        [((432, C), F32)],
        FIELD + [pltpu.VMEM(((N + 2) * 144, CELLS), BF)],
        CONV_FLOPS,
        4 << 20,
    )[0]
    terms = terms + swap(terms, "core", 1)
    got = swap(terms, "x", 1)

    conv_outs = [((N, 16, CELLS), BF), ((2, 16, CELLS), F32)]
    conv_scratch = FIELD + [pltpu.VMEM((288, CELLS), F32)]
    a_units[0] = after(activation, terms)
    out0, edge0, inner0, outer0 = call(
        output_body,
        "output_planes",
        [*a_units, kt],
        [VM] * 8 + [VM],
        conv_outs + [((16, CELLS), F32)] * 2,
        conv_scratch,
        CONV_FLOPS,
        4 << 20,
    )
    terms = after(terms, edge0, w_in) + got
    got = swap(terms, "x", 3)
    g_units[0] = after(cotangent, terms)
    out1, edge1, inner, outer = call(
        grad_input_body,
        "grad_input_planes",
        [*g_units, w_in, inner0, outer0],
        [VM] * 8 + [VM] * 3,
        conv_outs + [((2, 16, CELLS), F32)] * 2,
        conv_scratch,
        CONV_FLOPS,
        4 << 20,
    )
    outer = outer_swap(outer)
    inner = swap(inner, "core", 1)
    terms = (after(terms, edge1) + got).astype(BF)
    terms = terms.astype(F32) + swap(terms, "zh", 1).astype(F32)
    output, grad_input = call(
        finish_body,
        "finish_planes",
        [out0, edge0, out1, edge1, inner, outer],
        [VM] * 6,
        [((N, 16, CELLS), BF)] * 2,
    )
    grad_kernel = jnp.swapaxes((terms * 98304.0**-0.5).reshape(3, 3, 3, 16, C), 3, 4)
    return (output, grad_input, grad_kernel)


def solution(mesh):
    fine = Mesh(mesh.devices.reshape(2, 4, 2, 2, 4), SPACE + CHAN)
    field = P(SPACE, CHAN, None)
    filt = P(None, None, None, None, CHAN)
    return jax.shard_map(
        on_device,
        mesh=fine,
        in_specs=(field, field, filt),
        out_specs=(field, field, filt),
        check_vma=False,
    )
```

profile of v0, /device:TPU:1, one launch (start us, length us, event | category | flops | bytes accessed | tf_op | source)
XLA Modules:
  0.0 75.6 jit_solution(204747251320116853)
XLA Ops:
  1.7 2.2 %collective-permute-start = (bf16[12,16,1024]{2,1,0:T(8,128)(2,1)S(1)}, bf16[12,16,1024]{2,1,0:T(8,128)(2,1)S(1)}, u32[]{:S(2)}, u32[]{:S(2)}) collective-permute-start(bf16[12,16,1024]{2,1,0:T(8,128)(2,1)S(1)} %constant_dynamic-update-slice_fusion), channel_id=1, source_target_pairs={{0,1},{1,0},{2,3},{3,2},{4,5},{5,4},{6,7},{7,6},{8,9},{9,8},{10,11... | collective-permute-start | bytes 1179656 | tf_op jit(solution)/shard_map/ppermute | solution.py:24
  3.9 1.9 %collective-permute-start.2 = (bf16[12,16,1024]{2,1,0:T(8,128)(2,1)S(1)}, bf16[12,16,1024]{2,1,0:T(8,128)(2,1)S(1)}, u32[]{:S(2)}, u32[]{:S(2)}) collective-permute-start(bf16[12,16,1024]{2,1,0:T(8,128)(2,1)S(1)} %constant_dynamic-update-slice_fusion), channel_id=1, source_target_pairs={{0,3},{1,2},{2,1},{3,0},{4,7},{5,6},{6,5},{7,4},{8,11},{9,10},{10,... | collective-permute-start | bytes 1179656 | tf_op jit(solution)/shard_map/ppermute | solution.py:24
  5.8 1.6 %collective-permute-start.1 = (bf16[12,16,1024]{2,1,0:T(8,128)(2,1)S(1)}, bf16[12,16,1024]{2,1,0:T(8,128)(2,1)S(1)}, u32[]{:S(2)}, u32[]{:S(2)}) collective-permute-start(bf16[12,16,1024]{2,1,0:T(8,128)(2,1)S(1)} %constant_dynamic-update-slice_fusion), channel_id=1, source_target_pairs={{0,4},{4,0},{1,5},{5,1},{2,6},{6,2},{3,7},{7,3},{8,12},{12,8},{9,1... | collective-permute-start | bytes 1179656 | tf_op jit(solution)/shard_map/ppermute | solution.py:24
  7.4 4.9 %collective-permute-done.refs_1_ = bf16[12,16,1024]{2,1,0:T(8,128)(2,1)S(1)} collective-permute-done((bf16[12,16,1024]{2,1,0:T(8,128)(2,1)S(1)}, bf16[12,16,1024]{2,1,0:T(8,128)(2,1)S(1)}, u32[]{:S(2)}, u32[]{:S(2)}) %collective-permute-start) | collective-permute-done | bytes 393248 | tf_op jit(solution)/shard_map/ppermute | solution.py:24
  12.3 3.0 %collective-permute-start.6 = (bf16[12,16,1024]{2,1,0:T(8,128)(2,1)S(1)}, bf16[12,16,1024]{2,1,0:T(8,128)(2,1)S(1)}, u32[]{:S(2)}, u32[]{:S(2)}) collective-permute-start(bf16[12,16,1024]{2,1,0:T(8,128)(2,1)S(1)} %collective-permute-done.refs_1_), channel_id=1, source_target_pairs={{0,3},{1,2},{2,1},{3,0},{4,7},{5,6},{6,5},{7,4},{8,11},{9,10},{10,... | collective-permute-start | bytes 1179656 | tf_op jit(solution)/shard_map/ppermute | solution.py:24
  15.3 3.0 %collective-permute-start.3 = (bf16[1,16,1024]{2,1,0:T(8,128)(2,1)S(1)}, bf16[1,16,1024]{2,1,0:T(8,128)(2,1)S(1)}, u32[]{:S(2)}, u32[]{:S(2)}) collective-permute-start(bf16[1,16,1024]{2,1,0:T(8,128)(2,1)S(1)} %get-tuple-element.42), channel_id=1, source_target_pairs={{8,16},{16,8},{24,32},{32,24},{40,48},{48,40},{56,64},{64,56},{72,... | collective-permute-start | bytes 98312 | tf_op jit(solution)/shard_map/ppermute | solution.py:32
  18.3 1.7 %pack_filter.1 = (bf16[64,512]{1,0:T(8,128)(2,1)}, bf16[64,512]{1,0:T(8,128)(2,1)}) custom-call(bf16[432,128]{1,0:T(8,128)(2,1)} %bitcast.6), custom_call_target="tpu_custom_call" | custom-call | bytes 1048576 | tf_op jit(solution)/shard_map/pack_filter/pallas_call | solution.py:190
  20.2 1.7 %collective-permute-start.4 = (bf16[64,512]{1,0:T(8,128)(2,1)}, bf16[64,512]{1,0:T(8,128)(2,1)S(1)}, u32[]{:S(2)}, u32[]{:S(2)}) collective-permute-start(bf16[64,512]{1,0:T(8,128)(2,1)} %get-tuple-element.24), channel_id=1, source_target_pairs={{0,4},{4,0},{1,5},{5,1},{2,6},{6,2},{3,7},{7,3},{8,12},{12,8},{9,1... | collective-permute-start | bytes 196616 | tf_op jit(solution)/shard_map/ppermute | solution.py:24
  22.7 1.4 %collective-permute-done.4.far = bf16[64,512]{1,0:T(8,128)(2,1)S(1)} collective-permute-done((bf16[64,512]{1,0:T(8,128)(2,1)}, bf16[64,512]{1,0:T(8,128)(2,1)S(1)}, u32[]{:S(2)}, u32[]{:S(2)}) %collective-permute-start.4) | collective-permute-done | bytes 65568 | tf_op jit(solution)/shard_map/ppermute | solution.py:24
  25.0 1.5 %collective-permute-start.10 = (bf16[12,16,1024]{2,1,0:T(8,128)(2,1)S(1)}, bf16[12,16,1024]{2,1,0:T(8,128)(2,1)S(1)}, u32[]{:S(2)}, u32[]{:S(2)}) collective-permute-start(bf16[12,16,1024]{2,1,0:T(8,128)(2,1)S(1)} %collective-permute-done.2.refs_3_), channel_id=1, source_target_pairs={{0,4},{4,0},{1,5},{5,1},{2,6},{6,2},{3,7},{7,3},{8,12},{12,8},{9,1... | collective-permute-start | bytes 1179656 | tf_op jit(solution)/shard_map/ppermute | solution.py:24
  26.4 1.4 %collective-permute-start.8 = (bf16[12,16,1024]{2,1,0:T(8,128)(2,1)S(1)}, bf16[12,16,1024]{2,1,0:T(8,128)(2,1)S(1)}, u32[]{:S(2)}, u32[]{:S(2)}) collective-permute-start(bf16[12,16,1024]{2,1,0:T(8,128)(2,1)S(1)} %collective-permute-done.1.refs_4_), channel_id=1, source_target_pairs={{0,1},{1,0},{2,3},{3,2},{4,5},{5,4},{6,7},{7,6},{8,9},{9,8},{10,11... | collective-permute-start | bytes 1179656 | tf_op jit(solution)/shard_map/ppermute | solution.py:24
  28.8 6.4 %collective-permute-start.11 = (bf16[1,16,1024]{2,1,0:T(8,128)(2,1)S(1)}, bf16[1,16,1024]{2,1,0:T(8,128)(2,1)S(1)}, u32[]{:S(2)}, u32[]{:S(2)}) collective-permute-start(bf16[1,16,1024]{2,1,0:T(8,128)(2,1)S(1)} %get-tuple-element.41), channel_id=1, source_target_pairs={{0,8},{8,0},{1,9},{9,1},{2,10},{10,2},{3,11},{11,3},{4,12},{12,4},... | collective-permute-start | bytes 98312 | tf_op jit(solution)/shard_map/ppermute | solution.py:24
  37.7 4.2 %grad_kernel_terms.1 = f32[432,128]{1,0:T(8,128)} custom-call(bf16[6,16,1024]{2,1,0:T(8,128)(2,1)} %refs_0_.1, bf16[12,16,1024]{2,1,0:T(8,128)(2,1)} %copy-done.3, bf16[12,16,1024]{2,1,0:T(8,128)(2,1)} %copy-done, bf16[12,16,1024]{2,1,0:T(8,128)(2,1)} %copy-done.4, bf16[12,16,1024]{2,1,0:T(8,128)(2,1)} %copy-done.5, bf16[12,16,1024]{2,1,0:T(8,128)(2,1)} %copy-done.6, ...), custom_call_target="tpu_custom_call" | custom-call | flops 679477248 | bytes 4194304 | tf_op jit(solution)/shard_map/grad_kernel_terms/pallas_call | solution.py:190
  41.8 4.6 %collective-permute-start.12 = (f32[432,128]{1,0:T(8,128)}, f32[432,128]{1,0:T(8,128)S(1)}, u32[]{:S(2)}, u32[]{:S(2)}) collective-permute-start(f32[432,128]{1,0:T(8,128)} %grad_kernel_terms.1), channel_id=1, source_target_pairs={{0,8},{8,0},{1,9},{9,1},{2,10},{10,2},{3,11},{11,3},{4,12},{12,4},... | collective-permute-start | bytes 663560 | tf_op jit(solution)/shard_map/ppermute | solution.py:24
  46.4 1.3 %collective-permute-done.12 = f32[432,128]{1,0:T(8,128)S(1)} collective-permute-done((f32[432,128]{1,0:T(8,128)}, f32[432,128]{1,0:T(8,128)S(1)}, u32[]{:S(2)}, u32[]{:S(2)}) %collective-permute-start.12) | collective-permute-done | bytes 221216 | tf_op jit(solution)/shard_map/ppermute | solution.py:24
  49.4 1.5 %collective-permute-start.14 = (bf16[6,16,1024]{2,1,0:T(8,128)(2,1)S(1)}, bf16[6,16,1024]{2,1,0:T(8,128)(2,1)S(1)}, u32[]{:S(2)}, u32[]{:S(2)}) collective-permute-start(bf16[6,16,1024]{2,1,0:T(8,128)(2,1)S(1)} %slice.47), channel_id=1, source_target_pairs={{0,1},{1,0},{2,3},{3,2},{4,5},{5,4},{6,7},{7,6},{8,9},{9,8},{10,11... | collective-permute-start | bytes 589832 | tf_op jit(solution)/shard_map/ppermute | solution.py:24
  50.9 1.8 %unpack_filter.1.refs_8_ = bf16[432,128]{1,0:T(8,128)(2,1)} custom-call(bf16[64,512]{1,0:T(8,128)(2,1)} %get-tuple-element.22.near, bf16[64,512]{1,0:T(8,128)(2,1)} %copy-done.9, bf16[64,512]{1,0:T(8,128)(2,1)} %copy-done.11, bf16[64,512]{1,0:T(8,128)(2,1)} %copy-done.14), custom_call_target="tpu_custom_call" | custom-call | bytes 1048576 | tf_op jit(solution)/shard_map/unpack_filter/pallas_call | solution.py:190
  52.7 4.3 %output_planes.1 = (bf16[6,16,1024]{2,1,0:T(8,128)(2,1)}, f32[2,16,1024]{2,1,0:T(8,128)}, f32[16,1024]{1,0:T(8,128)}, f32[16,1024]{1,0:T(8,128)}) custom-call(bf16[6,16,1024]{2,1,0:T(8,128)(2,1)} %refs_0_.1, bf16[12,16,1024]{2,1,0:T(8,128)(2,1)} %copy-done.3, bf16[12,16,1024]{2,1,0:T(8,128)(2,1)} %copy-done, bf16[12,16,1024]{2,1,0:T(8,128)(2,1)} %copy-done.4, ...), custom_call_target="tpu_custom_call" | custom-call | flops 679477248 | bytes 4194304 | tf_op jit(solution)/shard_map/output_planes/pallas_call | solution.py:190
  57.0 2.9 %collective-permute-start.17 = (f32[432,128]{1,0:T(8,128)S(1)}, f32[432,128]{1,0:T(8,128)S(1)}, u32[]{:S(2)}, u32[]{:S(2)}) collective-permute-start(f32[432,128]{1,0:T(8,128)S(1)} %add.13), channel_id=1, source_target_pairs={{0,48},{16,32},{32,16},{48,0},{1,49},{17,33},{33,17},{49,1},{2,50}... | collective-permute-start | bytes 663560 | tf_op jit(solution)/shard_map/ppermute | solution.py:24
  60.6 4.2 %grad_input_planes.1 = (bf16[6,16,1024]{2,1,0:T(8,128)(2,1)}, f32[2,16,1024]{2,1,0:T(8,128)}, f32[2,16,1024]{2,1,0:T(8,128)}, f32[2,16,1024]{2,1,0:T(8,128)}) custom-call(bf16[6,16,1024]{2,1,0:T(8,128)(2,1)} %refs_0_.2, bf16[12,16,1024]{2,1,0:T(8,128)(2,1)} %copy-done.3, bf16[12,16,1024]{2,1,0:T(8,128)(2,1)} %copy-done, bf16[12,16,1024]{2,1,0:T(8,128)(2,1)} %copy-done.4, ...), custom_call_target="tpu_custom_call" | custom-call | flops 679477248 | bytes 4194304 | tf_op jit(solution)/shard_map/grad_input_planes/pallas_call | solution.py:190
  65.8 1.1 %collective-permute-start.16 = (f32[2,16,1024]{2,1,0:T(8,128)}, f32[2,16,1024]{2,1,0:T(8,128)S(1)}, u32[]{:S(2)}, u32[]{:S(2)}) collective-permute-start(f32[2,16,1024]{2,1,0:T(8,128)} %get-tuple-element.37), channel_id=1, source_target_pairs={{8,16},{16,8},{24,32},{32,24},{40,48},{48,40},{56,64},{64,56},{72,... | collective-permute-start | bytes 393224 | tf_op jit(solution)/shard_map/ppermute | solution.py:32
  66.9 3.7 %collective-permute-start.18 = (bf16[432,128]{1,0:T(8,128)(2,1)S(1)}, bf16[432,128]{1,0:T(8,128)(2,1)S(1)}, u32[]{:S(2)}, u32[]{:S(2)}) collective-permute-start(bf16[432,128]{1,0:T(8,128)(2,1)S(1)} %add_convert_fusion), channel_id=1, source_target_pairs={{0,64},{64,0},{1,65},{65,1},{2,66},{66,2},{3,67},{67,3},{4,68},{68... | collective-permute-start | bytes 331784 | tf_op jit(solution)/shard_map/ppermute | solution.py:24
  71.3 2.0 %finish_planes.1 = (bf16[6,16,1024]{2,1,0:T(8,128)(2,1)}, bf16[6,16,1024]{2,1,0:T(8,128)(2,1)}) custom-call(bf16[6,16,1024]{2,1,0:T(8,128)(2,1)} %get-tuple-element.28.o_in, f32[2,16,1024]{2,1,0:T(8,128)} %get-tuple-element.29.o_edge, bf16[6,16,1024]{2,1,0:T(8,128)(2,1)} %get-tuple-element.34.g_in, f32[2,16,1024]{2,1,0:T(8,128)} %get-tuple-element.35.g_edge, ...), custom_call_target="tpu_custom_call" | custom-call | bytes 1048576 | tf_op jit(solution)/shard_map/finish_planes/pallas_call | solution.py:190
  73.3 1.5 %collective-permute-done.18 = bf16[432,128]{1,0:T(8,128)(2,1)S(1)} collective-permute-done((bf16[432,128]{1,0:T(8,128)(2,1)S(1)}, bf16[432,128]{1,0:T(8,128)(2,1)S(1)}, u32[]{:S(2)}, u32[]{:S(2)}) %collective-permute-start.18) | collective-permute-done | bytes 110624 | tf_op jit(solution)/shard_map/ppermute | solution.py:24
  (71 shorter events, 10.8 us)
Async XLA Ops:
  1.7 10.6 %collective-permute-start = (bf16[12,16,1024]{2,1,0:T(8,128)(2,1)S(1)}, bf16[12,16,1024]{2,1,0:T(8,128)(2,1)S(1)}, u32[]{:S(2)}, u32[]{:S(2)}) collective-permute-start(bf16[12,16,1024]{2,1,0:T(8,128)(2,1)S(1)} %constant_dynamic-update-slice_fusion), channel_id=1, source_target_pairs={{0,1},{1,0},{2,3},{3,2},{4,5},{5,4},{6,7},{7,6},{8,9},{9,8},{10,11... | collective-permute-start | bytes 1179656 | tf_op jit(solution)/shard_map/ppermute | solution.py:24
  3.9 16.3 %collective-permute-start.2 = (bf16[12,16,1024]{2,1,0:T(8,128)(2,1)S(1)}, bf16[12,16,1024]{2,1,0:T(8,128)(2,1)S(1)}, u32[]{:S(2)}, u32[]{:S(2)}) collective-permute-start(bf16[12,16,1024]{2,1,0:T(8,128)(2,1)S(1)} %constant_dynamic-update-slice_fusion), channel_id=1, source_target_pairs={{0,3},{1,2},{2,1},{3,0},{4,7},{5,6},{6,5},{7,4},{8,11},{9,10},{10,... | collective-permute-start | bytes 1179656 | tf_op jit(solution)/shard_map/ppermute | solution.py:24
  5.8 14.4 %collective-permute-start.1 = (bf16[12,16,1024]{2,1,0:T(8,128)(2,1)S(1)}, bf16[12,16,1024]{2,1,0:T(8,128)(2,1)S(1)}, u32[]{:S(2)}, u32[]{:S(2)}) collective-permute-start(bf16[12,16,1024]{2,1,0:T(8,128)(2,1)S(1)} %constant_dynamic-update-slice_fusion), channel_id=1, source_target_pairs={{0,4},{4,0},{1,5},{5,1},{2,6},{6,2},{3,7},{7,3},{8,12},{12,8},{9,1... | collective-permute-start | bytes 1179656 | tf_op jit(solution)/shard_map/ppermute | solution.py:24
  12.3 15.6 %copy-start.3 = (bf16[12,16,1024]{2,1,0:T(8,128)(2,1)}, bf16[12,16,1024]{2,1,0:T(8,128)(2,1)S(1)}, u32[]{:S(2)}) copy-start(bf16[12,16,1024]{2,1,0:T(8,128)(2,1)S(1)} %collective-permute-done.refs_1_) | copy-start | bytes 1179652
  12.3 15.6 %collective-permute-start.6 = (bf16[12,16,1024]{2,1,0:T(8,128)(2,1)S(1)}, bf16[12,16,1024]{2,1,0:T(8,128)(2,1)S(1)}, u32[]{:S(2)}, u32[]{:S(2)}) collective-permute-start(bf16[12,16,1024]{2,1,0:T(8,128)(2,1)S(1)} %collective-permute-done.refs_1_), channel_id=1, source_target_pairs={{0,3},{1,2},{2,1},{3,0},{4,7},{5,6},{6,5},{7,4},{8,11},{9,10},{10,... | collective-permute-start | bytes 1179656 | tf_op jit(solution)/shard_map/ppermute | solution.py:24
  15.3 4.9 %collective-permute-start.3 = (bf16[1,16,1024]{2,1,0:T(8,128)(2,1)S(1)}, bf16[1,16,1024]{2,1,0:T(8,128)(2,1)S(1)}, u32[]{:S(2)}, u32[]{:S(2)}) collective-permute-start(bf16[1,16,1024]{2,1,0:T(8,128)(2,1)S(1)} %get-tuple-element.42), channel_id=1, source_target_pairs={{8,16},{16,8},{24,32},{32,24},{40,48},{48,40},{56,64},{64,56},{72,... | collective-permute-start | bytes 98312 | tf_op jit(solution)/shard_map/ppermute | solution.py:32
  20.2 15.9 %copy-start.4 = (bf16[12,16,1024]{2,1,0:T(8,128)(2,1)}, bf16[12,16,1024]{2,1,0:T(8,128)(2,1)S(1)}, u32[]{:S(2)}) copy-start(bf16[12,16,1024]{2,1,0:T(8,128)(2,1)S(1)} %collective-permute-done.2.refs_3_) | copy-start | bytes 1179652
  20.2 15.9 %copy-start.5 = (bf16[12,16,1024]{2,1,0:T(8,128)(2,1)}, bf16[12,16,1024]{2,1,0:T(8,128)(2,1)S(1)}, u32[]{:S(2)}) copy-start(bf16[12,16,1024]{2,1,0:T(8,128)(2,1)S(1)} %collective-permute-done.1.refs_4_) | copy-start | bytes 1179652
  20.2 3.9 %collective-permute-start.4 = (bf16[64,512]{1,0:T(8,128)(2,1)}, bf16[64,512]{1,0:T(8,128)(2,1)S(1)}, u32[]{:S(2)}, u32[]{:S(2)}) collective-permute-start(bf16[64,512]{1,0:T(8,128)(2,1)} %get-tuple-element.24), channel_id=1, source_target_pairs={{0,4},{4,0},{1,5},{5,1},{2,6},{6,2},{3,7},{7,3},{8,12},{12,8},{9,1... | collective-permute-start | bytes 196616 | tf_op jit(solution)/shard_map/ppermute | solution.py:24
  24.1 3.9 %collective-permute-start.5 = (bf16[64,512]{1,0:T(8,128)(2,1)S(1)}, bf16[64,512]{1,0:T(8,128)(2,1)S(1)}, u32[]{:S(2)}, u32[]{:S(2)}) collective-permute-start(bf16[64,512]{1,0:T(8,128)(2,1)S(1)} %pad_maximum_fusion), channel_id=1, source_target_pairs={{0,1},{1,0},{2,3},{3,2},{4,5},{5,4},{6,7},{7,6},{8,9},{9,8},{10,11... | collective-permute-start | bytes 196616 | tf_op jit(solution)/shard_map/ppermute | solution.py:24
  25.0 11.1 %collective-permute-start.10 = (bf16[12,16,1024]{2,1,0:T(8,128)(2,1)S(1)}, bf16[12,16,1024]{2,1,0:T(8,128)(2,1)S(1)}, u32[]{:S(2)}, u32[]{:S(2)}) collective-permute-start(bf16[12,16,1024]{2,1,0:T(8,128)(2,1)S(1)} %collective-permute-done.2.refs_3_), channel_id=1, source_target_pairs={{0,4},{4,0},{1,5},{5,1},{2,6},{6,2},{3,7},{7,3},{8,12},{12,8},{9,1... | collective-permute-start | bytes 1179656 | tf_op jit(solution)/shard_map/ppermute | solution.py:24
  26.4 9.6 %collective-permute-start.8 = (bf16[12,16,1024]{2,1,0:T(8,128)(2,1)S(1)}, bf16[12,16,1024]{2,1,0:T(8,128)(2,1)S(1)}, u32[]{:S(2)}, u32[]{:S(2)}) collective-permute-start(bf16[12,16,1024]{2,1,0:T(8,128)(2,1)S(1)} %collective-permute-done.1.refs_4_), channel_id=1, source_target_pairs={{0,1},{1,0},{2,3},{3,2},{4,5},{5,4},{6,7},{7,6},{8,9},{9,8},{10,11... | collective-permute-start | bytes 1179656 | tf_op jit(solution)/shard_map/ppermute | solution.py:24
  27.9 8.2 %copy-start = (bf16[12,16,1024]{2,1,0:T(8,128)(2,1)}, bf16[12,16,1024]{2,1,0:T(8,128)(2,1)S(1)}, u32[]{:S(2)}) copy-start(bf16[12,16,1024]{2,1,0:T(8,128)(2,1)S(1)} %collective-permute-done.6.refs_2_) | copy-start | bytes 1179652
  27.9 8.2 %collective-permute-start.9 = (bf16[6,16,1024]{2,1,0:T(8,128)(2,1)S(1)}, bf16[6,16,1024]{2,1,0:T(8,128)(2,1)S(1)}, u32[]{:S(2)}, u32[]{:S(2)}) collective-permute-start(bf16[6,16,1024]{2,1,0:T(8,128)(2,1)S(1)} %slice.46), channel_id=1, source_target_pairs={{0,4},{4,0},{1,5},{5,1},{2,6},{6,2},{3,7},{7,3},{8,12},{12,8},{9,1... | collective-permute-start | bytes 589832 | tf_op jit(solution)/shard_map/ppermute | solution.py:24
  28.7 6.5 %collective-permute-start.7 = (bf16[64,512]{1,0:T(8,128)(2,1)S(1)}, bf16[64,512]{1,0:T(8,128)(2,1)S(1)}, u32[]{:S(2)}, u32[]{:S(2)}) collective-permute-start(bf16[64,512]{1,0:T(8,128)(2,1)S(1)} %pad_maximum_fusion.1), channel_id=1, source_target_pairs={{0,3},{1,2},{2,1},{3,0},{4,7},{5,6},{6,5},{7,4},{8,11},{9,10},{10,... | collective-permute-start | bytes 196616 | tf_op jit(solution)/shard_map/ppermute | solution.py:24
  28.8 7.3 %collective-permute-start.11 = (bf16[1,16,1024]{2,1,0:T(8,128)(2,1)S(1)}, bf16[1,16,1024]{2,1,0:T(8,128)(2,1)S(1)}, u32[]{:S(2)}, u32[]{:S(2)}) collective-permute-start(bf16[1,16,1024]{2,1,0:T(8,128)(2,1)S(1)} %get-tuple-element.41), channel_id=1, source_target_pairs={{0,8},{8,0},{1,9},{9,1},{2,10},{10,2},{3,11},{11,3},{4,12},{12,4},... | collective-permute-start | bytes 98312 | tf_op jit(solution)/shard_map/ppermute | solution.py:24
  41.8 7.5 %copy-start.2 = (bf16[12,16,1024]{2,1,0:T(8,128)(2,1)S(1)}, bf16[12,16,1024]{2,1,0:T(8,128)(2,1)}, u32[]{:S(2)}) copy-start(bf16[12,16,1024]{2,1,0:T(8,128)(2,1)} %copy-done.1) | copy-start | bytes 1179652
  41.8 5.9 %collective-permute-start.12 = (f32[432,128]{1,0:T(8,128)}, f32[432,128]{1,0:T(8,128)S(1)}, u32[]{:S(2)}, u32[]{:S(2)}) collective-permute-start(f32[432,128]{1,0:T(8,128)} %grad_kernel_terms.1), channel_id=1, source_target_pairs={{0,8},{8,0},{1,9},{9,1},{2,10},{10,2},{3,11},{11,3},{4,12},{12,4},... | collective-permute-start | bytes 663560 | tf_op jit(solution)/shard_map/ppermute | solution.py:24
  48.7 8.3 %collective-permute-start.13 = (f32[432,128]{1,0:T(8,128)S(1)}, f32[432,128]{1,0:T(8,128)S(1)}, u32[]{:S(2)}, u32[]{:S(2)}) collective-permute-start(f32[432,128]{1,0:T(8,128)S(1)} %add.12), channel_id=1, source_target_pairs={{0,16},{16,0},{32,48},{48,32},{1,17},{17,1},{33,49},{49,33},{2,18}... | collective-permute-start | bytes 663560 | tf_op jit(solution)/shard_map/ppermute | solution.py:24
  49.4 10.6 %collective-permute-start.14 = (bf16[6,16,1024]{2,1,0:T(8,128)(2,1)S(1)}, bf16[6,16,1024]{2,1,0:T(8,128)(2,1)S(1)}, u32[]{:S(2)}, u32[]{:S(2)}) collective-permute-start(bf16[6,16,1024]{2,1,0:T(8,128)(2,1)S(1)} %slice.47), channel_id=1, source_target_pairs={{0,1},{1,0},{2,3},{3,2},{4,5},{5,4},{6,7},{7,6},{8,9},{9,8},{10,11... | collective-permute-start | bytes 589832 | tf_op jit(solution)/shard_map/ppermute | solution.py:24
  57.0 9.9 %collective-permute-start.17 = (f32[432,128]{1,0:T(8,128)S(1)}, f32[432,128]{1,0:T(8,128)S(1)}, u32[]{:S(2)}, u32[]{:S(2)}) collective-permute-start(f32[432,128]{1,0:T(8,128)S(1)} %add.13), channel_id=1, source_target_pairs={{0,48},{16,32},{32,16},{48,0},{1,49},{17,33},{33,17},{49,1},{2,50}... | collective-permute-start | bytes 663560 | tf_op jit(solution)/shard_map/ppermute | solution.py:24
  64.9 5.7 %collective-permute-start.15 = (f32[2,16,1024]{2,1,0:T(8,128)}, f32[2,16,1024]{2,1,0:T(8,128)S(1)}, u32[]{:S(2)}, u32[]{:S(2)}) collective-permute-start(f32[2,16,1024]{2,1,0:T(8,128)} %get-tuple-element.36), channel_id=1, source_target_pairs={{0,8},{8,0},{1,9},{9,1},{2,10},{10,2},{3,11},{11,3},{4,12},{12,4},... | collective-permute-start | bytes 393224 | tf_op jit(solution)/shard_map/ppermute | solution.py:24
  65.8 4.8 %collective-permute-start.16 = (f32[2,16,1024]{2,1,0:T(8,128)}, f32[2,16,1024]{2,1,0:T(8,128)S(1)}, u32[]{:S(2)}, u32[]{:S(2)}) collective-permute-start(f32[2,16,1024]{2,1,0:T(8,128)} %get-tuple-element.37), channel_id=1, source_target_pairs={{8,16},{16,8},{24,32},{32,24},{40,48},{48,40},{56,64},{64,56},{72,... | collective-permute-start | bytes 393224 | tf_op jit(solution)/shard_map/ppermute | solution.py:32
  66.9 7.9 %collective-permute-start.18 = (bf16[432,128]{1,0:T(8,128)(2,1)S(1)}, bf16[432,128]{1,0:T(8,128)(2,1)S(1)}, u32[]{:S(2)}, u32[]{:S(2)}) collective-permute-start(bf16[432,128]{1,0:T(8,128)(2,1)S(1)} %add_convert_fusion), channel_id=1, source_target_pairs={{0,64},{64,0},{1,65},{65,1},{2,66},{66,2},{3,67},{67,3},{4,68},{68... | collective-permute-start | bytes 331784 | tf_op jit(solution)/shard_map/ppermute | solution.py:24
  (13 other events, 21.7 us)
where the time goes:
time: 76.8 us; the launch traced here: 75.6 us
  starting transfers between devices  38.4 us (50%)
  Pallas kernels  18.2 us (24%)
  waiting for transfers between devices  10.2 us (13%)
  local copies, waits for them, and re-layouts  6.1 us (8%)
  other arithmetic  1.77 us (2%)
  between operations  0.84 us (1%)
    ppermute x17, starting transfers between devices, swap(): lax.ppermute(v, axis, [(i, i ^ bits) for i in range(lax.axis_size(axis))])  34.4 us
    pallas_call x6, Pallas kernels, call(): pl.pallas_call(body, out_shape=[jax.ShapeDtypeStruct(s, d) for s, d in ou...  18.2 us
    ppermute x17, waiting for transfers between devices, swap(): lax.ppermute(v, axis, [(i, i ^ bits) for i in range(lax.axis_size(axis))])  10 us
    ppermute x2, starting transfers between devices, outer_swap(): return lax.ppermute(v, SPACE, pairs)  4.06 us
    unnamed x35, local copies, waits for them, and re-layouts  3.95 us
  transfers between devices with their start and end apart: 19, of which 6 were waited for; matrix products, arithmetic and copies ran while one was open for 2% of the time, Pallas kernels for 19%

commit v1 on v0

v1 whole, which is shorter than its diff:
```python
import functools

import jax
import jax.numpy as jnp
from jax import lax
from jax.experimental import pallas as pl
from jax.experimental.pallas import tpu as pltpu
from jax.sharding import Mesh, PartitionSpec as P

NXY = 32
CELLS = NXY * NXY
C = 128
N = 6
SPACE = ("zh", "x", "core")
CHAN = ("zl", "y")
BF = jnp.bfloat16
F32 = jnp.float32
VMEM_LIMIT = 56 * 1024 * 1024
VM = pl.BlockSpec(memory_space=pltpu.VMEM)
KEYS = [(0, 0), (0, 1), (0, 2), (0, 3), (1, 0), (1, 1), (1, 2), (1, 3)]


def swap(v, axis, bits):
    return lax.ppermute(v, axis, [(i, i ^ bits) for i in range(lax.axis_size(axis))])


def outer_swap(v):
    pairs = []
    for i in range(1, 16, 2):
        j = (i + 1) % 16
        pairs += [(i, j), (j, i)]
    return lax.ppermute(v, SPACE, pairs)


def after(v, *deps):
    return lax.optimization_barrier((v,) + deps)[0]


def group(key):
    return (lax.axis_index("zl") ^ key[0]) * 4 + (lax.axis_index("y") ^ key[1])


def first_row(key):
    return pl.multiple_of(group(key) * 16, 16)


def lane_y():
    return lax.broadcasted_iota(jnp.int32, (16, CELLS), 1) % NXY


def from_y_before(v, y):
    return jnp.where(y == 0, pltpu.roll(v, CELLS - (NXY - 1), 1), pltpu.roll(v, 1, 1))


def from_y_after(v, y):
    return jnp.where(y == NXY - 1, pltpu.roll(v, NXY - 1, 1), pltpu.roll(v, CELLS - 1, 1))


def assemble(blocks, field, absolute, pair):
    for n, (key, (ref, start)) in enumerate(zip(KEYS, blocks)):
        row = first_row(key) if absolute else n * 16
        for z in (2 * pair, 2 * pair + 1):
            field[z, pl.ds(row, 16), :] = ref[start + z]


def pack_body(k_ref, a_ref, g_ref, by1, by3, byz, own, turned):
    turned[:, 0:432] = jnp.transpose(k_ref[...].astype(F32))
    turned[:, 432:512] = jnp.zeros((C, 80), F32)

    def piece(key):
        return turned[pl.ds(first_row(key), 16), :].astype(BF)

    own[...] = piece((0, 0))
    for dst, pairs in (
        (by1, (((0, 1), (0, 2)), ((1, 2), (1, 2)))),
        (by3, (((0, 3), (1, 3)),)),
        (byz, (((1, 0), (1, 1)),)),
    ):
        dst[pl.ds(0, N)] = a_ref[...]
        dst[pl.ds(N + len(pairs), N)] = g_ref[...]
        for n, (left, right) in enumerate(pairs):
            dst[N + n, :, 0:512] = piece(left)
            dst[N + n, :, 512:1024] = piece(right)


def unpack_filter(own, units, w_ref):
    lane = lax.broadcasted_iota(jnp.int32, (16, C), 1) // 16
    right = ((0, 2), (1, 3), (1, 1))
    pieces = [own[...].astype(F32)]
    for key, unit in zip(KEYS[1:], units[1:]):
        at = 512 if key in right else 0
        pieces.append(unit[N + 1 if key == (1, 2) else N, :, pl.ds(at, 512)].astype(F32))
    for tap in range(27):
        tile, spot = divmod(tap * 16, C)
        row = None
        for n, piece in enumerate(pieces):
            v = piece[:, tile * C : (tile + 1) * C]
            move = (n * 16 - spot) % C
            v = v if move == 0 else pltpu.roll(v, move, 1)
            row = v if row is None else jnp.where(lane == n, v, row)
        w_ref[pl.ds((26 - tap) * 16, 16), :] = row.astype(BF)


def gk_body(*refs):
    units, (g, g_in, g_out), (out,), (field, g9) = refs[:8], refs[8:11], refs[11:12], refs[12:]
    core = lax.axis_index("core")
    y = lane_y()
    for p in range(N + 2):
        if p == 0:
            plane = jnp.where(core == 0, g_out[0].astype(F32), g_in[0].astype(F32))
        elif p == N + 1:
            plane = jnp.where(core == 0, g_in[0].astype(F32), g_out[0].astype(F32))
        else:
            plane = g[p - 1].astype(F32)
        slot = N + 1 - p
        for c, v in enumerate((from_y_after(plane, y), plane, from_y_before(plane, y))):
            for b, w in enumerate((pltpu.roll(v, CELLS - NXY, 1), v, pltpu.roll(v, NXY, 1))):
                g9[pl.ds(slot * 144 + (b * 3 + c) * 16, 16), :] = w.astype(BF)
    for pair in range(N // 2):
        assemble([(u, 0) for u in units], field, True, pair)
        z = 2 * pair
        lhs = g9[pl.ds((N - 2 - z) * 144, 576), :]
        rhs = field[pl.ds(z, 2)].reshape(2 * C, CELLS)
        term = lax.dot_general(lhs, rhs, (((1,), (1,)), ((), ())), preferred_element_type=F32)
        term = term[144:576, 0:C] + term[0:432, C : 2 * C]
        if pair == 0:
            out[...] = term
        else:
            out[...] += term


def fold(t, y):
    s = t[48:96] + pltpu.roll(t[0:48], NXY, 1) + pltpu.roll(t[96:144], CELLS - NXY, 1)
    return s[16:32] + from_y_before(s[0:16], y) + from_y_after(s[32:48], y)


G_STARTS = {(0, 0): 0, (1, 2): 0, (0, 1): N + 2, (0, 2): N + 2}


def g_blocks(units):
    return [(u, G_STARTS.get(key, N + 1)) for key, u in zip(KEYS, units)]


def edges_body(*refs):
    units, (g, z2g, w, own), (inner, outer, w_in), (field,) = refs[:8], refs[8:12], refs[12:15], refs[15:]
    unpack_filter(own, units, w_in)
    y = lane_y()
    first = lax.axis_index("core") == 0
    g_units = [g, *units[1:6], z2g, units[7]]
    for n, (blocks, weights) in enumerate((([(u, 0) for u in units], w), (g_blocks(g_units), w_in))):
        for i, (key, (ref, start)) in enumerate(zip(KEYS, blocks)):
            row = first_row(key) if n == 0 else i * 16
            for k, z in enumerate((0, N - 1)):
                field[2 * n + k, pl.ds(row, 16), :] = ref[start + z]
        before = fold(jnp.dot(weights[pl.ds(288, 144), :], field[2 * n], preferred_element_type=F32), y)
        behind = fold(jnp.dot(weights[pl.ds(0, 144), :], field[2 * n + 1], preferred_element_type=F32), y)
        inner[n] = jnp.where(first, behind, before)
        outer[n] = jnp.where(first, before, behind)


def conv_body(which, *refs):
    units, w = refs[:8], refs[8]
    if which == 0:
        blocks = [(u, 0) for u in units]
        out_ref, edge, field, carry = refs[9:]
    else:
        blocks = g_blocks(units)
        inner, outer, done, edge, out_ref, done_ref, field, carry = refs[9:]
        first = lax.axis_index("core") == 0
        low = [jnp.where(first, outer[n], inner[n]) for n in range(2)]
        high = [jnp.where(first, inner[n], outer[n]) for n in range(2)]
        done_ref[0] = (edge[0] + low[0]).astype(BF)
        done_ref[pl.ds(1, N - 2)] = done[...]
        done_ref[N - 1] = (edge[1] + high[0]).astype(BF)
    y = lane_y()
    w0, w1, w2 = (w[pl.ds(a * 144, 144), :] for a in range(3))
    none = jnp.zeros((144, C), BF)
    rows = [jnp.concatenate(row, axis=1) for row in ((w2, none), (w1, w2), (w0, w1), (none, w0))]
    last = N // 2 - 1
    for pair in range(N // 2):
        assemble(blocks, field, which == 0, pair)
        rhs = field[pl.ds(2 * pair, 2)].reshape(2 * C, CELLS)
        used = range(1 if pair == 0 else 0, 3 if pair == last else 4)
        terms = jnp.dot(jnp.concatenate([rows[n] for n in used], axis=0), rhs, preferred_element_type=F32)
        for i, n in enumerate(used):
            z = 2 * pair - 1 + n
            t = terms[i * 144 : i * 144 + 144]
            if n < 2 and pair > 0:
                t = t + carry[pl.ds(n * 144, 144), :]
            if n >= 2 and pair < last:
                carry[pl.ds((n - 2) * 144, 144), :] = t
                continue
            out = fold(t, y)
            if which == 1:
                out = out + low[1] if z == 0 else out + high[1] if z == N - 1 else out
                out_ref[z] = out.astype(BF)
            elif z in (0, N - 1):
                edge[0 if z == 0 else 1] = out
            else:
                out_ref[z - 1] = out.astype(BF)


def call(body, name, args, outs, scratch=(), flops=0):
    return pl.pallas_call(
        body,
        out_shape=[jax.ShapeDtypeStruct(s, d) for s, d in outs],
        in_specs=[VM] * len(args),
        out_specs=[VM] * len(outs),
        scratch_shapes=list(scratch),
        compiler_params=pltpu.CompilerParams(vmem_limit_bytes=VMEM_LIMIT),
        cost_estimate=pl.CostEstimate(flops=flops, bytes_accessed=1 << 20, transcendentals=0),
        name=name,
    )(*args)


CONV_FLOPS = 2 * 432 * C * CELLS * N
FIELD = pltpu.VMEM((N, C, CELLS), BF)


def on_device(activation, cotangent, kernel):
    core = lax.axis_index("core")
    kt = jnp.swapaxes(kernel, 3, 4).reshape(432, C)
    plane = (16, CELLS)

    by1, by3, byz, own = call(
        pack_body,
        "pack_messages",
        [kt, activation, cotangent],
        [((N * 2 + 2, *plane), BF), ((N * 2 + 1, *plane), BF), ((N * 2 + 1, *plane), BF), ((16, 512), BF)],
        [pltpu.VMEM((C, 512), F32)],
    )
    k1 = swap(by1, "y", 1)
    k3 = swap(by3, "y", 3)
    z0 = swap(byz, "zl", 1)
    g_in = swap(jnp.where(core == 0, cotangent[N - 1 :], cotangent[:1]), "core", 1)
    g_out = outer_swap(jnp.where(core == 0, cotangent[:1], cotangent[N - 1 :]))
    k2 = swap(after(k1, g_out), "y", 3)
    z1 = swap(z0, "y", 1)
    z3 = swap(k3, "zl", 1)
    z2a = swap(k2[: N + 2], "zl", 1)
    z2g = swap(z1[N + 1 :], "y", 3)

    units = [k1, k2, k3, z0, z1, z2a, z3]
    terms = call(
        gk_body,
        "grad_kernel_terms",
        [after(activation, z2g), *units, cotangent, g_in, g_out],
        [((432, C), F32)],
        [FIELD, pltpu.VMEM(((N + 2) * 144, CELLS), BF)],
        CONV_FLOPS,
    )[0]
    terms = terms + swap(terms, "core", 1)
    got = swap(terms, "x", 1)
    inner, outer, w_in = call(
        edges_body,
        "edge_terms",
        [after(activation, terms), *units, cotangent, z2g, kt, own],
        [((2, *plane), F32)] * 2 + [((432, C), BF)],
        [pltpu.VMEM((4, C, CELLS), BF)],
        CONV_FLOPS // 9,
    )
    outer = outer_swap(outer)
    inner = swap(inner, "core", 1)
    terms = (after(terms, w_in) + got).astype(BF)
    got = swap(terms, "x", 3)
    middle, ends = call(
        functools.partial(conv_body, 0),
        "output_planes",
        [after(activation, terms), *units, kt],
        [((N - 2, *plane), BF), ((2, *plane), F32)],
        [FIELD, pltpu.VMEM((288, CELLS), F32)],
        CONV_FLOPS,
    )
    terms = after(terms, ends, outer).astype(F32) + got.astype(F32)
    got = swap(terms, "zh", 1)
    grad_input, output = call(
        functools.partial(conv_body, 1),
        "grad_input_planes",
        [after(cotangent, terms), *units[:5], z2g, z3, w_in, inner, outer, middle, ends],
        [((N, *plane), BF)] * 2,
        [FIELD, pltpu.VMEM((288, CELLS), F32)],
        CONV_FLOPS,
    )
    terms = (after(terms, grad_input) + got) * 98304.0**-0.5
    grad_kernel = jnp.swapaxes(terms.reshape(3, 3, 3, 16, C), 3, 4)
    return (output, grad_input, grad_kernel)


def solution(mesh):
    fine = Mesh(mesh.devices.reshape(2, 4, 2, 2, 4), SPACE + CHAN)
    field = P(SPACE, CHAN, None)
    filt = P(None, None, None, None, CHAN)
    return jax.shard_map(
        on_device,
        mesh=fine,
        in_specs=(field, field, filt),
        out_specs=(field, field, filt),
        check_vma=False,
    )
```

time: 76.8 us -> 72.4 us (0.943); the launches traced: 75.6 us -> 72.1 us
  starting transfers between devices: 38.4 us -> 33.2 us
  waiting for transfers between devices: 10.2 us -> 14.8 us
  local copies, waits for them, and re-layouts: 6.1 us -> 2.33 us
    ppermute x17 -> x14, starting transfers between devices: 34.4 us -> 29.8 us  [swap(): lax.ppermute(v, axis, [(i, i ^ bits) for i in range(lax.axis_size(axis))])]
    ppermute x17 -> x14, waiting for transfers between devices: 10 us -> 12.9 us  [swap(): lax.ppermute(v, axis, [(i, i ^ bits) for i in range(lax.axis_size(axis))])]
    slice x8 -> x2, local copies, waits for them, and re-layouts: 2.14 us -> 0.03 us  [the longest x1 0.02 us: on_device(): z2a = swap(k2[:N + 2], 'zl', 1)]
    ppermute x2, waiting for transfers between devices: 0.21 us -> 1.9 us  [outer_swap(): return lax.ppermute(v, SPACE, pairs)]
    unnamed x35 -> x26, local copies, waits for them, and re-layouts: 3.95 us -> 2.29 us
    select_n x1, other arithmetic: 0.01 us -> 0.78 us  [on_device(): jnp.where(core == 0, cotangent[N - 1:], cotangent[:1])]
    pallas_call x6 -> x5, Pallas kernels: 18.2 us -> 18.6 us  [call(): pl.pallas_call(body, out_shape=[jax.ShapeDtypeStruct(s, d) for s, d in ou...]
  transfers between devices with their start and end apart: 19 -> 16, of which waited for: 6 -> 10; matrix products, arithmetic and copies ran while one was open for 2% -> 1% of each run, Pallas kernels for 19% -> 17%
where the time goes in v1:
time: 72.4 us; the launch traced here: 72.1 us
  starting transfers between devices  33.2 us (46%)
  Pallas kernels  18.6 us (26%)
  waiting for transfers between devices  14.8 us (20%)
  other arithmetic  2.53 us (3%)
  local copies, waits for them, and re-layouts  2.33 us (3%)
    ppermute x14, starting transfers between devices, swap(): lax.ppermute(v, axis, [(i, i ^ bits) for i in range(lax.axis_size(axis))])  29.8 us
    pallas_call x5, Pallas kernels, call(): pl.pallas_call(body, out_shape=[jax.ShapeDtypeStruct(s, d) for s, d in ou...  18.6 us
    ppermute x14, waiting for transfers between devices, swap(): lax.ppermute(v, axis, [(i, i ^ bits) for i in range(lax.axis_size(axis))])  12.9 us
    ppermute x2, starting transfers between devices, outer_swap(): return lax.ppermute(v, SPACE, pairs)  3.47 us
    unnamed x26, local copies, waits for them, and re-layouts  2.29 us
    ppermute x2, waiting for transfers between devices, outer_swap(): return lax.ppermute(v, SPACE, pairs)  1.9 us
  transfers between devices with their start and end apart: 16, of which 10 were waited for; matrix products, arithmetic and copies ran while one was open for 1% of the time, Pallas kernels for 17%

profile of v1, /device:TPU:1, one launch (start us, length us, event | category | flops | bytes accessed | tf_op | source)
XLA Modules:
  0.0 72.1 jit_solution(9575791324001870718)
XLA Ops:
  0.6 2.3 %pack_messages.1 = (bf16[14,16,1024]{2,1,0:T(8,128)(2,1)}, bf16[13,16,1024]{2,1,0:T(8,128)(2,1)}, bf16[13,16,1024]{2,1,0:T(8,128)(2,1)}, bf16[16,512]{1,0:T(8,128)(2,1)}) custom-call(bf16[432,128]{1,0:T(8,128)(2,1)} %bitcast.6, bf16[6,16,1024]{2,1,0:T(8,128)(2,1)} %refs_0_.2, bf16[6,16,1024]{2,1,0:T(8,128)(2,1)} %refs_0_.3), custom_call_target="tpu_custom_call" | custom-call | bytes 1048576 | tf_op jit(solution)/shard_map/pack_messages/pallas_call | solution.py:204
  3.0 2.1 %collective-permute-start.3 = (bf16[14,16,1024]{2,1,0:T(8,128)(2,1)}, bf16[14,16,1024]{2,1,0:T(8,128)(2,1)S(1)}, u32[]{:S(2)}, u32[]{:S(2)}) collective-permute-start(bf16[14,16,1024]{2,1,0:T(8,128)(2,1)} %get-tuple-element.24), channel_id=1, source_target_pairs={{0,1},{1,0},{2,3},{3,2},{4,5},{5,4},{6,7},{7,6},{8,9},{9,8},{10,11... | collective-permute-start | bytes 1376264 | tf_op jit(solution)/shard_map/ppermute | solution.py:24
  5.1 1.6 %collective-permute-start = (bf16[13,16,1024]{2,1,0:T(8,128)(2,1)}, bf16[13,16,1024]{2,1,0:T(8,128)(2,1)S(1)}, u32[]{:S(2)}, u32[]{:S(2)}) collective-permute-start(bf16[13,16,1024]{2,1,0:T(8,128)(2,1)} %get-tuple-element.22), channel_id=1, source_target_pairs={{0,4},{4,0},{1,5},{5,1},{2,6},{6,2},{3,7},{7,3},{8,12},{12,8},{9,1... | collective-permute-start | bytes 1277960 | tf_op jit(solution)/shard_map/ppermute | solution.py:24
  6.7 1.9 %collective-permute-start.6 = (bf16[13,16,1024]{2,1,0:T(8,128)(2,1)}, bf16[13,16,1024]{2,1,0:T(8,128)(2,1)S(1)}, u32[]{:S(2)}, u32[]{:S(2)}) collective-permute-start(bf16[13,16,1024]{2,1,0:T(8,128)(2,1)} %get-tuple-element.26), channel_id=1, source_target_pairs={{0,3},{1,2},{2,1},{3,0},{4,7},{5,6},{6,5},{7,4},{8,11},{9,10},{10,... | collective-permute-start | bytes 1277960 | tf_op jit(solution)/shard_map/ppermute | solution.py:24
  9.4 2.7 %collective-permute-start.4 = (bf16[1,16,1024]{2,1,0:T(8,128)(2,1)S(1)}, bf16[1,16,1024]{2,1,0:T(8,128)(2,1)S(1)}, u32[]{:S(2)}, u32[]{:S(2)}) collective-permute-start(bf16[1,16,1024]{2,1,0:T(8,128)(2,1)S(1)} %get-tuple-element.42), channel_id=1, source_target_pairs={{8,16},{16,8},{24,32},{32,24},{40,48},{48,40},{56,64},{64,56},{72,... | collective-permute-start | bytes 98312 | tf_op jit(solution)/shard_map/ppermute | solution.py:32
  12.1 1.9 %collective-permute-done.4.refs_10_ = bf16[1,16,1024]{2,1,0:T(8,128)(2,1)S(1)} collective-permute-done((bf16[1,16,1024]{2,1,0:T(8,128)(2,1)S(1)}, bf16[1,16,1024]{2,1,0:T(8,128)(2,1)S(1)}, u32[]{:S(2)}, u32[]{:S(2)}) %collective-permute-start.4) | collective-permute-done | bytes 32800 | tf_op jit(solution)/shard_map/ppermute | solution.py:32
  14.0 1.1 %collective-permute-done.3.refs_1_ = bf16[14,16,1024]{2,1,0:T(8,128)(2,1)S(1)} collective-permute-done((bf16[14,16,1024]{2,1,0:T(8,128)(2,1)}, bf16[14,16,1024]{2,1,0:T(8,128)(2,1)S(1)}, u32[]{:S(2)}, u32[]{:S(2)}) %collective-permute-start.3) | collective-permute-done | bytes 458784 | tf_op jit(solution)/shard_map/ppermute | solution.py:24
  15.1 3.0 %collective-permute-start.5 = (bf16[14,16,1024]{2,1,0:T(8,128)(2,1)S(1)}, bf16[14,16,1024]{2,1,0:T(8,128)(2,1)S(1)}, u32[]{:S(2)}, u32[]{:S(2)}) collective-permute-start(bf16[14,16,1024]{2,1,0:T(8,128)(2,1)S(1)} %collective-permute-done.3.refs_1_), channel_id=1, source_target_pairs={{0,3},{1,2},{2,1},{3,0},{4,7},{5,6},{6,5},{7,4},{8,11},{9,10},{10,... | collective-permute-start | bytes 1376264 | tf_op jit(solution)/shard_map/ppermute | solution.py:24
  18.2 1.7 %collective-permute-start.8 = (bf16[13,16,1024]{2,1,0:T(8,128)(2,1)S(1)}, bf16[13,16,1024]{2,1,0:T(8,128)(2,1)S(1)}, u32[]{:S(2)}, u32[]{:S(2)}) collective-permute-start(bf16[13,16,1024]{2,1,0:T(8,128)(2,1)S(1)} %collective-permute-done.6.refs_3_), channel_id=1, source_target_pairs={{0,4},{4,0},{1,5},{5,1},{2,6},{6,2},{3,7},{7,3},{8,12},{12,8},{9,1... | collective-permute-start | bytes 1277960 | tf_op jit(solution)/shard_map/ppermute | solution.py:24
  19.9 7.3 %collective-permute-done.5.refs_2_ = bf16[14,16,1024]{2,1,0:T(8,128)(2,1)S(1)} collective-permute-done((bf16[14,16,1024]{2,1,0:T(8,128)(2,1)S(1)}, bf16[14,16,1024]{2,1,0:T(8,128)(2,1)S(1)}, u32[]{:S(2)}, u32[]{:S(2)}) %collective-permute-start.5) | collective-permute-done | bytes 458784 | tf_op jit(solution)/shard_map/ppermute | solution.py:24
  27.2 1.7 %collective-permute-start.7 = (bf16[8,16,1024]{2,1,0:T(8,128)(2,1)S(1)}, bf16[8,16,1024]{2,1,0:T(8,128)(2,1)S(1)}, u32[]{:S(2)}, u32[]{:S(2)}) collective-permute-start(bf16[8,16,1024]{2,1,0:T(8,128)(2,1)S(1)} %slice.19), channel_id=1, source_target_pairs={{0,4},{4,0},{1,5},{5,1},{2,6},{6,2},{3,7},{7,3},{8,12},{12,8},{9,1... | collective-permute-start | bytes 786440 | tf_op jit(solution)/shard_map/ppermute | solution.py:24
  29.0 2.7 %collective-permute-start.2 = (bf16[6,16,1024]{2,1,0:T(8,128)(2,1)S(1)}, bf16[6,16,1024]{2,1,0:T(8,128)(2,1)S(1)}, u32[]{:S(2)}, u32[]{:S(2)}) collective-permute-start(bf16[6,16,1024]{2,1,0:T(8,128)(2,1)S(1)} %slice.18), channel_id=1, source_target_pairs={{0,3},{1,2},{2,1},{3,0},{4,7},{5,6},{6,5},{7,4},{8,11},{9,10},{10,... | collective-permute-start | bytes 589832 | tf_op jit(solution)/shard_map/ppermute | solution.py:24
  31.7 3.0 %collective-permute-start.9 = (bf16[1,16,1024]{2,1,0:T(8,128)(2,1)S(1)}, bf16[1,16,1024]{2,1,0:T(8,128)(2,1)S(1)}, u32[]{:S(2)}, u32[]{:S(2)}) collective-permute-start(bf16[1,16,1024]{2,1,0:T(8,128)(2,1)S(1)} %get-tuple-element.41), channel_id=1, source_target_pairs={{0,8},{8,0},{1,9},{9,1},{2,10},{10,2},{3,11},{11,3},{4,12},{12,4},... | collective-permute-start | bytes 98312 | tf_op jit(solution)/shard_map/ppermute | solution.py:24
  37.0 4.3 %grad_kernel_terms.1 = f32[432,128]{1,0:T(8,128)} custom-call(bf16[6,16,1024]{2,1,0:T(8,128)(2,1)} %refs_0_.2, bf16[14,16,1024]{2,1,0:T(8,128)(2,1)} %copy-done.2, bf16[14,16,1024]{2,1,0:T(8,128)(2,1)} %copy-done, bf16[13,16,1024]{2,1,0:T(8,128)(2,1)} %copy-done.4, bf16[13,16,1024]{2,1,0:T(8,128)(2,1)} %copy-done.3, bf16[13,16,1024]{2,1,0:T(8,128)(2,1)} %copy-done.1, ...), custom_call_target="tpu_custom_call" | custom-call | flops 679477248 | bytes 1048576 | tf_op jit(solution)/shard_map/grad_kernel_terms/pallas_call | solution.py:204
  41.3 3.1 %collective-permute-start.10 = (f32[432,128]{1,0:T(8,128)}, f32[432,128]{1,0:T(8,128)S(1)}, u32[]{:S(2)}, u32[]{:S(2)}) collective-permute-start(f32[432,128]{1,0:T(8,128)} %grad_kernel_terms.1), channel_id=1, source_target_pairs={{0,8},{8,0},{1,9},{9,1},{2,10},{10,2},{3,11},{11,3},{4,12},{12,4},... | collective-permute-start | bytes 663560 | tf_op jit(solution)/shard_map/ppermute | solution.py:24
  44.4 1.3 %collective-permute-done.10 = f32[432,128]{1,0:T(8,128)S(1)} collective-permute-done((f32[432,128]{1,0:T(8,128)}, f32[432,128]{1,0:T(8,128)S(1)}, u32[]{:S(2)}, u32[]{:S(2)}) %collective-permute-start.10) | collective-permute-done | bytes 221216 | tf_op jit(solution)/shard_map/ppermute | solution.py:24
  46.7 1.3 %collective-permute-start.11 = (f32[432,128]{1,0:T(8,128)S(1)}, f32[432,128]{1,0:T(8,128)S(1)}, u32[]{:S(2)}, u32[]{:S(2)}) collective-permute-start(f32[432,128]{1,0:T(8,128)S(1)} %add.12), channel_id=1, source_target_pairs={{0,16},{16,0},{32,48},{48,32},{1,17},{17,1},{33,49},{49,33},{2,18}... | collective-permute-start | bytes 663560 | tf_op jit(solution)/shard_map/ppermute | solution.py:24
  48.0 3.9 %edge_terms.1 = (f32[2,16,1024]{2,1,0:T(8,128)}, f32[2,16,1024]{2,1,0:T(8,128)}, bf16[432,128]{1,0:T(8,128)(2,1)}) custom-call(bf16[6,16,1024]{2,1,0:T(8,128)(2,1)} %refs_0_.2, bf16[14,16,1024]{2,1,0:T(8,128)(2,1)} %copy-done.2, bf16[14,16,1024]{2,1,0:T(8,128)(2,1)} %copy-done, bf16[13,16,1024]{2,1,0:T(8,128)(2,1)} %copy-done.4, ...), custom_call_target="tpu_custom_call" | custom-call | flops 75497472 | bytes 1048576 | tf_op jit(solution)/shard_map/edge_terms/pallas_call | solution.py:204
  53.4 4.8 %collective-permute-start.13 = (bf16[432,128]{1,0:T(8,128)(2,1)S(1)}, bf16[432,128]{1,0:T(8,128)(2,1)S(1)}, u32[]{:S(2)}, u32[]{:S(2)}) collective-permute-start(bf16[432,128]{1,0:T(8,128)(2,1)S(1)} %add_convert_fusion), channel_id=1, source_target_pairs={{0,48},{16,32},{32,16},{48,0},{1,49},{17,33},{33,17},{49,1},{2,50}... | collective-permute-start | bytes 331784 | tf_op jit(solution)/shard_map/ppermute | solution.py:24
  58.2 4.0 %output_planes.1 = (bf16[4,16,1024]{2,1,0:T(8,128)(2,1)}, f32[2,16,1024]{2,1,0:T(8,128)}) custom-call(bf16[6,16,1024]{2,1,0:T(8,128)(2,1)} %refs_0_.2, bf16[14,16,1024]{2,1,0:T(8,128)(2,1)} %copy-done.2, bf16[14,16,1024]{2,1,0:T(8,128)(2,1)} %copy-done, bf16[13,16,1024]{2,1,0:T(8,128)(2,1)} %copy-done.4, bf16[13,16,1024]{2,1,0:T(8,128)(2,1)} %copy-done.3, ...), custom_call_target="tpu_custom_call" | custom-call | flops 679477248 | bytes 1048576 | tf_op jit(solution)/shard_map/output_planes/pallas_call | solution.py:204
  62.8 1.1 %collective-permute-start.15 = (f32[432,128]{1,0:T(8,128)S(1)}, f32[432,128]{1,0:T(8,128)S(1)}, u32[]{:S(2)}, u32[]{:S(2)}) collective-permute-start(f32[432,128]{1,0:T(8,128)S(1)} %convert_add_fusion), channel_id=1, source_target_pairs={{0,64},{64,0},{1,65},{65,1},{2,66},{66,2},{3,67},{67,3},{4,68},{68... | collective-permute-start | bytes 663560 | tf_op jit(solution)/shard_map/ppermute | solution.py:24
  63.9 1.8 %collective-permute-start.14 = (f32[2,16,1024]{2,1,0:T(8,128)S(1)}, f32[2,16,1024]{2,1,0:T(8,128)S(1)}, u32[]{:S(2)}, u32[]{:S(2)}) collective-permute-start(f32[2,16,1024]{2,1,0:T(8,128)S(1)} %copy-done.12), channel_id=1, source_target_pairs={{0,8},{8,0},{1,9},{9,1},{2,10},{10,2},{3,11},{11,3},{4,12},{12,4},... | collective-permute-start | bytes 393224 | tf_op jit(solution)/shard_map/ppermute | solution.py:24
  65.7 1.0 %collective-permute-done.14.refs_9_ = f32[2,16,1024]{2,1,0:T(8,128)S(1)} collective-permute-done((f32[2,16,1024]{2,1,0:T(8,128)S(1)}, f32[2,16,1024]{2,1,0:T(8,128)S(1)}, u32[]{:S(2)}, u32[]{:S(2)}) %collective-permute-start.14) | collective-permute-done | bytes 131104 | tf_op jit(solution)/shard_map/ppermute | solution.py:24
  67.3 4.1 %grad_input_planes.1 = (bf16[6,16,1024]{2,1,0:T(8,128)(2,1)}, bf16[6,16,1024]{2,1,0:T(8,128)(2,1)}) custom-call(bf16[6,16,1024]{2,1,0:T(8,128)(2,1)} %refs_0_.3, bf16[14,16,1024]{2,1,0:T(8,128)(2,1)} %copy-done.2, bf16[14,16,1024]{2,1,0:T(8,128)(2,1)} %copy-done, bf16[13,16,1024]{2,1,0:T(8,128)(2,1)} %copy-done.4, bf16[13,16,1024]{2,1,0:T(8,128)(2,1)} %copy-done.3, ...), custom_call_target="tpu_custom_call" | custom-call | flops 679477248 | bytes 1048576 | tf_op jit(solution)/shard_map/grad_input_planes/pallas_call | solution.py:204
  (46 shorter events, 7.8 us)
Async XLA Ops:
  3.0 12.2 %collective-permute-start.3 = (bf16[14,16,1024]{2,1,0:T(8,128)(2,1)}, bf16[14,16,1024]{2,1,0:T(8,128)(2,1)S(1)}, u32[]{:S(2)}, u32[]{:S(2)}) collective-permute-start(bf16[14,16,1024]{2,1,0:T(8,128)(2,1)} %get-tuple-element.24), channel_id=1, source_target_pairs={{0,1},{1,0},{2,3},{3,2},{4,5},{5,4},{6,7},{7,6},{8,9},{9,8},{10,11... | collective-permute-start | bytes 1376264 | tf_op jit(solution)/shard_map/ppermute | solution.py:24
  5.1 13.0 %collective-permute-start = (bf16[13,16,1024]{2,1,0:T(8,128)(2,1)}, bf16[13,16,1024]{2,1,0:T(8,128)(2,1)S(1)}, u32[]{:S(2)}, u32[]{:S(2)}) collective-permute-start(bf16[13,16,1024]{2,1,0:T(8,128)(2,1)} %get-tuple-element.22), channel_id=1, source_target_pairs={{0,4},{4,0},{1,5},{5,1},{2,6},{6,2},{3,7},{7,3},{8,12},{12,8},{9,1... | collective-permute-start | bytes 1277960 | tf_op jit(solution)/shard_map/ppermute | solution.py:24
  6.7 11.5 %collective-permute-start.6 = (bf16[13,16,1024]{2,1,0:T(8,128)(2,1)}, bf16[13,16,1024]{2,1,0:T(8,128)(2,1)S(1)}, u32[]{:S(2)}, u32[]{:S(2)}) collective-permute-start(bf16[13,16,1024]{2,1,0:T(8,128)(2,1)} %get-tuple-element.26), channel_id=1, source_target_pairs={{0,3},{1,2},{2,1},{3,0},{4,7},{5,6},{6,5},{7,4},{8,11},{9,10},{10,... | collective-permute-start | bytes 1277960 | tf_op jit(solution)/shard_map/ppermute | solution.py:24
  9.4 4.6 %collective-permute-start.4 = (bf16[1,16,1024]{2,1,0:T(8,128)(2,1)S(1)}, bf16[1,16,1024]{2,1,0:T(8,128)(2,1)S(1)}, u32[]{:S(2)}, u32[]{:S(2)}) collective-permute-start(bf16[1,16,1024]{2,1,0:T(8,128)(2,1)S(1)} %get-tuple-element.42), channel_id=1, source_target_pairs={{8,16},{16,8},{24,32},{32,24},{40,48},{48,40},{56,64},{64,56},{72,... | collective-permute-start | bytes 98312 | tf_op jit(solution)/shard_map/ppermute | solution.py:32
  14.0 13.2 %copy-start.10 = (bf16[1,16,1024]{2,1,0:T(8,128)(2,1)}, bf16[1,16,1024]{2,1,0:T(8,128)(2,1)S(1)}, u32[]{:S(2)}) copy-start(bf16[1,16,1024]{2,1,0:T(8,128)(2,1)S(1)} %collective-permute-done.4.refs_10_) | copy-start | bytes 98308
  15.1 16.5 %copy-start.2 = (bf16[14,16,1024]{2,1,0:T(8,128)(2,1)}, bf16[14,16,1024]{2,1,0:T(8,128)(2,1)S(1)}, u32[]{:S(2)}) copy-start(bf16[14,16,1024]{2,1,0:T(8,128)(2,1)S(1)} %collective-permute-done.3.refs_1_) | copy-start | bytes 1376260
  15.1 12.1 %collective-permute-start.5 = (bf16[14,16,1024]{2,1,0:T(8,128)(2,1)S(1)}, bf16[14,16,1024]{2,1,0:T(8,128)(2,1)S(1)}, u32[]{:S(2)}, u32[]{:S(2)}) collective-permute-start(bf16[14,16,1024]{2,1,0:T(8,128)(2,1)S(1)} %collective-permute-done.3.refs_1_), channel_id=1, source_target_pairs={{0,3},{1,2},{2,1},{3,0},{4,7},{5,6},{6,5},{7,4},{8,11},{9,10},{10,... | collective-permute-start | bytes 1376264 | tf_op jit(solution)/shard_map/ppermute | solution.py:24
  18.1 17.4 %copy-start.3 = (bf16[13,16,1024]{2,1,0:T(8,128)(2,1)}, bf16[13,16,1024]{2,1,0:T(8,128)(2,1)S(1)}, u32[]{:S(2)}) copy-start(bf16[13,16,1024]{2,1,0:T(8,128)(2,1)S(1)} %collective-permute-done.refs_4_) | copy-start | bytes 1277956
  18.1 10.8 %collective-permute-start.1 = (bf16[13,16,1024]{2,1,0:T(8,128)(2,1)S(1)}, bf16[13,16,1024]{2,1,0:T(8,128)(2,1)S(1)}, u32[]{:S(2)}, u32[]{:S(2)}) collective-permute-start(bf16[13,16,1024]{2,1,0:T(8,128)(2,1)S(1)} %collective-permute-done.refs_4_), channel_id=1, source_target_pairs={{0,1},{1,0},{2,3},{3,2},{4,5},{5,4},{6,7},{7,6},{8,9},{9,8},{10,11... | collective-permute-start | bytes 1277960 | tf_op jit(solution)/shard_map/ppermute | solution.py:24
  18.2 17.4 %copy-start.4 = (bf16[13,16,1024]{2,1,0:T(8,128)(2,1)}, bf16[13,16,1024]{2,1,0:T(8,128)(2,1)S(1)}, u32[]{:S(2)}) copy-start(bf16[13,16,1024]{2,1,0:T(8,128)(2,1)S(1)} %collective-permute-done.6.refs_3_) | copy-start | bytes 1277956
  18.2 17.3 %collective-permute-start.8 = (bf16[13,16,1024]{2,1,0:T(8,128)(2,1)S(1)}, bf16[13,16,1024]{2,1,0:T(8,128)(2,1)S(1)}, u32[]{:S(2)}, u32[]{:S(2)}) collective-permute-start(bf16[13,16,1024]{2,1,0:T(8,128)(2,1)S(1)} %collective-permute-done.6.refs_3_), channel_id=1, source_target_pairs={{0,4},{4,0},{1,5},{5,1},{2,6},{6,2},{3,7},{7,3},{8,12},{12,8},{9,1... | collective-permute-start | bytes 1277960 | tf_op jit(solution)/shard_map/ppermute | solution.py:24
  27.2 4.5 %copy-start = (bf16[14,16,1024]{2,1,0:T(8,128)(2,1)}, bf16[14,16,1024]{2,1,0:T(8,128)(2,1)S(1)}, u32[]{:S(2)}) copy-start(bf16[14,16,1024]{2,1,0:T(8,128)(2,1)S(1)} %collective-permute-done.5.refs_2_) | copy-start | bytes 1376260
  27.2 8.3 %collective-permute-start.7 = (bf16[8,16,1024]{2,1,0:T(8,128)(2,1)S(1)}, bf16[8,16,1024]{2,1,0:T(8,128)(2,1)S(1)}, u32[]{:S(2)}, u32[]{:S(2)}) collective-permute-start(bf16[8,16,1024]{2,1,0:T(8,128)(2,1)S(1)} %slice.19), channel_id=1, source_target_pairs={{0,4},{4,0},{1,5},{5,1},{2,6},{6,2},{3,7},{7,3},{8,12},{12,8},{9,1... | collective-permute-start | bytes 786440 | tf_op jit(solution)/shard_map/ppermute | solution.py:24
  28.9 6.6 %copy-start.1 = (bf16[13,16,1024]{2,1,0:T(8,128)(2,1)}, bf16[13,16,1024]{2,1,0:T(8,128)(2,1)S(1)}, u32[]{:S(2)}) copy-start(bf16[13,16,1024]{2,1,0:T(8,128)(2,1)S(1)} %collective-permute-done.1.refs_5_) | copy-start | bytes 1277956
  29.0 5.8 %collective-permute-start.2 = (bf16[6,16,1024]{2,1,0:T(8,128)(2,1)S(1)}, bf16[6,16,1024]{2,1,0:T(8,128)(2,1)S(1)}, u32[]{:S(2)}, u32[]{:S(2)}) collective-permute-start(bf16[6,16,1024]{2,1,0:T(8,128)(2,1)S(1)} %slice.18), channel_id=1, source_target_pairs={{0,3},{1,2},{2,1},{3,0},{4,7},{5,6},{6,5},{7,4},{8,11},{9,10},{10,... | collective-permute-start | bytes 589832 | tf_op jit(solution)/shard_map/ppermute | solution.py:24
  31.7 3.9 %collective-permute-start.9 = (bf16[1,16,1024]{2,1,0:T(8,128)(2,1)S(1)}, bf16[1,16,1024]{2,1,0:T(8,128)(2,1)S(1)}, u32[]{:S(2)}, u32[]{:S(2)}) collective-permute-start(bf16[1,16,1024]{2,1,0:T(8,128)(2,1)S(1)} %get-tuple-element.41), channel_id=1, source_target_pairs={{0,8},{8,0},{1,9},{9,1},{2,10},{10,2},{3,11},{11,3},{4,12},{12,4},... | collective-permute-start | bytes 98312 | tf_op jit(solution)/shard_map/ppermute | solution.py:24
  34.8 6.5 %copy-start.7 = (bf16[6,16,1024]{2,1,0:T(8,128)(2,1)}, bf16[6,16,1024]{2,1,0:T(8,128)(2,1)S(1)}, u32[]{:S(2)}) copy-start(bf16[6,16,1024]{2,1,0:T(8,128)(2,1)S(1)} %collective-permute-done.2.refs_9_.refs_6_) | copy-start | bytes 589828
  41.3 4.4 %collective-permute-start.10 = (f32[432,128]{1,0:T(8,128)}, f32[432,128]{1,0:T(8,128)S(1)}, u32[]{:S(2)}, u32[]{:S(2)}) collective-permute-start(f32[432,128]{1,0:T(8,128)} %grad_kernel_terms.1), channel_id=1, source_target_pairs={{0,8},{8,0},{1,9},{9,1},{2,10},{10,2},{3,11},{11,3},{4,12},{12,4},... | collective-permute-start | bytes 663560 | tf_op jit(solution)/shard_map/ppermute | solution.py:24
  46.7 6.7 %collective-permute-start.11 = (f32[432,128]{1,0:T(8,128)S(1)}, f32[432,128]{1,0:T(8,128)S(1)}, u32[]{:S(2)}, u32[]{:S(2)}) collective-permute-start(f32[432,128]{1,0:T(8,128)S(1)} %add.12), channel_id=1, source_target_pairs={{0,16},{16,0},{32,48},{48,32},{1,17},{17,1},{33,49},{49,33},{2,18}... | collective-permute-start | bytes 663560 | tf_op jit(solution)/shard_map/ppermute | solution.py:24
  51.9 10.3 %collective-permute-start.12 = (f32[2,16,1024]{2,1,0:T(8,128)}, f32[2,16,1024]{2,1,0:T(8,128)S(1)}, u32[]{:S(2)}, u32[]{:S(2)}) collective-permute-start(f32[2,16,1024]{2,1,0:T(8,128)} %get-tuple-element.33), channel_id=1, source_target_pairs={{8,16},{16,8},{24,32},{32,24},{40,48},{48,40},{56,64},{64,56},{72,... | collective-permute-start | bytes 393224 | tf_op jit(solution)/shard_map/ppermute | solution.py:32
  53.4 9.2 %collective-permute-start.13 = (bf16[432,128]{1,0:T(8,128)(2,1)S(1)}, bf16[432,128]{1,0:T(8,128)(2,1)S(1)}, u32[]{:S(2)}, u32[]{:S(2)}) collective-permute-start(bf16[432,128]{1,0:T(8,128)(2,1)S(1)} %add_convert_fusion), channel_id=1, source_target_pairs={{0,48},{16,32},{32,16},{48,0},{1,49},{17,33},{33,17},{49,1},{2,50}... | collective-permute-start | bytes 331784 | tf_op jit(solution)/shard_map/ppermute | solution.py:24
  62.2 1.7 %copy-start.12 = (f32[2,16,1024]{2,1,0:T(8,128)S(1)}, f32[2,16,1024]{2,1,0:T(8,128)}, u32[]{:S(2)}) copy-start(f32[2,16,1024]{2,1,0:T(8,128)} %get-tuple-element.36) | copy-start | bytes 393220
  62.8 8.6 %collective-permute-start.15 = (f32[432,128]{1,0:T(8,128)S(1)}, f32[432,128]{1,0:T(8,128)S(1)}, u32[]{:S(2)}, u32[]{:S(2)}) collective-permute-start(f32[432,128]{1,0:T(8,128)S(1)} %convert_add_fusion), channel_id=1, source_target_pairs={{0,64},{64,0},{1,65},{65,1},{2,66},{66,2},{3,67},{67,3},{4,68},{68... | collective-permute-start | bytes 663560 | tf_op jit(solution)/shard_map/ppermute | solution.py:24
  63.9 2.7 %collective-permute-start.14 = (f32[2,16,1024]{2,1,0:T(8,128)S(1)}, f32[2,16,1024]{2,1,0:T(8,128)S(1)}, u32[]{:S(2)}, u32[]{:S(2)}) collective-permute-start(f32[2,16,1024]{2,1,0:T(8,128)S(1)} %copy-done.12), channel_id=1, source_target_pairs={{0,8},{8,0},{1,9},{9,1},{2,10},{10,2},{3,11},{11,3},{4,12},{12,4},... | collective-permute-start | bytes 393224 | tf_op jit(solution)/shard_map/ppermute | solution.py:24
  (5 other events, 3.4 us)

commit v2 on v1

--- a/solution.py
+++ b/solution.py
@@ -15,7 +15,7 @@
 CHAN = ("zl", "y")
 BF = jnp.bfloat16
 F32 = jnp.float32
-VMEM_LIMIT = 56 * 1024 * 1024
+VMEM_LIMIT = 32 * 1024 * 1024
 VM = pl.BlockSpec(memory_space=pltpu.VMEM)
 KEYS = [(0, 0), (0, 1), (0, 2), (0, 3), (1, 0), (1, 1), (1, 2), (1, 3)]
 
@@ -63,21 +63,30 @@
             field[z, pl.ds(row, 16), :] = ref[start + z]
 
 
-def pack_body(k_ref, a_ref, g_ref, by1, by3, byz, own, turned):
-    turned[:, 0:432] = jnp.transpose(k_ref[...].astype(F32))
+def pack_body(k_ref, a_ref, g_ref, by1, by3, byz, own, near, far, turned, k_in, a_in, g_in, sems):
+    copies = [pltpu.make_async_copy(src, dst, sems.at[n]) for n, (src, dst) in enumerate(((k_ref, k_in), (a_ref, a_in), (g_ref, g_in)))]
+    for copy in copies:
+        copy.start()
+    copies[0].wait()
+    turned[:, 0:432] = jnp.transpose(k_in[...].astype(F32))
     turned[:, 432:512] = jnp.zeros((C, 80), F32)
 
     def piece(key):
         return turned[pl.ds(first_row(key), 16), :].astype(BF)
 
     own[...] = piece((0, 0))
+    first = lax.axis_index("core") == 0
+    copies[1].wait()
+    copies[2].wait()
+    near[0] = jnp.where(first, g_in[N - 1].astype(F32), g_in[0].astype(F32)).astype(BF)
+    far[0] = jnp.where(first, g_in[0].astype(F32), g_in[N - 1].astype(F32)).astype(BF)
     for dst, pairs in (
-        (by1, (((0, 1), (0, 2)), ((1, 2), (1, 2)))),
+        (by1, (((0, 1), (0, 2)),)),
         (by3, (((0, 3), (1, 3)),)),
-        (byz, (((1, 0), (1, 1)),)),
+        (byz, (((1, 0), (1, 1)), ((1, 2), (1, 2)))),
     ):
-        dst[pl.ds(0, N)] = a_ref[...]
-        dst[pl.ds(N + len(pairs), N)] = g_ref[...]
+        dst[pl.ds(0, N)] = a_in[...]
+        dst[pl.ds(N + len(pairs), N)] = g_in[...]
         for n, (left, right) in enumerate(pairs):
             dst[N + n, :, 0:512] = piece(left)
             dst[N + n, :, 512:1024] = piece(right)
@@ -89,7 +98,7 @@
     pieces = [own[...].astype(F32)]
     for key, unit in zip(KEYS[1:], units[1:]):
         at = 512 if key in right else 0
-        pieces.append(unit[N + 1 if key == (1, 2) else N, :, pl.ds(at, 512)].astype(F32))
+        pieces.append(unit[1 if key == (1, 2) else N, :, pl.ds(at, 512)].astype(F32))
     for tap in range(27):
         tile, spot = divmod(tap * 16, C)
         row = None
@@ -101,21 +110,24 @@
         w_ref[pl.ds((26 - tap) * 16, 16), :] = row.astype(BF)
 
 
-def gk_body(*refs):
-    units, (g, g_in, g_out), (out,), (field, g9) = refs[:8], refs[8:11], refs[11:12], refs[12:]
-    core = lax.axis_index("core")
+def shifts_body(g, g_in, g_out, g9):
+    first = lax.axis_index("core") == 0
     y = lane_y()
     for p in range(N + 2):
         if p == 0:
-            plane = jnp.where(core == 0, g_out[0].astype(F32), g_in[0].astype(F32))
+            plane = jnp.where(first, g_out[0].astype(F32), g_in[0].astype(F32))
         elif p == N + 1:
-            plane = jnp.where(core == 0, g_in[0].astype(F32), g_out[0].astype(F32))
+            plane = jnp.where(first, g_in[0].astype(F32), g_out[0].astype(F32))
         else:
             plane = g[p - 1].astype(F32)
         slot = N + 1 - p
         for c, v in enumerate((from_y_after(plane, y), plane, from_y_before(plane, y))):
             for b, w in enumerate((pltpu.roll(v, CELLS - NXY, 1), v, pltpu.roll(v, NXY, 1))):
                 g9[pl.ds(slot * 144 + (b * 3 + c) * 16, 16), :] = w.astype(BF)
+
+
+def gk_body(*refs):
+    units, g9, keep, send, out, field = refs[:8], *refs[8:]
     for pair in range(N // 2):
         assemble([(u, 0) for u in units], field, True, pair)
         z = 2 * pair
@@ -127,6 +139,16 @@
             out[...] = term
         else:
             out[...] += term
+    core = lax.axis_index("core")
+    keep[...] = out[pl.ds(pl.multiple_of(core * 216, 8), 216), :]
+    send[...] = out[pl.ds(pl.multiple_of((1 - core) * 216, 8), 216), :]
+
+
+def join_body(mine, other, out):
+    core = lax.axis_index("core")
+    scale = 98304.0**-0.5
+    out[pl.ds(pl.multiple_of(core * 216, 8), 216), :] = mine[...] * scale
+    out[pl.ds(pl.multiple_of((1 - core) * 216, 8), 216), :] = other[...] * scale
 
 
 def fold(t, y):
@@ -134,7 +156,7 @@
     return s[16:32] + from_y_before(s[0:16], y) + from_y_after(s[32:48], y)
 
 
-G_STARTS = {(0, 0): 0, (1, 2): 0, (0, 1): N + 2, (0, 2): N + 2}
+G_STARTS = {(0, 0): 0, (1, 2): 2, (1, 0): N + 2, (1, 1): N + 2}
 
 
 def g_blocks(units):
@@ -143,10 +165,10 @@
 
 def edges_body(*refs):
     units, (g, z2g, w, own), (inner, outer, w_in), (field,) = refs[:8], refs[8:12], refs[12:15], refs[15:]
-    unpack_filter(own, units, w_in)
     y = lane_y()
     first = lax.axis_index("core") == 0
     g_units = [g, *units[1:6], z2g, units[7]]
+    unpack_filter(own, g_units, w_in)
     for n, (blocks, weights) in enumerate((([(u, 0) for u in units], w), (g_blocks(g_units), w_in))):
         for i, (key, (ref, start)) in enumerate(zip(KEYS, blocks)):
             row = first_row(key) if n == 0 else i * 16
@@ -200,11 +222,11 @@
                 out_ref[z - 1] = out.astype(BF)
 
 
-def call(body, name, args, outs, scratch=(), flops=0):
+def call(body, name, args, outs, scratch=(), flops=0, anywhere=0):
     return pl.pallas_call(
         body,
         out_shape=[jax.ShapeDtypeStruct(s, d) for s, d in outs],
-        in_specs=[VM] * len(args),
+        in_specs=[pl.BlockSpec(memory_space=pl.ANY)] * anywhere + [VM] * (len(args) - anywhere),
         out_specs=[VM] * len(outs),
         scratch_shapes=list(scratch),
         compiler_params=pltpu.CompilerParams(vmem_limit_bytes=VMEM_LIMIT),
@@ -222,39 +244,49 @@
     kt = jnp.swapaxes(kernel, 3, 4).reshape(432, C)
     plane = (16, CELLS)
 
-    by1, by3, byz, own = call(
+    by1, by3, byz, own, g_in, g_out = call(
         pack_body,
         "pack_messages",
         [kt, activation, cotangent],
-        [((N * 2 + 2, *plane), BF), ((N * 2 + 1, *plane), BF), ((N * 2 + 1, *plane), BF), ((16, 512), BF)],
-        [pltpu.VMEM((C, 512), F32)],
+        [((N * 2 + 1, *plane), BF), ((N * 2 + 1, *plane), BF), ((N * 2 + 2, *plane), BF), ((16, 512), BF)]
+        + [((1, *plane), BF)] * 2,
+        [pltpu.VMEM((C, 512), F32), pltpu.VMEM((432, C), BF)]
+        + [pltpu.VMEM((N, *plane), BF)] * 2
+        + [pltpu.SemaphoreType.DMA((3,))],
+        anywhere=3,
     )
     k1 = swap(by1, "y", 1)
     k3 = swap(by3, "y", 3)
     z0 = swap(byz, "zl", 1)
-    g_in = swap(jnp.where(core == 0, cotangent[N - 1 :], cotangent[:1]), "core", 1)
-    g_out = outer_swap(jnp.where(core == 0, cotangent[:1], cotangent[N - 1 :]))
-    k2 = swap(after(k1, g_out), "y", 3)
+    g_in = swap(g_in, "core", 1)
+    g_out = outer_swap(g_out)
+    k2 = swap(after(k1, g_out, g_in), "y", 3)
     z1 = swap(z0, "y", 1)
     z3 = swap(k3, "zl", 1)
-    z2a = swap(k2[: N + 2], "zl", 1)
-    z2g = swap(z1[N + 1 :], "y", 3)
+    (moved,) = call(
+        shifts_body,
+        "moved_cotangent",
+        [after(cotangent, k1), g_in, g_out],
+        [(((N + 2) * 144, CELLS), BF)],
+    )
+    z2a = swap(after(k2[:N], moved), "zl", 1)
+    z2g = swap(z1[N:], "y", 3)
 
     units = [k1, k2, k3, z0, z1, z2a, z3]
-    terms = call(
+    keep, send = call(
         gk_body,
         "grad_kernel_terms",
-        [after(activation, z2g), *units, cotangent, g_in, g_out],
-        [((432, C), F32)],
-        [FIELD, pltpu.VMEM(((N + 2) * 144, CELLS), BF)],
+        [activation, *units, moved],
+        [((216, C), F32)] * 2,
+        [pltpu.VMEM((432, C), F32), FIELD],
         CONV_FLOPS,
-    )[0]
-    terms = terms + swap(terms, "core", 1)
+    )
+    terms = after(keep, z2g) + swap(send, "core", 1)
     got = swap(terms, "x", 1)
     inner, outer, w_in = call(
         edges_body,
         "edge_terms",
-        [after(activation, terms), *units, cotangent, z2g, kt, own],
+        [after(activation, keep), *units, cotangent, z2g, kt, own],
         [((2, *plane), F32)] * 2 + [((432, C), BF)],
         [pltpu.VMEM((4, C, CELLS), BF)],
         CONV_FLOPS // 9,
@@ -271,7 +303,7 @@
         [FIELD, pltpu.VMEM((288, CELLS), F32)],
         CONV_FLOPS,
     )
-    terms = after(terms, ends, outer).astype(F32) + got.astype(F32)
+    terms = after(terms, ends, outer, inner).astype(F32) + got.astype(F32)
     got = swap(terms, "zh", 1)
     grad_input, output = call(
         functools.partial(conv_body, 1),
@@ -281,8 +313,9 @@
         [FIELD, pltpu.VMEM((288, CELLS), F32)],
         CONV_FLOPS,
     )
-    terms = (after(terms, grad_input) + got) * 98304.0**-0.5
-    grad_kernel = jnp.swapaxes(terms.reshape(3, 3, 3, 16, C), 3, 4)
+    terms = after(terms, grad_input) + got
+    (joined,) = call(join_body, "join_grad_kernel", [terms, swap(terms, "core", 1)], [((432, C), F32)])
+    grad_kernel = jnp.swapaxes(joined.reshape(3, 3, 3, 16, C), 3, 4)
     return (output, grad_input, grad_kernel)
 
 

time: 72.4 us -> 60.8 us (0.84)
  Pallas kernels: 18.6 us -> 8.9 us
  waiting for transfers between devices: 14.8 us -> 17.3 us
  other arithmetic: 2.53 us -> 0.06 us
  starting transfers between devices: 33.2 us -> 30.9 us
    pallas_call x5 -> x7, Pallas kernels: 18.6 us -> 8.9 us  [call(): pl.pallas_call(body, out_shape=[jax.ShapeDtypeStruct(s, d) for s, d in ou...]
    ppermute x14 -> x15, waiting for transfers between devices: 12.9 us -> 17.3 us  [swap(): lax.ppermute(v, axis, [(i, i ^ bits) for i in range(lax.axis_size(axis))])]
    ppermute x14 -> x15, starting transfers between devices: 29.8 us -> 27.4 us  [swap(): lax.ppermute(v, axis, [(i, i ^ bits) for i in range(lax.axis_size(axis))])]
    ppermute x2, waiting for transfers between devices: 1.9 us -> 0.01 us  [outer_swap(): return lax.ppermute(v, SPACE, pairs)]
    add x2 -> x3, other arithmetic: 0.99 us -> 0.04 us  [the longest x1 0.01 us: on_device(): terms = after(terms, ends, outer, inner).astype(F32) + got.astype(F32)]
    select_n x1 -> x0, other arithmetic: 0.78 us -> none  [on_device(): jnp.where(core == 0, cotangent[N - 1:], cotangent[:1])]
    unnamed x26 -> x8, local copies, waits for them, and re-layouts: 2.29 us -> 2.75 us
  transfers between devices with their start and end apart: 16 -> 17, of which waited for: 10 -> 9; matrix products, arithmetic and copies ran while one was open for 1% -> 0% of each run, Pallas kernels for 17% -> 12%
where the time goes in v2:
time: 60.8 us; the launch traced here: 60.7 us
  starting transfers between devices  30.9 us (51%)
  waiting for transfers between devices  17.3 us (28%)
  Pallas kernels  8.9 us (15%)
  local copies, waits for them, and re-layouts  2.78 us (5%)
  between operations  0.74 us (1%)
    ppermute x15, starting transfers between devices, swap(): lax.ppermute(v, axis, [(i, i ^ bits) for i in range(lax.axis_size(axis))])  27.4 us
    ppermute x15, waiting for transfers between devices, swap(): lax.ppermute(v, axis, [(i, i ^ bits) for i in range(lax.axis_size(axis))])  17.3 us
    pallas_call x7, Pallas kernels, call(): pl.pallas_call(body, out_shape=[jax.ShapeDtypeStruct(s, d) for s, d in ou...  8.9 us
    ppermute x2, starting transfers between devices, outer_swap(): return lax.ppermute(v, SPACE, pairs)  3.57 us
    unnamed x8, local copies, waits for them, and re-layouts  2.75 us
  transfers between devices with their start and end apart: 17, of which 9 were waited for; matrix products, arithmetic and copies ran while one was open for 0% of the time, Pallas kernels for 12%

profile of v2, /device:TPU:1, one launch (start us, length us, event | category | flops | bytes accessed | tf_op | source)
XLA Modules:
  0.0 60.7 jit_solution(16637236458268005779)
XLA Ops:
  4.3 2.2 %collective-permute-start = (bf16[13,16,1024]{2,1,0:T(8,128)(2,1)S(1)}, bf16[13,16,1024]{2,1,0:T(8,128)(2,1)S(1)}, u32[]{:S(2)}, u32[]{:S(2)}) collective-permute-start(bf16[13,16,1024]{2,1,0:T(8,128)(2,1)S(1)} %get-tuple-element.28), channel_id=1, source_target_pairs={{0,1},{1,0},{2,3},{3,2},{4,5},{5,4},{6,7},{7,6},{8,9},{9,8},{10,11... | collective-permute-start | bytes 1277960 | tf_op jit(solution)/shard_map/ppermute | solution.py:24
  6.5 1.6 %collective-permute-start.5 = (bf16[14,16,1024]{2,1,0:T(8,128)(2,1)S(1)}, bf16[14,16,1024]{2,1,0:T(8,128)(2,1)S(1)}, u32[]{:S(2)}, u32[]{:S(2)}) collective-permute-start(bf16[14,16,1024]{2,1,0:T(8,128)(2,1)S(1)} %get-tuple-element.33), channel_id=1, source_target_pairs={{0,4},{4,0},{1,5},{5,1},{2,6},{6,2},{3,7},{7,3},{8,12},{12,8},{9,1... | collective-permute-start | bytes 1376264 | tf_op jit(solution)/shard_map/ppermute | solution.py:24
  8.1 1.9 %collective-permute-start.4 = (bf16[13,16,1024]{2,1,0:T(8,128)(2,1)S(1)}, bf16[13,16,1024]{2,1,0:T(8,128)(2,1)S(1)}, u32[]{:S(2)}, u32[]{:S(2)}) collective-permute-start(bf16[13,16,1024]{2,1,0:T(8,128)(2,1)S(1)} %get-tuple-element.32), channel_id=1, source_target_pairs={{0,3},{1,2},{2,1},{3,0},{4,7},{5,6},{6,5},{7,4},{8,11},{9,10},{10,... | collective-permute-start | bytes 1277960 | tf_op jit(solution)/shard_map/ppermute | solution.py:24
  10.0 2.6 %collective-permute-start.1 = (bf16[1,16,1024]{2,1,0:T(8,128)(2,1)S(1)}, bf16[1,16,1024]{2,1,0:T(8,128)(2,1)S(1)}, u32[]{:S(2)}, u32[]{:S(2)}) collective-permute-start(bf16[1,16,1024]{2,1,0:T(8,128)(2,1)S(1)} %get-tuple-element.29), channel_id=1, source_target_pairs={{8,16},{16,8},{24,32},{32,24},{40,48},{48,40},{56,64},{64,56},{72,... | collective-permute-start | bytes 98312 | tf_op jit(solution)/shard_map/ppermute | solution.py:32
  12.6 3.3 %collective-permute-start.2 = (bf16[1,16,1024]{2,1,0:T(8,128)(2,1)S(1)}, bf16[1,16,1024]{2,1,0:T(8,128)(2,1)S(1)}, u32[]{:S(2)}, u32[]{:S(2)}) collective-permute-start(bf16[1,16,1024]{2,1,0:T(8,128)(2,1)S(1)} %get-tuple-element.30), channel_id=1, source_target_pairs={{0,8},{8,0},{1,9},{9,1},{2,10},{10,2},{3,11},{11,3},{4,12},{12,4},... | collective-permute-start | bytes 98312 | tf_op jit(solution)/shard_map/ppermute | solution.py:24
  16.8 1.8 %collective-permute-start.3 = (bf16[13,16,1024]{2,1,0:T(8,128)(2,1)S(1)}, bf16[13,16,1024]{2,1,0:T(8,128)(2,1)S(1)}, u32[]{:S(2)}, u32[]{:S(2)}) collective-permute-start(bf16[13,16,1024]{2,1,0:T(8,128)(2,1)S(1)} %collective-permute-done.refs_1_), channel_id=1, source_target_pairs={{0,3},{1,2},{2,1},{3,0},{4,7},{5,6},{6,5},{7,4},{8,11},{9,10},{10,... | collective-permute-start | bytes 1277960 | tf_op jit(solution)/shard_map/ppermute | solution.py:24
  20.3 1.1 %moved_cotangent.1.refs_8_ = bf16[1152,1024]{1,0:T(8,128)(2,1)S(1)} custom-call(bf16[6,16,1024]{2,1,0:T(8,128)(2,1)S(1)} %copy-done, bf16[1,16,1024]{2,1,0:T(8,128)(2,1)S(1)} %collective-permute-done.2.g_in, bf16[1,16,1024]{2,1,0:T(8,128)(2,1)S(1)} %collective-permute-done.1.g_out), custom_call_target="tpu_custom_call" | custom-call | bytes 1048576 | tf_op jit(solution)/shard_map/moved_cotangent/pallas_call | solution.py:226
  21.5 6.9 %collective-permute-done.3.refs_2_ = bf16[13,16,1024]{2,1,0:T(8,128)(2,1)S(1)} collective-permute-done((bf16[13,16,1024]{2,1,0:T(8,128)(2,1)S(1)}, bf16[13,16,1024]{2,1,0:T(8,128)(2,1)S(1)}, u32[]{:S(2)}, u32[]{:S(2)}) %collective-permute-start.3) | collective-permute-done | bytes 426016 | tf_op jit(solution)/shard_map/ppermute | solution.py:24
  28.8 2.6 %collective-permute-start.9 = (bf16[8,16,1024]{2,1,0:T(8,128)(2,1)S(1)}, bf16[8,16,1024]{2,1,0:T(8,128)(2,1)S(1)}, u32[]{:S(2)}, u32[]{:S(2)}) collective-permute-start(bf16[8,16,1024]{2,1,0:T(8,128)(2,1)S(1)} %slice.9), channel_id=1, source_target_pairs={{0,3},{1,2},{2,1},{3,0},{4,7},{5,6},{6,5},{7,4},{8,11},{9,10},{10,... | collective-permute-start | bytes 786440 | tf_op jit(solution)/shard_map/ppermute | solution.py:24
  31.4 1.6 %collective-permute-done.7.refs_6_ = bf16[6,16,1024]{2,1,0:T(8,128)(2,1)S(1)} collective-permute-done((bf16[6,16,1024]{2,1,0:T(8,128)(2,1)S(1)}, bf16[6,16,1024]{2,1,0:T(8,128)(2,1)S(1)}, u32[]{:S(2)}, u32[]{:S(2)}) %collective-permute-start.7) | collective-permute-done | bytes 196640 | tf_op jit(solution)/shard_map/ppermute | solution.py:24
  33.0 1.3 %grad_kernel_terms.1 = (f32[216,128]{1,0:T(8,128)S(1)}, f32[216,128]{1,0:T(8,128)S(1)}) custom-call(bf16[6,16,1024]{2,1,0:T(8,128)(2,1)S(1)} %copy-done.2, bf16[13,16,1024]{2,1,0:T(8,128)(2,1)S(1)} %collective-permute-done.refs_1_, bf16[13,16,1024]{2,1,0:T(8,128)(2,1)S(1)} %collective-permute-done.3.refs_2_, ...), custom_call_target="tpu_custom_call" | custom-call | flops 679477248 | bytes 1048576 | tf_op jit(solution)/shard_map/grad_kernel_terms/pallas_call | solution.py:226
  34.3 3.5 %collective-permute-start.10 = (f32[216,128]{1,0:T(8,128)S(1)}, f32[216,128]{1,0:T(8,128)S(1)}, u32[]{:S(2)}, u32[]{:S(2)}) collective-permute-start(f32[216,128]{1,0:T(8,128)S(1)} %get-tuple-element.38), channel_id=1, source_target_pairs={{0,8},{8,0},{1,9},{9,1},{2,10},{10,2},{3,11},{11,3},{4,12},{12,4},... | collective-permute-start | bytes 331784 | tf_op jit(solution)/shard_map/ppermute | solution.py:24
  37.8 1.0 %collective-permute-done.10 = f32[216,128]{1,0:T(8,128)S(1)} collective-permute-done((f32[216,128]{1,0:T(8,128)S(1)}, f32[216,128]{1,0:T(8,128)S(1)}, u32[]{:S(2)}, u32[]{:S(2)}) %collective-permute-start.10) | collective-permute-done | bytes 110624 | tf_op jit(solution)/shard_map/ppermute | solution.py:24
  38.8 1.3 %collective-permute-start.11 = (f32[216,128]{1,0:T(8,128)S(1)}, f32[216,128]{1,0:T(8,128)S(1)}, u32[]{:S(2)}, u32[]{:S(2)}) collective-permute-start(f32[216,128]{1,0:T(8,128)S(1)} %add.12), channel_id=1, source_target_pairs={{0,16},{16,0},{32,48},{48,32},{1,17},{17,1},{33,49},{49,33},{2,18}... | collective-permute-start | bytes 331784 | tf_op jit(solution)/shard_map/ppermute | solution.py:24
  40.1 1.2 %edge_terms.1 = (f32[2,16,1024]{2,1,0:T(8,128)S(1)}, f32[2,16,1024]{2,1,0:T(8,128)S(1)}, bf16[432,128]{1,0:T(8,128)(2,1)S(1)}) custom-call(bf16[6,16,1024]{2,1,0:T(8,128)(2,1)S(1)} %copy-done.2, bf16[13,16,1024]{2,1,0:T(8,128)(2,1)S(1)} %collective-permute-done.refs_1_, bf16[13,16,1024]{2,1,0:T(8,128)(2,1)S(1)} %collective-permute-done.3.refs_2_, ...), custom_call_target="tpu_custom_call" | custom-call | flops 75497472 | bytes 1048576 | tf_op jit(solution)/shard_map/edge_terms/pallas_call | solution.py:226
  41.3 1.0 %collective-permute-start.12 = (f32[2,16,1024]{2,1,0:T(8,128)S(1)}, f32[2,16,1024]{2,1,0:T(8,128)S(1)}, u32[]{:S(2)}, u32[]{:S(2)}) collective-permute-start(f32[2,16,1024]{2,1,0:T(8,128)S(1)} %get-tuple-element.45), channel_id=1, source_target_pairs={{8,16},{16,8},{24,32},{32,24},{40,48},{48,40},{56,64},{64,56},{72,... | collective-permute-start | bytes 393224 | tf_op jit(solution)/shard_map/ppermute | solution.py:32
  42.3 4.6 %collective-permute-start.13 = (f32[2,16,1024]{2,1,0:T(8,128)S(1)}, f32[2,16,1024]{2,1,0:T(8,128)S(1)}, u32[]{:S(2)}, u32[]{:S(2)}) collective-permute-start(f32[2,16,1024]{2,1,0:T(8,128)S(1)} %get-tuple-element.46), channel_id=1, source_target_pairs={{0,8},{8,0},{1,9},{9,1},{2,10},{10,2},{3,11},{11,3},{4,12},{12,4},... | collective-permute-start | bytes 393224 | tf_op jit(solution)/shard_map/ppermute | solution.py:24
  47.0 1.2 %collective-permute-start.14 = (bf16[216,128]{1,0:T(8,128)(2,1)S(1)}, bf16[216,128]{1,0:T(8,128)(2,1)S(1)}, u32[]{:S(2)}, u32[]{:S(2)}) collective-permute-start(bf16[216,128]{1,0:T(8,128)(2,1)S(1)} %add_convert_fusion), channel_id=1, source_target_pairs={{0,48},{16,32},{32,16},{48,0},{1,49},{17,33},{33,17},{49,1},{2,50}... | collective-permute-start | bytes 165896 | tf_op jit(solution)/shard_map/ppermute | solution.py:24
  48.1 1.5 %output_planes.1 = (bf16[4,16,1024]{2,1,0:T(8,128)(2,1)S(1)}, f32[2,16,1024]{2,1,0:T(8,128)S(1)}) custom-call(bf16[6,16,1024]{2,1,0:T(8,128)(2,1)S(1)} %copy-done.2, bf16[13,16,1024]{2,1,0:T(8,128)(2,1)S(1)} %collective-permute-done.refs_1_, bf16[13,16,1024]{2,1,0:T(8,128)(2,1)S(1)} %collective-permute-done.3.refs_2_, ...), custom_call_target="tpu_custom_call" | custom-call | flops 679477248 | bytes 1048576 | tf_op jit(solution)/shard_map/output_planes/pallas_call | solution.py:226
  49.6 2.1 %collective-permute-done.14 = bf16[216,128]{1,0:T(8,128)(2,1)S(1)} collective-permute-done((bf16[216,128]{1,0:T(8,128)(2,1)S(1)}, bf16[216,128]{1,0:T(8,128)(2,1)S(1)}, u32[]{:S(2)}, u32[]{:S(2)}) %collective-permute-start.14) | collective-permute-done | bytes 55328 | tf_op jit(solution)/shard_map/ppermute | solution.py:24
  51.9 2.2 %grad_input_planes.1 = (bf16[6,16,1024]{2,1,0:T(8,128)(2,1)}, bf16[6,16,1024]{2,1,0:T(8,128)(2,1)}) custom-call(bf16[6,16,1024]{2,1,0:T(8,128)(2,1)S(1)} %copy-done, bf16[13,16,1024]{2,1,0:T(8,128)(2,1)S(1)} %collective-permute-done.refs_1_, bf16[13,16,1024]{2,1,0:T(8,128)(2,1)S(1)} %collective-permute-done.3.refs_2_, ...), custom_call_target="tpu_custom_call" | custom-call | flops 679477248 | bytes 1048576 | tf_op jit(solution)/shard_map/grad_input_planes/pallas_call | solution.py:226
  54.0 2.9 %collective-permute-done.15 = f32[216,128]{1,0:T(8,128)S(1)} collective-permute-done((f32[216,128]{1,0:T(8,128)S(1)}, f32[216,128]{1,0:T(8,128)S(1)}, u32[]{:S(2)}, u32[]{:S(2)}) %collective-permute-start.15) | collective-permute-done | bytes 110624 | tf_op jit(solution)/shard_map/ppermute | solution.py:24
  57.0 2.0 %collective-permute-start.16 = (f32[216,128]{1,0:T(8,128)S(1)}, f32[216,128]{1,0:T(8,128)S(1)}, u32[]{:S(2)}, u32[]{:S(2)}) collective-permute-start(f32[216,128]{1,0:T(8,128)S(1)} %add.15.mine), channel_id=1, source_target_pairs={{0,8},{8,0},{1,9},{9,1},{2,10},{10,2},{3,11},{11,3},{4,12},{12,4},... | collective-permute-start | bytes 331784 | tf_op jit(solution)/shard_map/ppermute | solution.py:24
  59.0 1.0 %collective-permute-done.16.other = f32[216,128]{1,0:T(8,128)S(1)} collective-permute-done((f32[216,128]{1,0:T(8,128)S(1)}, f32[216,128]{1,0:T(8,128)S(1)}, u32[]{:S(2)}, u32[]{:S(2)}) %collective-permute-start.16) | collective-permute-done | bytes 110624 | tf_op jit(solution)/shard_map/ppermute | solution.py:24
  (31 shorter events, 7.5 us)
Async XLA Ops:
  0.6 0.9 %copy-start = (bf16[6,16,1024]{2,1,0:T(8,128)(2,1)S(1)}, bf16[6,16,1024]{2,1,0:T(8,128)(2,1)}, u32[]{:S(2)}) copy-start(bf16[6,16,1024]{2,1,0:T(8,128)(2,1)} %refs_0_.4) | copy-start | bytes 589828
  1.6 0.9 %copy-start.1 = (bf16[6,16,1024]{2,1,0:T(8,128)(2,1)S(1)}, bf16[6,16,1024]{2,1,0:T(8,128)(2,1)}, u32[]{:S(2)}) copy-start(bf16[6,16,1024]{2,1,0:T(8,128)(2,1)} %refs_0_.3) | copy-start | bytes 589828
  2.5 0.9 %copy-start.3 = (bf16[3,3,3,128,16]{3,4,2,1,0:T(8,128)(2,1)S(1)}, bf16[3,3,3,128,16]{3,4,2,1,0:T(8,128)(2,1)}, u32[]{:S(2)}) copy-start(bf16[3,3,3,128,16]{3,4,2,1,0:T(8,128)(2,1)} %param.5) | copy-start | bytes 331780
  3.4 29.7 %copy-start.2 = (bf16[6,16,1024]{2,1,0:T(8,128)(2,1)S(1)}, bf16[6,16,1024]{2,1,0:T(8,128)(2,1)}, u32[]{:S(2)}) copy-start(bf16[6,16,1024]{2,1,0:T(8,128)(2,1)} %refs_0_.3) | copy-start | bytes 589828
  4.3 12.5 %collective-permute-start = (bf16[13,16,1024]{2,1,0:T(8,128)(2,1)S(1)}, bf16[13,16,1024]{2,1,0:T(8,128)(2,1)S(1)}, u32[]{:S(2)}, u32[]{:S(2)}) collective-permute-start(bf16[13,16,1024]{2,1,0:T(8,128)(2,1)S(1)} %get-tuple-element.28), channel_id=1, source_target_pairs={{0,1},{1,0},{2,3},{3,2},{4,5},{5,4},{6,7},{7,6},{8,9},{9,8},{10,11... | collective-permute-start | bytes 1277960 | tf_op jit(solution)/shard_map/ppermute | solution.py:24
  6.5 12.1 %collective-permute-start.5 = (bf16[14,16,1024]{2,1,0:T(8,128)(2,1)S(1)}, bf16[14,16,1024]{2,1,0:T(8,128)(2,1)S(1)}, u32[]{:S(2)}, u32[]{:S(2)}) collective-permute-start(bf16[14,16,1024]{2,1,0:T(8,128)(2,1)S(1)} %get-tuple-element.33), channel_id=1, source_target_pairs={{0,4},{4,0},{1,5},{5,1},{2,6},{6,2},{3,7},{7,3},{8,12},{12,8},{9,1... | collective-permute-start | bytes 1376264 | tf_op jit(solution)/shard_map/ppermute | solution.py:24
  8.1 11.3 %collective-permute-start.4 = (bf16[13,16,1024]{2,1,0:T(8,128)(2,1)S(1)}, bf16[13,16,1024]{2,1,0:T(8,128)(2,1)S(1)}, u32[]{:S(2)}, u32[]{:S(2)}) collective-permute-start(bf16[13,16,1024]{2,1,0:T(8,128)(2,1)S(1)} %get-tuple-element.32), channel_id=1, source_target_pairs={{0,3},{1,2},{2,1},{3,0},{4,7},{5,6},{6,5},{7,4},{8,11},{9,10},{10,... | collective-permute-start | bytes 1277960 | tf_op jit(solution)/shard_map/ppermute | solution.py:24
  10.0 5.9 %collective-permute-start.1 = (bf16[1,16,1024]{2,1,0:T(8,128)(2,1)S(1)}, bf16[1,16,1024]{2,1,0:T(8,128)(2,1)S(1)}, u32[]{:S(2)}, u32[]{:S(2)}) collective-permute-start(bf16[1,16,1024]{2,1,0:T(8,128)(2,1)S(1)} %get-tuple-element.29), channel_id=1, source_target_pairs={{8,16},{16,8},{24,32},{32,24},{40,48},{48,40},{56,64},{64,56},{72,... | collective-permute-start | bytes 98312 | tf_op jit(solution)/shard_map/ppermute | solution.py:32
  12.6 4.1 %collective-permute-start.2 = (bf16[1,16,1024]{2,1,0:T(8,128)(2,1)S(1)}, bf16[1,16,1024]{2,1,0:T(8,128)(2,1)S(1)}, u32[]{:S(2)}, u32[]{:S(2)}) collective-permute-start(bf16[1,16,1024]{2,1,0:T(8,128)(2,1)S(1)} %get-tuple-element.30), channel_id=1, source_target_pairs={{0,8},{8,0},{1,9},{9,1},{2,10},{10,2},{3,11},{11,3},{4,12},{12,4},... | collective-permute-start | bytes 98312 | tf_op jit(solution)/shard_map/ppermute | solution.py:24
  16.8 11.6 %collective-permute-start.3 = (bf16[13,16,1024]{2,1,0:T(8,128)(2,1)S(1)}, bf16[13,16,1024]{2,1,0:T(8,128)(2,1)S(1)}, u32[]{:S(2)}, u32[]{:S(2)}) collective-permute-start(bf16[13,16,1024]{2,1,0:T(8,128)(2,1)S(1)} %collective-permute-done.refs_1_), channel_id=1, source_target_pairs={{0,3},{1,2},{2,1},{3,0},{4,7},{5,6},{6,5},{7,4},{8,11},{9,10},{10,... | collective-permute-start | bytes 1277960 | tf_op jit(solution)/shard_map/ppermute | solution.py:24
  18.6 10.2 %collective-permute-start.6 = (bf16[14,16,1024]{2,1,0:T(8,128)(2,1)S(1)}, bf16[14,16,1024]{2,1,0:T(8,128)(2,1)S(1)}, u32[]{:S(2)}, u32[]{:S(2)}) collective-permute-start(bf16[14,16,1024]{2,1,0:T(8,128)(2,1)S(1)} %collective-permute-done.5.refs_4_), channel_id=1, source_target_pairs={{0,1},{1,0},{2,3},{3,2},{4,5},{5,4},{6,7},{7,6},{8,9},{9,8},{10,11... | collective-permute-start | bytes 1376264 | tf_op jit(solution)/shard_map/ppermute | solution.py:24
  19.4 12.0 %collective-permute-start.8 = (bf16[13,16,1024]{2,1,0:T(8,128)(2,1)S(1)}, bf16[13,16,1024]{2,1,0:T(8,128)(2,1)S(1)}, u32[]{:S(2)}, u32[]{:S(2)}) collective-permute-start(bf16[13,16,1024]{2,1,0:T(8,128)(2,1)S(1)} %collective-permute-done.4.refs_3_), channel_id=1, source_target_pairs={{0,4},{4,0},{1,5},{5,1},{2,6},{6,2},{3,7},{7,3},{8,12},{12,8},{9,1... | collective-permute-start | bytes 1277960 | tf_op jit(solution)/shard_map/ppermute | solution.py:24
  28.4 4.6 %collective-permute-start.7 = (bf16[6,16,1024]{2,1,0:T(8,128)(2,1)S(1)}, bf16[6,16,1024]{2,1,0:T(8,128)(2,1)S(1)}, u32[]{:S(2)}, u32[]{:S(2)}) collective-permute-start(bf16[6,16,1024]{2,1,0:T(8,128)(2,1)S(1)} %slice.8), channel_id=1, source_target_pairs={{0,4},{4,0},{1,5},{5,1},{2,6},{6,2},{3,7},{7,3},{8,12},{12,8},{9,1... | collective-permute-start | bytes 589832 | tf_op jit(solution)/shard_map/ppermute | solution.py:24
  28.8 9.0 %collective-permute-start.9 = (bf16[8,16,1024]{2,1,0:T(8,128)(2,1)S(1)}, bf16[8,16,1024]{2,1,0:T(8,128)(2,1)S(1)}, u32[]{:S(2)}, u32[]{:S(2)}) collective-permute-start(bf16[8,16,1024]{2,1,0:T(8,128)(2,1)S(1)} %slice.9), channel_id=1, source_target_pairs={{0,3},{1,2},{2,1},{3,0},{4,7},{5,6},{6,5},{7,4},{8,11},{9,10},{10,... | collective-permute-start | bytes 786440 | tf_op jit(solution)/shard_map/ppermute | solution.py:24
  34.3 4.4 %collective-permute-start.10 = (f32[216,128]{1,0:T(8,128)S(1)}, f32[216,128]{1,0:T(8,128)S(1)}, u32[]{:S(2)}, u32[]{:S(2)}) collective-permute-start(f32[216,128]{1,0:T(8,128)S(1)} %get-tuple-element.38), channel_id=1, source_target_pairs={{0,8},{8,0},{1,9},{9,1},{2,10},{10,2},{3,11},{11,3},{4,12},{12,4},... | collective-permute-start | bytes 331784 | tf_op jit(solution)/shard_map/ppermute | solution.py:24
  38.8 8.2 %collective-permute-start.11 = (f32[216,128]{1,0:T(8,128)S(1)}, f32[216,128]{1,0:T(8,128)S(1)}, u32[]{:S(2)}, u32[]{:S(2)}) collective-permute-start(f32[216,128]{1,0:T(8,128)S(1)} %add.12), channel_id=1, source_target_pairs={{0,16},{16,0},{32,48},{48,32},{1,17},{17,1},{33,49},{49,33},{2,18}... | collective-permute-start | bytes 331784 | tf_op jit(solution)/shard_map/ppermute | solution.py:24
  41.3 8.3 %collective-permute-start.12 = (f32[2,16,1024]{2,1,0:T(8,128)S(1)}, f32[2,16,1024]{2,1,0:T(8,128)S(1)}, u32[]{:S(2)}, u32[]{:S(2)}) collective-permute-start(f32[2,16,1024]{2,1,0:T(8,128)S(1)} %get-tuple-element.45), channel_id=1, source_target_pairs={{8,16},{16,8},{24,32},{32,24},{40,48},{48,40},{56,64},{64,56},{72,... | collective-permute-start | bytes 393224 | tf_op jit(solution)/shard_map/ppermute | solution.py:32
  42.3 7.3 %collective-permute-start.13 = (f32[2,16,1024]{2,1,0:T(8,128)S(1)}, f32[2,16,1024]{2,1,0:T(8,128)S(1)}, u32[]{:S(2)}, u32[]{:S(2)}) collective-permute-start(f32[2,16,1024]{2,1,0:T(8,128)S(1)} %get-tuple-element.46), channel_id=1, source_target_pairs={{0,8},{8,0},{1,9},{9,1},{2,10},{10,2},{3,11},{11,3},{4,12},{12,4},... | collective-permute-start | bytes 393224 | tf_op jit(solution)/shard_map/ppermute | solution.py:24
  47.0 4.8 %collective-permute-start.14 = (bf16[216,128]{1,0:T(8,128)(2,1)S(1)}, bf16[216,128]{1,0:T(8,128)(2,1)S(1)}, u32[]{:S(2)}, u32[]{:S(2)}) collective-permute-start(bf16[216,128]{1,0:T(8,128)(2,1)S(1)} %add_convert_fusion), channel_id=1, source_target_pairs={{0,48},{16,32},{32,16},{48,0},{1,49},{17,33},{33,17},{49,1},{2,50}... | collective-permute-start | bytes 165896 | tf_op jit(solution)/shard_map/ppermute | solution.py:24
  51.8 5.2 %collective-permute-start.15 = (f32[216,128]{1,0:T(8,128)S(1)}, f32[216,128]{1,0:T(8,128)S(1)}, u32[]{:S(2)}, u32[]{:S(2)}) collective-permute-start(f32[216,128]{1,0:T(8,128)S(1)} %convert_add_fusion), channel_id=1, source_target_pairs={{0,64},{64,0},{1,65},{65,1},{2,66},{66,2},{3,67},{67,3},{4,68},{68... | collective-permute-start | bytes 331784 | tf_op jit(solution)/shard_map/ppermute | solution.py:24
  57.0 3.0 %collective-permute-start.16 = (f32[216,128]{1,0:T(8,128)S(1)}, f32[216,128]{1,0:T(8,128)S(1)}, u32[]{:S(2)}, u32[]{:S(2)}) collective-permute-start(f32[216,128]{1,0:T(8,128)S(1)} %add.15.mine), channel_id=1, source_target_pairs={{0,8},{8,0},{1,9},{9,1},{2,10},{10,2},{3,11},{11,3},{4,12},{12,4},... | collective-permute-start | bytes 331784 | tf_op jit(solution)/shard_map/ppermute | solution.py:24

commit v3 on v2

--- a/solution.py
+++ b/solution.py
@@ -15,7 +15,6 @@
 CHAN = ("zl", "y")
 BF = jnp.bfloat16
 F32 = jnp.float32
-VMEM_LIMIT = 32 * 1024 * 1024
 VM = pl.BlockSpec(memory_space=pltpu.VMEM)
 KEYS = [(0, 0), (0, 1), (0, 2), (0, 3), (1, 0), (1, 1), (1, 2), (1, 3)]
 
@@ -63,12 +62,8 @@
             field[z, pl.ds(row, 16), :] = ref[start + z]
 
 
-def pack_body(k_ref, a_ref, g_ref, by1, by3, byz, own, near, far, turned, k_in, a_in, g_in, sems):
-    copies = [pltpu.make_async_copy(src, dst, sems.at[n]) for n, (src, dst) in enumerate(((k_ref, k_in), (a_ref, a_in), (g_ref, g_in)))]
-    for copy in copies:
-        copy.start()
-    copies[0].wait()
-    turned[:, 0:432] = jnp.transpose(k_in[...].astype(F32))
+def pack_body(k_ref, a_ref, g_ref, by1, by3, byz, own, near, far, turned):
+    turned[:, 0:432] = jnp.transpose(k_ref[...].astype(F32))
     turned[:, 432:512] = jnp.zeros((C, 80), F32)
 
     def piece(key):
@@ -76,17 +71,15 @@
 
     own[...] = piece((0, 0))
     first = lax.axis_index("core") == 0
-    copies[1].wait()
-    copies[2].wait()
-    near[0] = jnp.where(first, g_in[N - 1].astype(F32), g_in[0].astype(F32)).astype(BF)
-    far[0] = jnp.where(first, g_in[0].astype(F32), g_in[N - 1].astype(F32)).astype(BF)
+    near[0] = jnp.where(first, g_ref[N - 1].astype(F32), g_ref[0].astype(F32)).astype(BF)
+    far[0] = jnp.where(first, g_ref[0].astype(F32), g_ref[N - 1].astype(F32)).astype(BF)
     for dst, pairs in (
         (by1, (((0, 1), (0, 2)),)),
         (by3, (((0, 3), (1, 3)),)),
         (byz, (((1, 0), (1, 1)), ((1, 2), (1, 2)))),
     ):
-        dst[pl.ds(0, N)] = a_in[...]
-        dst[pl.ds(N + len(pairs), N)] = g_in[...]
+        dst[pl.ds(0, N)] = a_ref[...]
+        dst[pl.ds(N + len(pairs), N)] = g_ref[...]
         for n, (left, right) in enumerate(pairs):
             dst[N + n, :, 0:512] = piece(left)
             dst[N + n, :, 512:1024] = piece(right)
@@ -222,14 +215,14 @@
                 out_ref[z - 1] = out.astype(BF)
 
 
-def call(body, name, args, outs, scratch=(), flops=0, anywhere=0):
+def call(body, name, args, outs, scratch=(), flops=0, limit=32):
     return pl.pallas_call(
         body,
         out_shape=[jax.ShapeDtypeStruct(s, d) for s, d in outs],
-        in_specs=[pl.BlockSpec(memory_space=pl.ANY)] * anywhere + [VM] * (len(args) - anywhere),
+        in_specs=[VM] * len(args),
         out_specs=[VM] * len(outs),
         scratch_shapes=list(scratch),
-        compiler_params=pltpu.CompilerParams(vmem_limit_bytes=VMEM_LIMIT),
+        compiler_params=pltpu.CompilerParams(vmem_limit_bytes=limit << 20),
         cost_estimate=pl.CostEstimate(flops=flops, bytes_accessed=1 << 20, transcendentals=0),
         name=name,
     )(*args)
@@ -250,10 +243,8 @@
         [kt, activation, cotangent],
         [((N * 2 + 1, *plane), BF), ((N * 2 + 1, *plane), BF), ((N * 2 + 2, *plane), BF), ((16, 512), BF)]
         + [((1, *plane), BF)] * 2,
-        [pltpu.VMEM((C, 512), F32), pltpu.VMEM((432, C), BF)]
-        + [pltpu.VMEM((N, *plane), BF)] * 2
-        + [pltpu.SemaphoreType.DMA((3,))],
-        anywhere=3,
+        [pltpu.VMEM((C, 512), F32)],
+        limit=56,
     )
     k1 = swap(by1, "y", 1)
     k3 = swap(by3, "y", 3)

time: 60.8 us -> 59.6 us (0.980)
  local copies, waits for them, and re-layouts: 2.78 us -> 0.98 us
  Pallas kernels: 8.9 us -> 10.4 us
  waiting for transfers between devices: 17.3 us -> 16.5 us
    unnamed x8 -> x10, local copies, waits for them, and re-layouts: 2.75 us -> 0.95 us
    pallas_call x7, Pallas kernels: 8.9 us -> 10.4 us  [call(): pl.pallas_call(body, out_shape=[jax.ShapeDtypeStruct(s, d) for s, d in ou...]
    ppermute x15, waiting for transfers between devices: 17.3 us -> 16.5 us  [swap(): lax.ppermute(v, axis, [(i, i ^ bits) for i in range(lax.axis_size(axis))])]
where the time goes in v3:
time: 59.6 us; the launch traced here: 59.5 us
  starting transfers between devices  30.9 us (52%)
  waiting for transfers between devices  16.5 us (28%)
  Pallas kernels  10.4 us (17%)
  local copies, waits for them, and re-layouts  0.98 us (2%)
  between operations  0.75 us (1%)
    ppermute x15, starting transfers between devices, swap(): lax.ppermute(v, axis, [(i, i ^ bits) for i in range(lax.axis_size(axis))])  27.2 us
    ppermute x15, waiting for transfers between devices, swap(): lax.ppermute(v, axis, [(i, i ^ bits) for i in range(lax.axis_size(axis))])  16.5 us
    pallas_call x7, Pallas kernels, call(): pl.pallas_call(body, out_shape=[jax.ShapeDtypeStruct(s, d) for s, d in ou...  10.4 us
    ppermute x2, starting transfers between devices, outer_swap(): return lax.ppermute(v, SPACE, pairs)  3.64 us
  transfers between devices with their start and end apart: 17, of which 9 were waited for; matrix products, arithmetic and copies ran while one was open for 0% of the time, Pallas kernels for 12%

profile of v3, /device:TPU:1, one launch (start us, length us, event | category | flops | bytes accessed | tf_op | source)
XLA Modules:
  0.0 59.5 jit_solution(3263159736332107119)
XLA Ops:
  0.6 2.4 %pack_messages.1 = (bf16[13,16,1024]{2,1,0:T(8,128)(2,1)}, bf16[13,16,1024]{2,1,0:T(8,128)(2,1)}, bf16[14,16,1024]{2,1,0:T(8,128)(2,1)}, bf16[16,512]{1,0:T(8,12...) custom-call(bf16[432,128]{1,0:T(8,128)(2,1)} %bitcast.6, bf16[6,16,1024]{2,1,0:T(8,128)(2,1)} %refs_0_.3, ...), custom_call_target="tpu_custom_call" | custom-call | bytes 1048576 | tf_op jit(solution)/shard_map/pack_messages/pallas_call | solution.py:219
  3.0 2.1 %collective-permute-start = (bf16[13,16,1024]{2,1,0:T(8,128)(2,1)}, bf16[13,16,1024]{2,1,0:T(8,128)(2,1)S(1)}, u32[]{:S(2)}, u32[]{:S(2)}) collective-permute-start(bf16[13,16,1024]{2,1,0:T(8,128)(2,1)} %get-tuple-element.28), channel_id=1, source_target_pairs={{0,1},{1,0},{2,3},{3,2},{4,5},{5,4},{6,7},{7,6},{8,9},{9,8},{10,11... | collective-permute-start | bytes 1277960 | tf_op jit(solution)/shard_map/ppermute | solution.py:23
  5.1 1.6 %collective-permute-start.5 = (bf16[14,16,1024]{2,1,0:T(8,128)(2,1)}, bf16[14,16,1024]{2,1,0:T(8,128)(2,1)S(1)}, u32[]{:S(2)}, u32[]{:S(2)}) collective-permute-start(bf16[14,16,1024]{2,1,0:T(8,128)(2,1)} %get-tuple-element.33), channel_id=1, source_target_pairs={{0,4},{4,0},{1,5},{5,1},{2,6},{6,2},{3,7},{7,3},{8,12},{12,8},{9,1... | collective-permute-start | bytes 1376264 | tf_op jit(solution)/shard_map/ppermute | solution.py:23
  6.8 1.9 %collective-permute-start.4 = (bf16[13,16,1024]{2,1,0:T(8,128)(2,1)}, bf16[13,16,1024]{2,1,0:T(8,128)(2,1)S(1)}, u32[]{:S(2)}, u32[]{:S(2)}) collective-permute-start(bf16[13,16,1024]{2,1,0:T(8,128)(2,1)} %get-tuple-element.32), channel_id=1, source_target_pairs={{0,3},{1,2},{2,1},{3,0},{4,7},{5,6},{6,5},{7,4},{8,11},{9,10},{10,... | collective-permute-start | bytes 1277960 | tf_op jit(solution)/shard_map/ppermute | solution.py:23
  8.7 2.6 %collective-permute-start.1 = (bf16[1,16,1024]{2,1,0:T(8,128)(2,1)}, bf16[1,16,1024]{2,1,0:T(8,128)(2,1)S(1)}, u32[]{:S(2)}, u32[]{:S(2)}) collective-permute-start(bf16[1,16,1024]{2,1,0:T(8,128)(2,1)} %get-tuple-element.29), channel_id=1, source_target_pairs={{8,16},{16,8},{24,32},{32,24},{40,48},{48,40},{56,64},{64,56},{72,... | collective-permute-start | bytes 98312 | tf_op jit(solution)/shard_map/ppermute | solution.py:31
  11.3 3.3 %collective-permute-start.2 = (bf16[1,16,1024]{2,1,0:T(8,128)(2,1)}, bf16[1,16,1024]{2,1,0:T(8,128)(2,1)S(1)}, u32[]{:S(2)}, u32[]{:S(2)}) collective-permute-start(bf16[1,16,1024]{2,1,0:T(8,128)(2,1)} %get-tuple-element.30), channel_id=1, source_target_pairs={{0,8},{8,0},{1,9},{9,1},{2,10},{10,2},{3,11},{11,3},{4,12},{12,4},... | collective-permute-start | bytes 98312 | tf_op jit(solution)/shard_map/ppermute | solution.py:23
  14.6 1.1 %collective-permute-done.2.g_in = bf16[1,16,1024]{2,1,0:T(8,128)(2,1)S(1)} collective-permute-done((bf16[1,16,1024]{2,1,0:T(8,128)(2,1)}, bf16[1,16,1024]{2,1,0:T(8,128)(2,1)S(1)}, u32[]{:S(2)}, u32[]{:S(2)}) %collective-permute-start.2) | collective-permute-done | bytes 32800 | tf_op jit(solution)/shard_map/ppermute | solution.py:23
  15.6 1.8 %collective-permute-start.3 = (bf16[13,16,1024]{2,1,0:T(8,128)(2,1)S(1)}, bf16[13,16,1024]{2,1,0:T(8,128)(2,1)S(1)}, u32[]{:S(2)}, u32[]{:S(2)}) collective-permute-start(bf16[13,16,1024]{2,1,0:T(8,128)(2,1)S(1)} %collective-permute-done.refs_1_), channel_id=1, source_target_pairs={{0,3},{1,2},{2,1},{3,0},{4,7},{5,6},{6,5},{7,4},{8,11},{9,10},{10,... | collective-permute-start | bytes 1277960 | tf_op jit(solution)/shard_map/ppermute | solution.py:23
  20.1 1.1 %moved_cotangent.1.refs_8_ = bf16[1152,1024]{1,0:T(8,128)(2,1)S(1)} custom-call(bf16[6,16,1024]{2,1,0:T(8,128)(2,1)S(1)} %copy-done, bf16[1,16,1024]{2,1,0:T(8,128)(2,1)S(1)} %collective-permute-done.2.g_in, bf16[1,16,1024]{2,1,0:T(8,128)(2,1)S(1)} %collective-permute-done.1.g_out), custom_call_target="tpu_custom_call" | custom-call | bytes 1048576 | tf_op jit(solution)/shard_map/moved_cotangent/pallas_call | solution.py:219
  21.2 6.0 %collective-permute-done.3.refs_2_ = bf16[13,16,1024]{2,1,0:T(8,128)(2,1)S(1)} collective-permute-done((bf16[13,16,1024]{2,1,0:T(8,128)(2,1)S(1)}, bf16[13,16,1024]{2,1,0:T(8,128)(2,1)S(1)}, u32[]{:S(2)}, u32[]{:S(2)}) %collective-permute-start.3) | collective-permute-done | bytes 426016 | tf_op jit(solution)/shard_map/ppermute | solution.py:23
  27.7 2.6 %collective-permute-start.9 = (bf16[8,16,1024]{2,1,0:T(8,128)(2,1)S(1)}, bf16[8,16,1024]{2,1,0:T(8,128)(2,1)S(1)}, u32[]{:S(2)}, u32[]{:S(2)}) collective-permute-start(bf16[8,16,1024]{2,1,0:T(8,128)(2,1)S(1)} %slice.9), channel_id=1, source_target_pairs={{0,3},{1,2},{2,1},{3,0},{4,7},{5,6},{6,5},{7,4},{8,11},{9,10},{10,... | collective-permute-start | bytes 786440 | tf_op jit(solution)/shard_map/ppermute | solution.py:23
  30.3 1.6 %collective-permute-done.7.refs_6_ = bf16[6,16,1024]{2,1,0:T(8,128)(2,1)S(1)} collective-permute-done((bf16[6,16,1024]{2,1,0:T(8,128)(2,1)S(1)}, bf16[6,16,1024]{2,1,0:T(8,128)(2,1)S(1)}, u32[]{:S(2)}, u32[]{:S(2)}) %collective-permute-start.7) | collective-permute-done | bytes 196640 | tf_op jit(solution)/shard_map/ppermute | solution.py:23
  31.9 1.3 %grad_kernel_terms.1 = (f32[216,128]{1,0:T(8,128)S(1)}, f32[216,128]{1,0:T(8,128)S(1)}) custom-call(bf16[6,16,1024]{2,1,0:T(8,128)(2,1)S(1)} %copy-done.2, bf16[13,16,1024]{2,1,0:T(8,128)(2,1)S(1)} %collective-permute-done.refs_1_, bf16[13,16,1024]{2,1,0:T(8,128)(2,1)S(1)} %collective-permute-done.3.refs_2_, ...), custom_call_target="tpu_custom_call" | custom-call | flops 679477248 | bytes 1048576 | tf_op jit(solution)/shard_map/grad_kernel_terms/pallas_call | solution.py:219
  33.2 3.5 %collective-permute-start.10 = (f32[216,128]{1,0:T(8,128)S(1)}, f32[216,128]{1,0:T(8,128)S(1)}, u32[]{:S(2)}, u32[]{:S(2)}) collective-permute-start(f32[216,128]{1,0:T(8,128)S(1)} %get-tuple-element.38), channel_id=1, source_target_pairs={{0,8},{8,0},{1,9},{9,1},{2,10},{10,2},{3,11},{11,3},{4,12},{12,4},... | collective-permute-start | bytes 331784 | tf_op jit(solution)/shard_map/ppermute | solution.py:23
  37.6 1.3 %collective-permute-start.11 = (f32[216,128]{1,0:T(8,128)S(1)}, f32[216,128]{1,0:T(8,128)S(1)}, u32[]{:S(2)}, u32[]{:S(2)}) collective-permute-start(f32[216,128]{1,0:T(8,128)S(1)} %add.12), channel_id=1, source_target_pairs={{0,16},{16,0},{32,48},{48,32},{1,17},{17,1},{33,49},{49,33},{2,18}... | collective-permute-start | bytes 331784 | tf_op jit(solution)/shard_map/ppermute | solution.py:23
  38.9 1.2 %edge_terms.1 = (f32[2,16,1024]{2,1,0:T(8,128)S(1)}, f32[2,16,1024]{2,1,0:T(8,128)S(1)}, bf16[432,128]{1,0:T(8,128)(2,1)S(1)}) custom-call(bf16[6,16,1024]{2,1,0:T(8,128)(2,1)S(1)} %copy-done.2, bf16[13,16,1024]{2,1,0:T(8,128)(2,1)S(1)} %collective-permute-done.refs_1_, bf16[13,16,1024]{2,1,0:T(8,128)(2,1)S(1)} %collective-permute-done.3.refs_2_, ...), custom_call_target="tpu_custom_call" | custom-call | flops 75497472 | bytes 1048576 | tf_op jit(solution)/shard_map/edge_terms/pallas_call | solution.py:219
  40.2 1.0 %collective-permute-start.12 = (f32[2,16,1024]{2,1,0:T(8,128)S(1)}, f32[2,16,1024]{2,1,0:T(8,128)S(1)}, u32[]{:S(2)}, u32[]{:S(2)}) collective-permute-start(f32[2,16,1024]{2,1,0:T(8,128)S(1)} %get-tuple-element.45), channel_id=1, source_target_pairs={{8,16},{16,8},{24,32},{32,24},{40,48},{48,40},{56,64},{64,56},{72,... | collective-permute-start | bytes 393224 | tf_op jit(solution)/shard_map/ppermute | solution.py:31
  41.2 4.6 %collective-permute-start.13 = (f32[2,16,1024]{2,1,0:T(8,128)S(1)}, f32[2,16,1024]{2,1,0:T(8,128)S(1)}, u32[]{:S(2)}, u32[]{:S(2)}) collective-permute-start(f32[2,16,1024]{2,1,0:T(8,128)S(1)} %get-tuple-element.46), channel_id=1, source_target_pairs={{0,8},{8,0},{1,9},{9,1},{2,10},{10,2},{3,11},{11,3},{4,12},{12,4},... | collective-permute-start | bytes 393224 | tf_op jit(solution)/shard_map/ppermute | solution.py:23
  45.8 1.2 %collective-permute-start.14 = (bf16[216,128]{1,0:T(8,128)(2,1)S(1)}, bf16[216,128]{1,0:T(8,128)(2,1)S(1)}, u32[]{:S(2)}, u32[]{:S(2)}) collective-permute-start(bf16[216,128]{1,0:T(8,128)(2,1)S(1)} %add_convert_fusion), channel_id=1, source_target_pairs={{0,48},{16,32},{32,16},{48,0},{1,49},{17,33},{33,17},{49,1},{2,50}... | collective-permute-start | bytes 165896 | tf_op jit(solution)/shard_map/ppermute | solution.py:23
  47.0 1.5 %output_planes.1 = (bf16[4,16,1024]{2,1,0:T(8,128)(2,1)S(1)}, f32[2,16,1024]{2,1,0:T(8,128)S(1)}) custom-call(bf16[6,16,1024]{2,1,0:T(8,128)(2,1)S(1)} %copy-done.2, bf16[13,16,1024]{2,1,0:T(8,128)(2,1)S(1)} %collective-permute-done.refs_1_, bf16[13,16,1024]{2,1,0:T(8,128)(2,1)S(1)} %collective-permute-done.3.refs_2_, ...), custom_call_target="tpu_custom_call" | custom-call | flops 679477248 | bytes 1048576 | tf_op jit(solution)/shard_map/output_planes/pallas_call | solution.py:219
  48.6 2.0 %collective-permute-done.14 = bf16[216,128]{1,0:T(8,128)(2,1)S(1)} collective-permute-done((bf16[216,128]{1,0:T(8,128)(2,1)S(1)}, bf16[216,128]{1,0:T(8,128)(2,1)S(1)}, u32[]{:S(2)}, u32[]{:S(2)}) %collective-permute-start.14) | collective-permute-done | bytes 55328 | tf_op jit(solution)/shard_map/ppermute | solution.py:23
  50.7 2.2 %grad_input_planes.1 = (bf16[6,16,1024]{2,1,0:T(8,128)(2,1)}, bf16[6,16,1024]{2,1,0:T(8,128)(2,1)}) custom-call(bf16[6,16,1024]{2,1,0:T(8,128)(2,1)S(1)} %copy-done.1, bf16[13,16,1024]{2,1,0:T(8,128)(2,1)S(1)} %collective-permute-done.refs_1_, bf16[13,16,1024]{2,1,0:T(8,128)(2,1)S(1)} %collective-permute-done.3.refs_2_, ...), custom_call_target="tpu_custom_call" | custom-call | flops 679477248 | bytes 1048576 | tf_op jit(solution)/shard_map/grad_input_planes/pallas_call | solution.py:219
  52.9 2.9 %collective-permute-done.15 = f32[216,128]{1,0:T(8,128)S(1)} collective-permute-done((f32[216,128]{1,0:T(8,128)S(1)}, f32[216,128]{1,0:T(8,128)S(1)}, u32[]{:S(2)}, u32[]{:S(2)}) %collective-permute-start.15) | collective-permute-done | bytes 110624 | tf_op jit(solution)/shard_map/ppermute | solution.py:23
  55.8 2.0 %collective-permute-start.16 = (f32[216,128]{1,0:T(8,128)S(1)}, f32[216,128]{1,0:T(8,128)S(1)}, u32[]{:S(2)}, u32[]{:S(2)}) collective-permute-start(f32[216,128]{1,0:T(8,128)S(1)} %add.15.mine), channel_id=1, source_target_pairs={{0,8},{8,0},{1,9},{9,1},{2,10},{10,2},{3,11},{11,3},{4,12},{12,4},... | collective-permute-start | bytes 331784 | tf_op jit(solution)/shard_map/ppermute | solution.py:23
  (33 shorter events, 5.9 us)
Async XLA Ops:
  0.6 31.3 %copy-start.2 = (bf16[6,16,1024]{2,1,0:T(8,128)(2,1)S(1)}, bf16[6,16,1024]{2,1,0:T(8,128)(2,1)}, u32[]{:S(2)}) copy-start(bf16[6,16,1024]{2,1,0:T(8,128)(2,1)} %refs_0_.3) | copy-start | bytes 589828
  3.0 12.6 %collective-permute-start = (bf16[13,16,1024]{2,1,0:T(8,128)(2,1)}, bf16[13,16,1024]{2,1,0:T(8,128)(2,1)S(1)}, u32[]{:S(2)}, u32[]{:S(2)}) collective-permute-start(bf16[13,16,1024]{2,1,0:T(8,128)(2,1)} %get-tuple-element.28), channel_id=1, source_target_pairs={{0,1},{1,0},{2,3},{3,2},{4,5},{5,4},{6,7},{7,6},{8,9},{9,8},{10,11... | collective-permute-start | bytes 1277960 | tf_op jit(solution)/shard_map/ppermute | solution.py:23
  5.1 12.3 %collective-permute-start.5 = (bf16[14,16,1024]{2,1,0:T(8,128)(2,1)}, bf16[14,16,1024]{2,1,0:T(8,128)(2,1)S(1)}, u32[]{:S(2)}, u32[]{:S(2)}) collective-permute-start(bf16[14,16,1024]{2,1,0:T(8,128)(2,1)} %get-tuple-element.33), channel_id=1, source_target_pairs={{0,4},{4,0},{1,5},{5,1},{2,6},{6,2},{3,7},{7,3},{8,12},{12,8},{9,1... | collective-permute-start | bytes 1376264 | tf_op jit(solution)/shard_map/ppermute | solution.py:23
  6.8 11.5 %collective-permute-start.4 = (bf16[13,16,1024]{2,1,0:T(8,128)(2,1)}, bf16[13,16,1024]{2,1,0:T(8,128)(2,1)S(1)}, u32[]{:S(2)}, u32[]{:S(2)}) collective-permute-start(bf16[13,16,1024]{2,1,0:T(8,128)(2,1)} %get-tuple-element.32), channel_id=1, source_target_pairs={{0,3},{1,2},{2,1},{3,0},{4,7},{5,6},{6,5},{7,4},{8,11},{9,10},{10,... | collective-permute-start | bytes 1277960 | tf_op jit(solution)/shard_map/ppermute | solution.py:23
  8.7 5.9 %collective-permute-start.1 = (bf16[1,16,1024]{2,1,0:T(8,128)(2,1)}, bf16[1,16,1024]{2,1,0:T(8,128)(2,1)S(1)}, u32[]{:S(2)}, u32[]{:S(2)}) collective-permute-start(bf16[1,16,1024]{2,1,0:T(8,128)(2,1)} %get-tuple-element.29), channel_id=1, source_target_pairs={{8,16},{16,8},{24,32},{32,24},{40,48},{48,40},{56,64},{64,56},{72,... | collective-permute-start | bytes 98312 | tf_op jit(solution)/shard_map/ppermute | solution.py:31
  11.3 4.4 %collective-permute-start.2 = (bf16[1,16,1024]{2,1,0:T(8,128)(2,1)}, bf16[1,16,1024]{2,1,0:T(8,128)(2,1)S(1)}, u32[]{:S(2)}, u32[]{:S(2)}) collective-permute-start(bf16[1,16,1024]{2,1,0:T(8,128)(2,1)} %get-tuple-element.30), channel_id=1, source_target_pairs={{0,8},{8,0},{1,9},{9,1},{2,10},{10,2},{3,11},{11,3},{4,12},{12,4},... | collective-permute-start | bytes 98312 | tf_op jit(solution)/shard_map/ppermute | solution.py:23
  15.6 11.6 %collective-permute-start.3 = (bf16[13,16,1024]{2,1,0:T(8,128)(2,1)S(1)}, bf16[13,16,1024]{2,1,0:T(8,128)(2,1)S(1)}, u32[]{:S(2)}, u32[]{:S(2)}) collective-permute-start(bf16[13,16,1024]{2,1,0:T(8,128)(2,1)S(1)} %collective-permute-done.refs_1_), channel_id=1, source_target_pairs={{0,3},{1,2},{2,1},{3,0},{4,7},{5,6},{6,5},{7,4},{8,11},{9,10},{10,... | collective-permute-start | bytes 1277960 | tf_op jit(solution)/shard_map/ppermute | solution.py:23
  17.5 10.2 %collective-permute-start.6 = (bf16[14,16,1024]{2,1,0:T(8,128)(2,1)S(1)}, bf16[14,16,1024]{2,1,0:T(8,128)(2,1)S(1)}, u32[]{:S(2)}, u32[]{:S(2)}) collective-permute-start(bf16[14,16,1024]{2,1,0:T(8,128)(2,1)S(1)} %collective-permute-done.5.refs_4_), channel_id=1, source_target_pairs={{0,1},{1,0},{2,3},{3,2},{4,5},{5,4},{6,7},{7,6},{8,9},{9,8},{10,11... | collective-permute-start | bytes 1376264 | tf_op jit(solution)/shard_map/ppermute | solution.py:23
  18.2 12.1 %collective-permute-start.8 = (bf16[13,16,1024]{2,1,0:T(8,128)(2,1)S(1)}, bf16[13,16,1024]{2,1,0:T(8,128)(2,1)S(1)}, u32[]{:S(2)}, u32[]{:S(2)}) collective-permute-start(bf16[13,16,1024]{2,1,0:T(8,128)(2,1)S(1)} %collective-permute-done.4.refs_3_), channel_id=1, source_target_pairs={{0,4},{4,0},{1,5},{5,1},{2,6},{6,2},{3,7},{7,3},{8,12},{12,8},{9,1... | collective-permute-start | bytes 1277960 | tf_op jit(solution)/shard_map/ppermute | solution.py:23
  19.2 0.9 %copy-start = (bf16[6,16,1024]{2,1,0:T(8,128)(2,1)S(1)}, bf16[6,16,1024]{2,1,0:T(8,128)(2,1)}, u32[]{:S(2)}) copy-start(bf16[6,16,1024]{2,1,0:T(8,128)(2,1)} %refs_0_.4) | copy-start | bytes 589828
  27.3 4.6 %collective-permute-start.7 = (bf16[6,16,1024]{2,1,0:T(8,128)(2,1)S(1)}, bf16[6,16,1024]{2,1,0:T(8,128)(2,1)S(1)}, u32[]{:S(2)}, u32[]{:S(2)}) collective-permute-start(bf16[6,16,1024]{2,1,0:T(8,128)(2,1)S(1)} %slice.8), channel_id=1, source_target_pairs={{0,4},{4,0},{1,5},{5,1},{2,6},{6,2},{3,7},{7,3},{8,12},{12,8},{9,1... | collective-permute-start | bytes 589832 | tf_op jit(solution)/shard_map/ppermute | solution.py:23
  27.7 11.2 %copy-start.1 = (bf16[6,16,1024]{2,1,0:T(8,128)(2,1)S(1)}, bf16[6,16,1024]{2,1,0:T(8,128)(2,1)}, u32[]{:S(2)}) copy-start(bf16[6,16,1024]{2,1,0:T(8,128)(2,1)} %refs_0_.4) | copy-start | bytes 589828
  27.7 11.2 %copy-start.3 = (bf16[3,3,3,128,16]{3,4,2,1,0:T(8,128)(2,1)S(1)}, bf16[3,3,3,128,16]{3,4,2,1,0:T(8,128)(2,1)}, u32[]{:S(2)}) copy-start(bf16[3,3,3,128,16]{3,4,2,1,0:T(8,128)(2,1)} %param.5) | copy-start | bytes 331780
  27.7 11.2 %copy-start.4 = (bf16[16,512]{1,0:T(8,128)(2,1)S(1)}, bf16[16,512]{1,0:T(8,128)(2,1)}, u32[]{:S(2)}) copy-start(bf16[16,512]{1,0:T(8,128)(2,1)} %get-tuple-element.40.refs_11_) | copy-start | bytes 49156
  27.7 8.9 %collective-permute-start.9 = (bf16[8,16,1024]{2,1,0:T(8,128)(2,1)S(1)}, bf16[8,16,1024]{2,1,0:T(8,128)(2,1)S(1)}, u32[]{:S(2)}, u32[]{:S(2)}) collective-permute-start(bf16[8,16,1024]{2,1,0:T(8,128)(2,1)S(1)} %slice.9), channel_id=1, source_target_pairs={{0,3},{1,2},{2,1},{3,0},{4,7},{5,6},{6,5},{7,4},{8,11},{9,10},{10,... | collective-permute-start | bytes 786440 | tf_op jit(solution)/shard_map/ppermute | solution.py:23
  33.2 4.4 %collective-permute-start.10 = (f32[216,128]{1,0:T(8,128)S(1)}, f32[216,128]{1,0:T(8,128)S(1)}, u32[]{:S(2)}, u32[]{:S(2)}) collective-permute-start(f32[216,128]{1,0:T(8,128)S(1)} %get-tuple-element.38), channel_id=1, source_target_pairs={{0,8},{8,0},{1,9},{9,1},{2,10},{10,2},{3,11},{11,3},{4,12},{12,4},... | collective-permute-start | bytes 331784 | tf_op jit(solution)/shard_map/ppermute | solution.py:23
  37.6 8.2 %collective-permute-start.11 = (f32[216,128]{1,0:T(8,128)S(1)}, f32[216,128]{1,0:T(8,128)S(1)}, u32[]{:S(2)}, u32[]{:S(2)}) collective-permute-start(f32[216,128]{1,0:T(8,128)S(1)} %add.12), channel_id=1, source_target_pairs={{0,16},{16,0},{32,48},{48,32},{1,17},{17,1},{33,49},{49,33},{2,18}... | collective-permute-start | bytes 331784 | tf_op jit(solution)/shard_map/ppermute | solution.py:23
  40.2 8.4 %collective-permute-start.12 = (f32[2,16,1024]{2,1,0:T(8,128)S(1)}, f32[2,16,1024]{2,1,0:T(8,128)S(1)}, u32[]{:S(2)}, u32[]{:S(2)}) collective-permute-start(f32[2,16,1024]{2,1,0:T(8,128)S(1)} %get-tuple-element.45), channel_id=1, source_target_pairs={{8,16},{16,8},{24,32},{32,24},{40,48},{48,40},{56,64},{64,56},{72,... | collective-permute-start | bytes 393224 | tf_op jit(solution)/shard_map/ppermute | solution.py:31
  41.2 7.4 %collective-permute-start.13 = (f32[2,16,1024]{2,1,0:T(8,128)S(1)}, f32[2,16,1024]{2,1,0:T(8,128)S(1)}, u32[]{:S(2)}, u32[]{:S(2)}) collective-permute-start(f32[2,16,1024]{2,1,0:T(8,128)S(1)} %get-tuple-element.46), channel_id=1, source_target_pairs={{0,8},{8,0},{1,9},{9,1},{2,10},{10,2},{3,11},{11,3},{4,12},{12,4},... | collective-permute-start | bytes 393224 | tf_op jit(solution)/shard_map/ppermute | solution.py:23
  45.8 4.8 %collective-permute-start.14 = (bf16[216,128]{1,0:T(8,128)(2,1)S(1)}, bf16[216,128]{1,0:T(8,128)(2,1)S(1)}, u32[]{:S(2)}, u32[]{:S(2)}) collective-permute-start(bf16[216,128]{1,0:T(8,128)(2,1)S(1)} %add_convert_fusion), channel_id=1, source_target_pairs={{0,48},{16,32},{32,16},{48,0},{1,49},{17,33},{33,17},{49,1},{2,50}... | collective-permute-start | bytes 165896 | tf_op jit(solution)/shard_map/ppermute | solution.py:23
  50.6 5.2 %collective-permute-start.15 = (f32[216,128]{1,0:T(8,128)S(1)}, f32[216,128]{1,0:T(8,128)S(1)}, u32[]{:S(2)}, u32[]{:S(2)}) collective-permute-start(f32[216,128]{1,0:T(8,128)S(1)} %convert_add_fusion), channel_id=1, source_target_pairs={{0,64},{64,0},{1,65},{65,1},{2,66},{66,2},{3,67},{67,3},{4,68},{68... | collective-permute-start | bytes 331784 | tf_op jit(solution)/shard_map/ppermute | solution.py:23
  55.8 3.0 %collective-permute-start.16 = (f32[216,128]{1,0:T(8,128)S(1)}, f32[216,128]{1,0:T(8,128)S(1)}, u32[]{:S(2)}, u32[]{:S(2)}) collective-permute-start(f32[216,128]{1,0:T(8,128)S(1)} %add.15.mine), channel_id=1, source_target_pairs={{0,8},{8,0},{1,9},{9,1},{2,10},{10,2},{3,11},{11,3},{4,12},{12,4},... | collective-permute-start | bytes 331784 | tf_op jit(solution)/shard_map/ppermute | solution.py:23

commit v4 on v3

--- a/solution.py
+++ b/solution.py
@@ -91,7 +91,7 @@
     pieces = [own[...].astype(F32)]
     for key, unit in zip(KEYS[1:], units[1:]):
         at = 512 if key in right else 0
-        pieces.append(unit[1 if key == (1, 2) else N, :, pl.ds(at, 512)].astype(F32))
+        pieces.append(unit[0 if key == (1, 2) else N, :, pl.ds(at, 512)].astype(F32))
     for tap in range(27):
         tile, spot = divmod(tap * 16, C)
         row = None
@@ -149,7 +149,7 @@
     return s[16:32] + from_y_before(s[0:16], y) + from_y_after(s[32:48], y)
 
 
-G_STARTS = {(0, 0): 0, (1, 2): 2, (1, 0): N + 2, (1, 1): N + 2}
+G_STARTS = {(0, 0): 0, (0, 2): 0, (1, 3): 0, (1, 2): 1, (1, 0): N + 2, (1, 1): N + 2}
 
 
 def g_blocks(units):
@@ -157,11 +157,10 @@
 
 
 def edges_body(*refs):
-    units, (g, z2g, w, own), (inner, outer, w_in), (field,) = refs[:8], refs[8:12], refs[12:15], refs[15:]
+    units, g_units, (w, own, inner, outer, w_in, field) = refs[:8], refs[8:16], refs[16:]
     y = lane_y()
     first = lax.axis_index("core") == 0
-    g_units = [g, *units[1:6], z2g, units[7]]
-    unpack_filter(own, g_units, w_in)
+    unpack_filter(own, [*units[:6], g_units[6], units[7]], w_in)
     for n, (blocks, weights) in enumerate((([(u, 0) for u in units], w), (g_blocks(g_units), w_in))):
         for i, (key, (ref, start)) in enumerate(zip(KEYS, blocks)):
             row = first_row(key) if n == 0 else i * 16
@@ -251,33 +250,37 @@
     z0 = swap(byz, "zl", 1)
     g_in = swap(g_in, "core", 1)
     g_out = outer_swap(g_out)
-    k2 = swap(after(k1, g_out, g_in), "y", 3)
-    z1 = swap(z0, "y", 1)
-    z3 = swap(k3, "zl", 1)
+    k2a = swap(after(k1[: N + 1], g_out), "y", 3)
+    z1 = swap(after(z0, g_out, g_in), "y", 1)
+    z3a = swap(k3[: N + 1], "zl", 1)
     (moved,) = call(
         shifts_body,
         "moved_cotangent",
-        [after(cotangent, k1), g_in, g_out],
+        [after(cotangent, k1, k3), g_in, g_out],
         [(((N + 2) * 144, CELLS), BF)],
     )
-    z2a = swap(after(k2[:N], moved), "zl", 1)
-    z2g = swap(z1[N:], "y", 3)
-
-    units = [k1, k2, k3, z0, z1, z2a, z3]
+    z2a = swap(after(k2a[:N], moved), "zl", 1)
+    g3 = after(k3[N + 1 :], k2a)
+    z3g = swap(g3, "zl", 1)
+    k2g = swap(g3, "y", 1)
+    z2g = swap(z1[N + 1 :], "y", 3)
+
+    units = [activation, k1, k2a, k3, z0, z1, z2a, z3a]
+    g_units = [cotangent, k1, k2g, k3, z0, z1, z2g, z3g]
     keep, send = call(
         gk_body,
         "grad_kernel_terms",
-        [activation, *units, moved],
+        [*units, moved],
         [((216, C), F32)] * 2,
         [pltpu.VMEM((432, C), F32), FIELD],
         CONV_FLOPS,
     )
-    terms = after(keep, z2g) + swap(send, "core", 1)
+    terms = after(keep, z2g, k2g, z3g) + swap(send, "core", 1)
     got = swap(terms, "x", 1)
     inner, outer, w_in = call(
         edges_body,
         "edge_terms",
-        [after(activation, keep), *units, cotangent, z2g, kt, own],
+        [*units, *g_units, after(kt, keep), own],
         [((2, *plane), F32)] * 2 + [((432, C), BF)],
         [pltpu.VMEM((4, C, CELLS), BF)],
         CONV_FLOPS // 9,
@@ -289,7 +292,7 @@
     middle, ends = call(
         functools.partial(conv_body, 0),
         "output_planes",
-        [after(activation, terms), *units, kt],
+        [*units, after(kt, terms)],
         [((N - 2, *plane), BF), ((2, *plane), F32)],
         [FIELD, pltpu.VMEM((288, CELLS), F32)],
         CONV_FLOPS,
@@ -299,7 +302,7 @@
     grad_input, output = call(
         functools.partial(conv_body, 1),
         "grad_input_planes",
-        [after(cotangent, terms), *units[:5], z2g, z3, w_in, inner, outer, middle, ends],
+        [*g_units, after(w_in, terms), inner, outer, middle, ends],
         [((N, *plane), BF)] * 2,
         [FIELD, pltpu.VMEM((288, CELLS), F32)],
         CONV_FLOPS,

time: 59.6 us -> 58.7 us (0.985)
  waiting for transfers between devices: 16.5 us -> 12.2 us
  starting transfers between devices: 30.9 us -> 34.2 us
    ppermute x15 -> x17, waiting for transfers between devices: 16.5 us -> 12.2 us  [swap(): lax.ppermute(v, axis, [(i, i ^ bits) for i in range(lax.axis_size(axis))])]
    ppermute x15 -> x17, starting transfers between devices: 27.2 us -> 28.9 us  [swap(): lax.ppermute(v, axis, [(i, i ^ bits) for i in range(lax.axis_size(axis))])]
    ppermute x2, starting transfers between devices: 3.64 us -> 5.28 us  [outer_swap(): return lax.ppermute(v, SPACE, pairs)]
  transfers between devices with their start and end apart: 17 -> 19, of which waited for: 9 -> 8; matrix products, arithmetic and copies ran while one was open for 0% -> 0% of each run, Pallas kernels for 12% -> 12%
where the time goes in v4:
time: 58.7 us; the launch traced here: 58.6 us
  starting transfers between devices  34.2 us (58%)
  waiting for transfers between devices  12.2 us (21%)
  Pallas kernels  10.3 us (18%)
  local copies, waits for them, and re-layouts  1.02 us (2%)
  between operations  0.77 us (1%)
    ppermute x17, starting transfers between devices, swap(): lax.ppermute(v, axis, [(i, i ^ bits) for i in range(lax.axis_size(axis))])  28.9 us
    ppermute x17, waiting for transfers between devices, swap(): lax.ppermute(v, axis, [(i, i ^ bits) for i in range(lax.axis_size(axis))])  12.2 us
    pallas_call x7, Pallas kernels, call(): pl.pallas_call(body, out_shape=[jax.ShapeDtypeStruct(s, d) for s, d in ou...  10.3 us
    ppermute x2, starting transfers between devices, outer_swap(): return lax.ppermute(v, SPACE, pairs)  5.28 us
  transfers between devices with their start and end apart: 19, of which 8 were waited for; matrix products, arithmetic and copies ran while one was open for 0% of the time, Pallas kernels for 12%

profile of v4, /device:TPU:1, one launch (start us, length us, event | category | flops | bytes accessed | tf_op | source)
XLA Modules:
  0.0 58.6 jit_solution(12139878133200992417)
XLA Ops:
  0.6 2.3 %pack_messages.1 = (bf16[13,16,1024]{2,1,0:T(8,128)(2,1)}, bf16[13,16,1024]{2,1,0:T(8,128)(2,1)}, bf16[14,16,1024]{2,1,0:T(8,128)(2,1)}, bf16[16,512]{1,0:T(8,12...) custom-call(bf16[432,128]{1,0:T(8,128)(2,1)} %bitcast.6, bf16[6,16,1024]{2,1,0:T(8,128)(2,1)} %refs_0_.6, ...), custom_call_target="tpu_custom_call" | custom-call | bytes 1048576 | tf_op jit(solution)/shard_map/pack_messages/pallas_call | solution.py:218
  2.9 2.5 %collective-permute-start.5 = (bf16[14,16,1024]{2,1,0:T(8,128)(2,1)}, bf16[14,16,1024]{2,1,0:T(8,128)(2,1)S(1)}, u32[]{:S(2)}, u32[]{:S(2)}) collective-permute-start(bf16[14,16,1024]{2,1,0:T(8,128)(2,1)} %get-tuple-element.35), channel_id=1, source_target_pairs={{0,4},{4,0},{1,5},{5,1},{2,6},{6,2},{3,7},{7,3},{8,12},{12,8},{9,1... | collective-permute-start | bytes 1376264 | tf_op jit(solution)/shard_map/ppermute | solution.py:23
  5.4 1.3 %collective-permute-start = (bf16[13,16,1024]{2,1,0:T(8,128)(2,1)}, bf16[13,16,1024]{2,1,0:T(8,128)(2,1)S(1)}, u32[]{:S(2)}, u32[]{:S(2)}) collective-permute-start(bf16[13,16,1024]{2,1,0:T(8,128)(2,1)} %get-tuple-element.30), channel_id=1, source_target_pairs={{0,1},{1,0},{2,3},{3,2},{4,5},{5,4},{6,7},{7,6},{8,9},{9,8},{10,11... | collective-permute-start | bytes 1277960 | tf_op jit(solution)/shard_map/ppermute | solution.py:23
  6.7 1.9 %collective-permute-start.1 = (bf16[13,16,1024]{2,1,0:T(8,128)(2,1)}, bf16[13,16,1024]{2,1,0:T(8,128)(2,1)S(1)}, u32[]{:S(2)}, u32[]{:S(2)}) collective-permute-start(bf16[13,16,1024]{2,1,0:T(8,128)(2,1)} %get-tuple-element.31), channel_id=1, source_target_pairs={{0,3},{1,2},{2,1},{3,0},{4,7},{5,6},{6,5},{7,4},{8,11},{9,10},{10,... | collective-permute-start | bytes 1277960 | tf_op jit(solution)/shard_map/ppermute | solution.py:23
  8.6 2.6 %collective-permute-start.2 = (bf16[1,16,1024]{2,1,0:T(8,128)(2,1)}, bf16[1,16,1024]{2,1,0:T(8,128)(2,1)S(1)}, u32[]{:S(2)}, u32[]{:S(2)}) collective-permute-start(bf16[1,16,1024]{2,1,0:T(8,128)(2,1)} %get-tuple-element.32), channel_id=1, source_target_pairs={{8,16},{16,8},{24,32},{32,24},{40,48},{48,40},{56,64},{64,56},{72,... | collective-permute-start | bytes 98312 | tf_op jit(solution)/shard_map/ppermute | solution.py:31
  11.2 3.3 %collective-permute-start.6 = (bf16[1,16,1024]{2,1,0:T(8,128)(2,1)}, bf16[1,16,1024]{2,1,0:T(8,128)(2,1)S(1)}, u32[]{:S(2)}, u32[]{:S(2)}) collective-permute-start(bf16[1,16,1024]{2,1,0:T(8,128)(2,1)} %get-tuple-element.36), channel_id=1, source_target_pairs={{0,8},{8,0},{1,9},{9,1},{2,10},{10,2},{3,11},{11,3},{4,12},{12,4},... | collective-permute-start | bytes 98312 | tf_op jit(solution)/shard_map/ppermute | solution.py:23
  15.8 1.5 %collective-permute-start.7 = (bf16[14,16,1024]{2,1,0:T(8,128)(2,1)S(1)}, bf16[14,16,1024]{2,1,0:T(8,128)(2,1)S(1)}, u32[]{:S(2)}, u32[]{:S(2)}) collective-permute-start(bf16[14,16,1024]{2,1,0:T(8,128)(2,1)S(1)} %collective-permute-done.5.refs_4_.refs_12_), channel_id=1, source_target_pairs={{0,1},{1,0},{2,3},{3,2},{4,5},{5,4},{6,7},{7,6},{8,9},{9,8},{10,11... | collective-permute-start | bytes 1376264 | tf_op jit(solution)/shard_map/ppermute | solution.py:23
  17.4 2.0 %collective-permute-start.3 = (bf16[7,16,1024]{2,1,0:T(8,128)(2,1)S(1)}, bf16[7,16,1024]{2,1,0:T(8,128)(2,1)S(1)}, u32[]{:S(2)}, u32[]{:S(2)}) collective-permute-start(bf16[7,16,1024]{2,1,0:T(8,128)(2,1)S(1)} %slice.21), channel_id=1, source_target_pairs={{0,3},{1,2},{2,1},{3,0},{4,7},{5,6},{6,5},{7,4},{8,11},{9,10},{10,... | collective-permute-start | bytes 688136 | tf_op jit(solution)/shard_map/ppermute | solution.py:23
  19.4 1.4 %collective-permute-start.11 = (bf16[7,16,1024]{2,1,0:T(8,128)(2,1)S(1)}, bf16[7,16,1024]{2,1,0:T(8,128)(2,1)S(1)}, u32[]{:S(2)}, u32[]{:S(2)}) collective-permute-start(bf16[7,16,1024]{2,1,0:T(8,128)(2,1)S(1)} %slice.24), channel_id=1, source_target_pairs={{0,4},{4,0},{1,5},{5,1},{2,6},{6,2},{3,7},{7,3},{8,12},{12,8},{9,1... | collective-permute-start | bytes 688136 | tf_op jit(solution)/shard_map/ppermute | solution.py:23
  21.7 1.1 %moved_cotangent.1.refs_8_ = bf16[1152,1024]{1,0:T(8,128)(2,1)S(1)} custom-call(bf16[6,16,1024]{2,1,0:T(8,128)(2,1)S(1)} %copy-done.1, bf16[1,16,1024]{2,1,0:T(8,128)(2,1)S(1)} %collective-permute-done.6.g_in, bf16[1,16,1024]{2,1,0:T(8,128)(2,1)S(1)} %collective-permute-done.2.g_out), custom_call_target="tpu_custom_call" | custom-call | bytes 1048576 | tf_op jit(solution)/shard_map/moved_cotangent/pallas_call | solution.py:218
  22.8 1.3 %collective-permute-done.3.refs_2_ = bf16[7,16,1024]{2,1,0:T(8,128)(2,1)S(1)} collective-permute-done((bf16[7,16,1024]{2,1,0:T(8,128)(2,1)S(1)}, bf16[7,16,1024]{2,1,0:T(8,128)(2,1)S(1)}, u32[]{:S(2)}, u32[]{:S(2)}) %collective-permute-start.3) | collective-permute-done | bytes 229408 | tf_op jit(solution)/shard_map/ppermute | solution.py:23
  24.6 1.8 %collective-permute-done.7.refs_5_.refs_13_ = bf16[14,16,1024]{2,1,0:T(8,128)(2,1)S(1)} collective-permute-done((bf16[14,16,1024]{2,1,0:T(8,128)(2,1)S(1)}, bf16[14,16,1024]{2,1,0:T(8,128)(2,1)S(1)}, u32[]{:S(2)}, u32[]{:S(2)}) %collective-permute-start.7) | collective-permute-done | bytes 458784 | tf_op jit(solution)/shard_map/ppermute | solution.py:23
  26.4 3.2 %collective-permute-start.8 = (bf16[7,16,1024]{2,1,0:T(8,128)(2,1)S(1)}, bf16[7,16,1024]{2,1,0:T(8,128)(2,1)S(1)}, u32[]{:S(2)}, u32[]{:S(2)}) collective-permute-start(bf16[7,16,1024]{2,1,0:T(8,128)(2,1)S(1)} %slice.22), channel_id=1, source_target_pairs={{0,3},{1,2},{2,1},{3,0},{4,7},{5,6},{6,5},{7,4},{8,11},{9,10},{10,... | collective-permute-start | bytes 688136 | tf_op jit(solution)/shard_map/ppermute | solution.py:23
  29.7 1.1 %collective-permute-start.9 = (bf16[6,16,1024]{2,1,0:T(8,128)(2,1)S(1)}, bf16[6,16,1024]{2,1,0:T(8,128)(2,1)S(1)}, u32[]{:S(2)}, u32[]{:S(2)}) collective-permute-start(bf16[6,16,1024]{2,1,0:T(8,128)(2,1)S(1)} %slice.20), channel_id=1, source_target_pairs={{0,4},{4,0},{1,5},{5,1},{2,6},{6,2},{3,7},{7,3},{8,12},{12,8},{9,1... | collective-permute-start | bytes 589832 | tf_op jit(solution)/shard_map/ppermute | solution.py:23
  30.9 1.3 %grad_kernel_terms.1 = (f32[216,128]{1,0:T(8,128)S(1)}, f32[216,128]{1,0:T(8,128)S(1)}) custom-call(bf16[6,16,1024]{2,1,0:T(8,128)(2,1)S(1)} %copy-done, bf16[13,16,1024]{2,1,0:T(8,128)(2,1)S(1)} %collective-permute-done.refs_1_.refs_9_, bf16[7,16,1024]{2,1,0:T(8,128)(2,1)S(1)} %collective-permute-done.3.refs_2_, ...), custom_call_target="tpu_custom_call" | custom-call | flops 679477248 | bytes 1048576 | tf_op jit(solution)/shard_map/grad_kernel_terms/pallas_call | solution.py:218
  32.2 3.1 %collective-permute-start.12 = (f32[216,128]{1,0:T(8,128)S(1)}, f32[216,128]{1,0:T(8,128)S(1)}, u32[]{:S(2)}, u32[]{:S(2)}) collective-permute-start(f32[216,128]{1,0:T(8,128)S(1)} %get-tuple-element.45), channel_id=1, source_target_pairs={{0,8},{8,0},{1,9},{9,1},{2,10},{10,2},{3,11},{11,3},{4,12},{12,4},... | collective-permute-start | bytes 331784 | tf_op jit(solution)/shard_map/ppermute | solution.py:23
  37.2 1.3 %edge_terms.1 = (f32[2,16,1024]{2,1,0:T(8,128)S(1)}, f32[2,16,1024]{2,1,0:T(8,128)S(1)}, bf16[432,128]{1,0:T(8,128)(2,1)S(1)}) custom-call(bf16[6,16,1024]{2,1,0:T(8,128)(2,1)S(1)} %copy-done, bf16[13,16,1024]{2,1,0:T(8,128)(2,1)S(1)} %collective-permute-done.refs_1_.refs_9_, bf16[7,16,1024]{2,1,0:T(8,128)(2,1)S(1)} %collective-permute-done.3.refs_2_, ...), custom_call_target="tpu_custom_call" | custom-call | flops 75497472 | bytes 1048576 | tf_op jit(solution)/shard_map/edge_terms/pallas_call | solution.py:218
  38.5 2.7 %collective-permute-start.14 = (f32[2,16,1024]{2,1,0:T(8,128)S(1)}, f32[2,16,1024]{2,1,0:T(8,128)S(1)}, u32[]{:S(2)}, u32[]{:S(2)}) collective-permute-start(f32[2,16,1024]{2,1,0:T(8,128)S(1)} %get-tuple-element.49), channel_id=1, source_target_pairs={{8,16},{16,8},{24,32},{32,24},{40,48},{48,40},{56,64},{64,56},{72,... | collective-permute-start | bytes 393224 | tf_op jit(solution)/shard_map/ppermute | solution.py:31
  41.2 2.6 %collective-permute-start.15 = (f32[2,16,1024]{2,1,0:T(8,128)S(1)}, f32[2,16,1024]{2,1,0:T(8,128)S(1)}, u32[]{:S(2)}, u32[]{:S(2)}) collective-permute-start(f32[2,16,1024]{2,1,0:T(8,128)S(1)} %get-tuple-element.50), channel_id=1, source_target_pairs={{0,8},{8,0},{1,9},{9,1},{2,10},{10,2},{3,11},{11,3},{4,12},{12,4},... | collective-permute-start | bytes 393224 | tf_op jit(solution)/shard_map/ppermute | solution.py:23
  43.8 2.5 %collective-permute-start.16 = (bf16[216,128]{1,0:T(8,128)(2,1)S(1)}, bf16[216,128]{1,0:T(8,128)(2,1)S(1)}, u32[]{:S(2)}, u32[]{:S(2)}) collective-permute-start(bf16[216,128]{1,0:T(8,128)(2,1)S(1)} %add_convert_fusion), channel_id=1, source_target_pairs={{0,48},{16,32},{32,16},{48,0},{1,49},{17,33},{33,17},{49,1},{2,50}... | collective-permute-start | bytes 165896 | tf_op jit(solution)/shard_map/ppermute | solution.py:23
  46.3 1.5 %output_planes.1 = (bf16[4,16,1024]{2,1,0:T(8,128)(2,1)S(1)}, f32[2,16,1024]{2,1,0:T(8,128)S(1)}) custom-call(bf16[6,16,1024]{2,1,0:T(8,128)(2,1)S(1)} %copy-done, bf16[13,16,1024]{2,1,0:T(8,128)(2,1)S(1)} %collective-permute-done.refs_1_.refs_9_, bf16[7,16,1024]{2,1,0:T(8,128)(2,1)S(1)} %collective-permute-done.3.refs_2_, ...), custom_call_target="tpu_custom_call" | custom-call | flops 679477248 | bytes 1048576 | tf_op jit(solution)/shard_map/output_planes/pallas_call | solution.py:218
  47.8 1.9 %collective-permute-done.16 = bf16[216,128]{1,0:T(8,128)(2,1)S(1)} collective-permute-done((bf16[216,128]{1,0:T(8,128)(2,1)S(1)}, bf16[216,128]{1,0:T(8,128)(2,1)S(1)}, u32[]{:S(2)}, u32[]{:S(2)}) %collective-permute-start.16) | collective-permute-done | bytes 55328 | tf_op jit(solution)/shard_map/ppermute | solution.py:23
  49.8 2.2 %grad_input_planes.1 = (bf16[6,16,1024]{2,1,0:T(8,128)(2,1)}, bf16[6,16,1024]{2,1,0:T(8,128)(2,1)}) custom-call(bf16[6,16,1024]{2,1,0:T(8,128)(2,1)S(1)} %copy-done.2, bf16[13,16,1024]{2,1,0:T(8,128)(2,1)S(1)} %collective-permute-done.refs_1_.refs_9_, bf16[6,16,1024]{2,1,0:T(8,128)(2,1)S(1)} %collective-permute-done.4.refs_10_.refs_2_, ...), custom_call_target="tpu_custom_call" | custom-call | flops 679477248 | bytes 1048576 | tf_op jit(solution)/shard_map/grad_input_planes/pallas_call | solution.py:218
  52.0 3.8 %collective-permute-done.17 = f32[216,128]{1,0:T(8,128)S(1)} collective-permute-done((f32[216,128]{1,0:T(8,128)S(1)}, f32[216,128]{1,0:T(8,128)S(1)}, u32[]{:S(2)}, u32[]{:S(2)}) %collective-permute-start.17) | collective-permute-done | bytes 110624 | tf_op jit(solution)/shard_map/ppermute | solution.py:23
  (40 shorter events, 7.6 us)
Async XLA Ops:
  2.9 12.9 %collective-permute-start.5 = (bf16[14,16,1024]{2,1,0:T(8,128)(2,1)}, bf16[14,16,1024]{2,1,0:T(8,128)(2,1)S(1)}, u32[]{:S(2)}, u32[]{:S(2)}) collective-permute-start(bf16[14,16,1024]{2,1,0:T(8,128)(2,1)} %get-tuple-element.35), channel_id=1, source_target_pairs={{0,4},{4,0},{1,5},{5,1},{2,6},{6,2},{3,7},{7,3},{8,12},{12,8},{9,1... | collective-permute-start | bytes 1376264 | tf_op jit(solution)/shard_map/ppermute | solution.py:23
  5.4 12.0 %collective-permute-start = (bf16[13,16,1024]{2,1,0:T(8,128)(2,1)}, bf16[13,16,1024]{2,1,0:T(8,128)(2,1)S(1)}, u32[]{:S(2)}, u32[]{:S(2)}) collective-permute-start(bf16[13,16,1024]{2,1,0:T(8,128)(2,1)} %get-tuple-element.30), channel_id=1, source_target_pairs={{0,1},{1,0},{2,3},{3,2},{4,5},{5,4},{6,7},{7,6},{8,9},{9,8},{10,11... | collective-permute-start | bytes 1277960 | tf_op jit(solution)/shard_map/ppermute | solution.py:23
  6.7 12.7 %collective-permute-start.1 = (bf16[13,16,1024]{2,1,0:T(8,128)(2,1)}, bf16[13,16,1024]{2,1,0:T(8,128)(2,1)S(1)}, u32[]{:S(2)}, u32[]{:S(2)}) collective-permute-start(bf16[13,16,1024]{2,1,0:T(8,128)(2,1)} %get-tuple-element.31), channel_id=1, source_target_pairs={{0,3},{1,2},{2,1},{3,0},{4,7},{5,6},{6,5},{7,4},{8,11},{9,10},{10,... | collective-permute-start | bytes 1277960 | tf_op jit(solution)/shard_map/ppermute | solution.py:23
  8.6 5.9 %collective-permute-start.2 = (bf16[1,16,1024]{2,1,0:T(8,128)(2,1)}, bf16[1,16,1024]{2,1,0:T(8,128)(2,1)S(1)}, u32[]{:S(2)}, u32[]{:S(2)}) collective-permute-start(bf16[1,16,1024]{2,1,0:T(8,128)(2,1)} %get-tuple-element.32), channel_id=1, source_target_pairs={{8,16},{16,8},{24,32},{32,24},{40,48},{48,40},{56,64},{64,56},{72,... | collective-permute-start | bytes 98312 | tf_op jit(solution)/shard_map/ppermute | solution.py:31
  11.2 19.7 %copy-start = (bf16[6,16,1024]{2,1,0:T(8,128)(2,1)S(1)}, bf16[6,16,1024]{2,1,0:T(8,128)(2,1)}, u32[]{:S(2)}) copy-start(bf16[6,16,1024]{2,1,0:T(8,128)(2,1)} %refs_0_.6) | copy-start | bytes 589828
  11.2 4.4 %collective-permute-start.6 = (bf16[1,16,1024]{2,1,0:T(8,128)(2,1)}, bf16[1,16,1024]{2,1,0:T(8,128)(2,1)S(1)}, u32[]{:S(2)}, u32[]{:S(2)}) collective-permute-start(bf16[1,16,1024]{2,1,0:T(8,128)(2,1)} %get-tuple-element.36), channel_id=1, source_target_pairs={{0,8},{8,0},{1,9},{9,1},{2,10},{10,2},{3,11},{11,3},{4,12},{12,4},... | collective-permute-start | bytes 98312 | tf_op jit(solution)/shard_map/ppermute | solution.py:23
  15.8 10.6 %collective-permute-start.7 = (bf16[14,16,1024]{2,1,0:T(8,128)(2,1)S(1)}, bf16[14,16,1024]{2,1,0:T(8,128)(2,1)S(1)}, u32[]{:S(2)}, u32[]{:S(2)}) collective-permute-start(bf16[14,16,1024]{2,1,0:T(8,128)(2,1)S(1)} %collective-permute-done.5.refs_4_.refs_12_), channel_id=1, source_target_pairs={{0,1},{1,0},{2,3},{3,2},{4,5},{5,4},{6,7},{7,6},{8,9},{9,8},{10,11... | collective-permute-start | bytes 1376264 | tf_op jit(solution)/shard_map/ppermute | solution.py:23
  17.4 6.8 %collective-permute-start.3 = (bf16[7,16,1024]{2,1,0:T(8,128)(2,1)S(1)}, bf16[7,16,1024]{2,1,0:T(8,128)(2,1)S(1)}, u32[]{:S(2)}, u32[]{:S(2)}) collective-permute-start(bf16[7,16,1024]{2,1,0:T(8,128)(2,1)S(1)} %slice.21), channel_id=1, source_target_pairs={{0,3},{1,2},{2,1},{3,0},{4,7},{5,6},{6,5},{7,4},{8,11},{9,10},{10,... | collective-permute-start | bytes 688136 | tf_op jit(solution)/shard_map/ppermute | solution.py:23
  19.4 11.5 %collective-permute-start.11 = (bf16[7,16,1024]{2,1,0:T(8,128)(2,1)S(1)}, bf16[7,16,1024]{2,1,0:T(8,128)(2,1)S(1)}, u32[]{:S(2)}, u32[]{:S(2)}) collective-permute-start(bf16[7,16,1024]{2,1,0:T(8,128)(2,1)S(1)} %slice.24), channel_id=1, source_target_pairs={{0,4},{4,0},{1,5},{5,1},{2,6},{6,2},{3,7},{7,3},{8,12},{12,8},{9,1... | collective-permute-start | bytes 688136 | tf_op jit(solution)/shard_map/ppermute | solution.py:23
  20.8 0.9 %copy-start.1 = (bf16[6,16,1024]{2,1,0:T(8,128)(2,1)S(1)}, bf16[6,16,1024]{2,1,0:T(8,128)(2,1)}, u32[]{:S(2)}) copy-start(bf16[6,16,1024]{2,1,0:T(8,128)(2,1)} %refs_0_.7) | copy-start | bytes 589828
  24.2 6.7 %collective-permute-start.10 = (bf16[6,16,1024]{2,1,0:T(8,128)(2,1)S(1)}, bf16[6,16,1024]{2,1,0:T(8,128)(2,1)S(1)}, u32[]{:S(2)}, u32[]{:S(2)}) collective-permute-start(bf16[6,16,1024]{2,1,0:T(8,128)(2,1)S(1)} %slice.23), channel_id=1, source_target_pairs={{0,4},{4,0},{1,5},{5,1},{2,6},{6,2},{3,7},{7,3},{8,12},{12,8},{9,1... | collective-permute-start | bytes 589832 | tf_op jit(solution)/shard_map/ppermute | solution.py:23
  26.4 8.9 %collective-permute-start.8 = (bf16[7,16,1024]{2,1,0:T(8,128)(2,1)S(1)}, bf16[7,16,1024]{2,1,0:T(8,128)(2,1)S(1)}, u32[]{:S(2)}, u32[]{:S(2)}) collective-permute-start(bf16[7,16,1024]{2,1,0:T(8,128)(2,1)S(1)} %slice.22), channel_id=1, source_target_pairs={{0,3},{1,2},{2,1},{3,0},{4,7},{5,6},{6,5},{7,4},{8,11},{9,10},{10,... | collective-permute-start | bytes 688136 | tf_op jit(solution)/shard_map/ppermute | solution.py:23
  29.6 7.6 %copy-start.2 = (bf16[6,16,1024]{2,1,0:T(8,128)(2,1)S(1)}, bf16[6,16,1024]{2,1,0:T(8,128)(2,1)}, u32[]{:S(2)}) copy-start(bf16[6,16,1024]{2,1,0:T(8,128)(2,1)} %refs_0_.7) | copy-start | bytes 589828
  29.6 7.6 %copy-start.3 = (bf16[3,3,3,128,16]{3,4,2,1,0:T(8,128)(2,1)S(1)}, bf16[3,3,3,128,16]{3,4,2,1,0:T(8,128)(2,1)}, u32[]{:S(2)}) copy-start(bf16[3,3,3,128,16]{3,4,2,1,0:T(8,128)(2,1)} %param.5) | copy-start | bytes 331780
  29.6 7.6 %copy-start.4 = (bf16[16,512]{1,0:T(8,128)(2,1)S(1)}, bf16[16,512]{1,0:T(8,128)(2,1)}, u32[]{:S(2)}) copy-start(bf16[16,512]{1,0:T(8,128)(2,1)} %get-tuple-element.42.refs_17_) | copy-start | bytes 49156
  29.6 5.7 %collective-permute-start.4 = (bf16[6,16,1024]{2,1,0:T(8,128)(2,1)S(1)}, bf16[6,16,1024]{2,1,0:T(8,128)(2,1)S(1)}, u32[]{:S(2)}, u32[]{:S(2)}) collective-permute-start(bf16[6,16,1024]{2,1,0:T(8,128)(2,1)S(1)} %slice.20), channel_id=1, source_target_pairs={{0,1},{1,0},{2,3},{3,2},{4,5},{5,4},{6,7},{7,6},{8,9},{9,8},{10,11... | collective-permute-start | bytes 589832 | tf_op jit(solution)/shard_map/ppermute | solution.py:23
  29.7 5.6 %collective-permute-start.9 = (bf16[6,16,1024]{2,1,0:T(8,128)(2,1)S(1)}, bf16[6,16,1024]{2,1,0:T(8,128)(2,1)S(1)}, u32[]{:S(2)}, u32[]{:S(2)}) collective-permute-start(bf16[6,16,1024]{2,1,0:T(8,128)(2,1)S(1)} %slice.20), channel_id=1, source_target_pairs={{0,4},{4,0},{1,5},{5,1},{2,6},{6,2},{3,7},{7,3},{8,12},{12,8},{9,1... | collective-permute-start | bytes 589832 | tf_op jit(solution)/shard_map/ppermute | solution.py:23
  32.2 4.1 %collective-permute-start.12 = (f32[216,128]{1,0:T(8,128)S(1)}, f32[216,128]{1,0:T(8,128)S(1)}, u32[]{:S(2)}, u32[]{:S(2)}) collective-permute-start(f32[216,128]{1,0:T(8,128)S(1)} %get-tuple-element.45), channel_id=1, source_target_pairs={{0,8},{8,0},{1,9},{9,1},{2,10},{10,2},{3,11},{11,3},{4,12},{12,4},... | collective-permute-start | bytes 331784 | tf_op jit(solution)/shard_map/ppermute | solution.py:23
  36.3 7.5 %collective-permute-start.13 = (f32[216,128]{1,0:T(8,128)S(1)}, f32[216,128]{1,0:T(8,128)S(1)}, u32[]{:S(2)}, u32[]{:S(2)}) collective-permute-start(f32[216,128]{1,0:T(8,128)S(1)} %add.12), channel_id=1, source_target_pairs={{0,16},{16,0},{32,48},{48,32},{1,17},{17,1},{33,49},{49,33},{2,18}... | collective-permute-start | bytes 331784 | tf_op jit(solution)/shard_map/ppermute | solution.py:23
  38.5 9.3 %collective-permute-start.14 = (f32[2,16,1024]{2,1,0:T(8,128)S(1)}, f32[2,16,1024]{2,1,0:T(8,128)S(1)}, u32[]{:S(2)}, u32[]{:S(2)}) collective-permute-start(f32[2,16,1024]{2,1,0:T(8,128)S(1)} %get-tuple-element.49), channel_id=1, source_target_pairs={{8,16},{16,8},{24,32},{32,24},{40,48},{48,40},{56,64},{64,56},{72,... | collective-permute-start | bytes 393224 | tf_op jit(solution)/shard_map/ppermute | solution.py:31
  41.2 6.6 %collective-permute-start.15 = (f32[2,16,1024]{2,1,0:T(8,128)S(1)}, f32[2,16,1024]{2,1,0:T(8,128)S(1)}, u32[]{:S(2)}, u32[]{:S(2)}) collective-permute-start(f32[2,16,1024]{2,1,0:T(8,128)S(1)} %get-tuple-element.50), channel_id=1, source_target_pairs={{0,8},{8,0},{1,9},{9,1},{2,10},{10,2},{3,11},{11,3},{4,12},{12,4},... | collective-permute-start | bytes 393224 | tf_op jit(solution)/shard_map/ppermute | solution.py:23
  43.8 5.9 %collective-permute-start.16 = (bf16[216,128]{1,0:T(8,128)(2,1)S(1)}, bf16[216,128]{1,0:T(8,128)(2,1)S(1)}, u32[]{:S(2)}, u32[]{:S(2)}) collective-permute-start(bf16[216,128]{1,0:T(8,128)(2,1)S(1)} %add_convert_fusion), channel_id=1, source_target_pairs={{0,48},{16,32},{32,16},{48,0},{1,49},{17,33},{33,17},{49,1},{2,50}... | collective-permute-start | bytes 165896 | tf_op jit(solution)/shard_map/ppermute | solution.py:23
  49.7 6.1 %collective-permute-start.17 = (f32[216,128]{1,0:T(8,128)S(1)}, f32[216,128]{1,0:T(8,128)S(1)}, u32[]{:S(2)}, u32[]{:S(2)}) collective-permute-start(f32[216,128]{1,0:T(8,128)S(1)} %convert_add_fusion), channel_id=1, source_target_pairs={{0,64},{64,0},{1,65},{65,1},{2,66},{66,2},{3,67},{67,3},{4,68},{68... | collective-permute-start | bytes 331784 | tf_op jit(solution)/shard_map/ppermute | solution.py:23
  55.9 2.0 %collective-permute-start.18 = (f32[216,128]{1,0:T(8,128)S(1)}, f32[216,128]{1,0:T(8,128)S(1)}, u32[]{:S(2)}, u32[]{:S(2)}) collective-permute-start(f32[216,128]{1,0:T(8,128)S(1)} %add.15.mine), channel_id=1, source_target_pairs={{0,8},{8,0},{1,9},{9,1},{2,10},{10,2},{3,11},{11,3},{4,12},{12,4},... | collective-permute-start | bytes 331784 | tf_op jit(solution)/shard_map/ppermute | solution.py:23

commit v5 on v4

--- a/solution.py
+++ b/solution.py
@@ -275,7 +275,7 @@
         [pltpu.VMEM((432, C), F32), FIELD],
         CONV_FLOPS,
     )
-    terms = after(keep, z2g, k2g, z3g) + swap(send, "core", 1)
+    terms = after(keep, k2g, z3g) + swap(send, "core", 1)
     got = swap(terms, "x", 1)
     inner, outer, w_in = call(
         edges_body,

time: 58.7 us -> 57.6 us (0.981)
  waiting for transfers between devices: 12.2 us -> 10.2 us
  starting transfers between devices: 34.2 us -> 35 us
    ppermute x17, starting transfers between devices: 28.9 us -> 31.2 us  [swap(): lax.ppermute(v, axis, [(i, i ^ bits) for i in range(lax.axis_size(axis))])]
    ppermute x17, waiting for transfers between devices: 12.2 us -> 10.2 us  [swap(): lax.ppermute(v, axis, [(i, i ^ bits) for i in range(lax.axis_size(axis))])]
    ppermute x2, starting transfers between devices: 5.28 us -> 3.8 us  [outer_swap(): return lax.ppermute(v, SPACE, pairs)]
  transfers between devices with their start and end apart: 19 -> 19, of which waited for: 8 -> 8; matrix products, arithmetic and copies ran while one was open for 0% -> 0% of each run, Pallas kernels for 12% -> 13%
where the time goes in v5:
time: 57.6 us; the launch traced here: 57.4 us
  starting transfers between devices  35 us (61%)
  Pallas kernels  10.3 us (18%)
  waiting for transfers between devices  10.2 us (18%)
  local copies, waits for them, and re-layouts  1.02 us (2%)
  between operations  0.77 us (1%)
    ppermute x17, starting transfers between devices, swap(): lax.ppermute(v, axis, [(i, i ^ bits) for i in range(lax.axis_size(axis))])  31.2 us
    pallas_call x7, Pallas kernels, call(): pl.pallas_call(body, out_shape=[jax.ShapeDtypeStruct(s, d) for s, d in ou...  10.3 us
    ppermute x17, waiting for transfers between devices, swap(): lax.ppermute(v, axis, [(i, i ^ bits) for i in range(lax.axis_size(axis))])  10.2 us
    ppermute x2, starting transfers between devices, outer_swap(): return lax.ppermute(v, SPACE, pairs)  3.8 us
  transfers between devices with their start and end apart: 19, of which 8 were waited for; matrix products, arithmetic and copies ran while one was open for 0% of the time, Pallas kernels for 13%

profile of v5, /device:TPU:1, one launch (start us, length us, event | category | flops | bytes accessed | tf_op | source)
XLA Modules:
  0.0 57.4 jit_solution(18271300383671201270)
XLA Ops:
  0.6 2.3 %pack_messages.1 = (bf16[13,16,1024]{2,1,0:T(8,128)(2,1)}, bf16[13,16,1024]{2,1,0:T(8,128)(2,1)}, bf16[14,16,1024]{2,1,0:T(8,128)(2,1)}, bf16[16,512]{1,0:T(8,12...) custom-call(bf16[432,128]{1,0:T(8,128)(2,1)} %bitcast.6, bf16[6,16,1024]{2,1,0:T(8,128)(2,1)} %refs_0_.6, ...), custom_call_target="tpu_custom_call" | custom-call | bytes 1048576 | tf_op jit(solution)/shard_map/pack_messages/pallas_call | solution.py:218
  2.9 2.5 %collective-permute-start.5 = (bf16[14,16,1024]{2,1,0:T(8,128)(2,1)}, bf16[14,16,1024]{2,1,0:T(8,128)(2,1)S(1)}, u32[]{:S(2)}, u32[]{:S(2)}) collective-permute-start(bf16[14,16,1024]{2,1,0:T(8,128)(2,1)} %get-tuple-element.35), channel_id=1, source_target_pairs={{0,4},{4,0},{1,5},{5,1},{2,6},{6,2},{3,7},{7,3},{8,12},{12,8},{9,1... | collective-permute-start | bytes 1376264 | tf_op jit(solution)/shard_map/ppermute | solution.py:23
  5.4 1.3 %collective-permute-start = (bf16[13,16,1024]{2,1,0:T(8,128)(2,1)}, bf16[13,16,1024]{2,1,0:T(8,128)(2,1)S(1)}, u32[]{:S(2)}, u32[]{:S(2)}) collective-permute-start(bf16[13,16,1024]{2,1,0:T(8,128)(2,1)} %get-tuple-element.30), channel_id=1, source_target_pairs={{0,1},{1,0},{2,3},{3,2},{4,5},{5,4},{6,7},{7,6},{8,9},{9,8},{10,11... | collective-permute-start | bytes 1277960 | tf_op jit(solution)/shard_map/ppermute | solution.py:23
  6.7 1.9 %collective-permute-start.1 = (bf16[13,16,1024]{2,1,0:T(8,128)(2,1)}, bf16[13,16,1024]{2,1,0:T(8,128)(2,1)S(1)}, u32[]{:S(2)}, u32[]{:S(2)}) collective-permute-start(bf16[13,16,1024]{2,1,0:T(8,128)(2,1)} %get-tuple-element.31), channel_id=1, source_target_pairs={{0,3},{1,2},{2,1},{3,0},{4,7},{5,6},{6,5},{7,4},{8,11},{9,10},{10,... | collective-permute-start | bytes 1277960 | tf_op jit(solution)/shard_map/ppermute | solution.py:23
  8.6 2.6 %collective-permute-start.2 = (bf16[1,16,1024]{2,1,0:T(8,128)(2,1)}, bf16[1,16,1024]{2,1,0:T(8,128)(2,1)S(1)}, u32[]{:S(2)}, u32[]{:S(2)}) collective-permute-start(bf16[1,16,1024]{2,1,0:T(8,128)(2,1)} %get-tuple-element.32), channel_id=1, source_target_pairs={{8,16},{16,8},{24,32},{32,24},{40,48},{48,40},{56,64},{64,56},{72,... | collective-permute-start | bytes 98312 | tf_op jit(solution)/shard_map/ppermute | solution.py:31
  11.2 3.3 %collective-permute-start.6 = (bf16[1,16,1024]{2,1,0:T(8,128)(2,1)}, bf16[1,16,1024]{2,1,0:T(8,128)(2,1)S(1)}, u32[]{:S(2)}, u32[]{:S(2)}) collective-permute-start(bf16[1,16,1024]{2,1,0:T(8,128)(2,1)} %get-tuple-element.36), channel_id=1, source_target_pairs={{0,8},{8,0},{1,9},{9,1},{2,10},{10,2},{3,11},{11,3},{4,12},{12,4},... | collective-permute-start | bytes 98312 | tf_op jit(solution)/shard_map/ppermute | solution.py:23
  14.5 1.1 %collective-permute-done.6.g_in = bf16[1,16,1024]{2,1,0:T(8,128)(2,1)S(1)} collective-permute-done((bf16[1,16,1024]{2,1,0:T(8,128)(2,1)}, bf16[1,16,1024]{2,1,0:T(8,128)(2,1)S(1)}, u32[]{:S(2)}, u32[]{:S(2)}) %collective-permute-start.6) | collective-permute-done | bytes 32800 | tf_op jit(solution)/shard_map/ppermute | solution.py:23
  15.8 1.5 %collective-permute-start.7 = (bf16[14,16,1024]{2,1,0:T(8,128)(2,1)S(1)}, bf16[14,16,1024]{2,1,0:T(8,128)(2,1)S(1)}, u32[]{:S(2)}, u32[]{:S(2)}) collective-permute-start(bf16[14,16,1024]{2,1,0:T(8,128)(2,1)S(1)} %collective-permute-done.5.refs_4_.refs_12_), channel_id=1, source_target_pairs={{0,1},{1,0},{2,3},{3,2},{4,5},{5,4},{6,7},{7,6},{8,9},{9,8},{10,11... | collective-permute-start | bytes 1376264 | tf_op jit(solution)/shard_map/ppermute | solution.py:23
  17.4 2.0 %collective-permute-start.3 = (bf16[7,16,1024]{2,1,0:T(8,128)(2,1)S(1)}, bf16[7,16,1024]{2,1,0:T(8,128)(2,1)S(1)}, u32[]{:S(2)}, u32[]{:S(2)}) collective-permute-start(bf16[7,16,1024]{2,1,0:T(8,128)(2,1)S(1)} %slice.21), channel_id=1, source_target_pairs={{0,3},{1,2},{2,1},{3,0},{4,7},{5,6},{6,5},{7,4},{8,11},{9,10},{10,... | collective-permute-start | bytes 688136 | tf_op jit(solution)/shard_map/ppermute | solution.py:23
  19.4 1.4 %collective-permute-start.11 = (bf16[7,16,1024]{2,1,0:T(8,128)(2,1)S(1)}, bf16[7,16,1024]{2,1,0:T(8,128)(2,1)S(1)}, u32[]{:S(2)}, u32[]{:S(2)}) collective-permute-start(bf16[7,16,1024]{2,1,0:T(8,128)(2,1)S(1)} %slice.24), channel_id=1, source_target_pairs={{0,4},{4,0},{1,5},{5,1},{2,6},{6,2},{3,7},{7,3},{8,12},{12,8},{9,1... | collective-permute-start | bytes 688136 | tf_op jit(solution)/shard_map/ppermute | solution.py:23
  21.7 1.1 %moved_cotangent.1.refs_8_ = bf16[1152,1024]{1,0:T(8,128)(2,1)S(1)} custom-call(bf16[6,16,1024]{2,1,0:T(8,128)(2,1)S(1)} %copy-done.1, bf16[1,16,1024]{2,1,0:T(8,128)(2,1)S(1)} %collective-permute-done.6.g_in, bf16[1,16,1024]{2,1,0:T(8,128)(2,1)S(1)} %collective-permute-done.2.g_out), custom_call_target="tpu_custom_call" | custom-call | bytes 1048576 | tf_op jit(solution)/shard_map/moved_cotangent/pallas_call | solution.py:218
  22.8 1.3 %collective-permute-done.3.refs_2_ = bf16[7,16,1024]{2,1,0:T(8,128)(2,1)S(1)} collective-permute-done((bf16[7,16,1024]{2,1,0:T(8,128)(2,1)S(1)}, bf16[7,16,1024]{2,1,0:T(8,128)(2,1)S(1)}, u32[]{:S(2)}, u32[]{:S(2)}) %collective-permute-start.3) | collective-permute-done | bytes 229408 | tf_op jit(solution)/shard_map/ppermute | solution.py:23
  26.5 3.2 %collective-permute-start.8 = (bf16[7,16,1024]{2,1,0:T(8,128)(2,1)S(1)}, bf16[7,16,1024]{2,1,0:T(8,128)(2,1)S(1)}, u32[]{:S(2)}, u32[]{:S(2)}) collective-permute-start(bf16[7,16,1024]{2,1,0:T(8,128)(2,1)S(1)} %slice.22), channel_id=1, source_target_pairs={{0,3},{1,2},{2,1},{3,0},{4,7},{5,6},{6,5},{7,4},{8,11},{9,10},{10,... | collective-permute-start | bytes 688136 | tf_op jit(solution)/shard_map/ppermute | solution.py:23
  29.6 1.3 %grad_kernel_terms.1 = (f32[216,128]{1,0:T(8,128)S(1)}, f32[216,128]{1,0:T(8,128)S(1)}) custom-call(bf16[6,16,1024]{2,1,0:T(8,128)(2,1)S(1)} %copy-done, bf16[13,16,1024]{2,1,0:T(8,128)(2,1)S(1)} %collective-permute-done.refs_1_.refs_9_, bf16[7,16,1024]{2,1,0:T(8,128)(2,1)S(1)} %collective-permute-done.3.refs_2_, ...), custom_call_target="tpu_custom_call" | custom-call | flops 679477248 | bytes 1048576 | tf_op jit(solution)/shard_map/grad_kernel_terms/pallas_call | solution.py:218
  30.9 4.2 %collective-permute-start.12 = (f32[216,128]{1,0:T(8,128)S(1)}, f32[216,128]{1,0:T(8,128)S(1)}, u32[]{:S(2)}, u32[]{:S(2)}) collective-permute-start(f32[216,128]{1,0:T(8,128)S(1)} %get-tuple-element.45), channel_id=1, source_target_pairs={{0,8},{8,0},{1,9},{9,1},{2,10},{10,2},{3,11},{11,3},{4,12},{12,4},... | collective-permute-start | bytes 331784 | tf_op jit(solution)/shard_map/ppermute | solution.py:23
  37.1 1.3 %edge_terms.1 = (f32[2,16,1024]{2,1,0:T(8,128)S(1)}, f32[2,16,1024]{2,1,0:T(8,128)S(1)}, bf16[432,128]{1,0:T(8,128)(2,1)S(1)}) custom-call(bf16[6,16,1024]{2,1,0:T(8,128)(2,1)S(1)} %copy-done, bf16[13,16,1024]{2,1,0:T(8,128)(2,1)S(1)} %collective-permute-done.refs_1_.refs_9_, bf16[7,16,1024]{2,1,0:T(8,128)(2,1)S(1)} %collective-permute-done.3.refs_2_, ...), custom_call_target="tpu_custom_call" | custom-call | flops 75497472 | bytes 1048576 | tf_op jit(solution)/shard_map/edge_terms/pallas_call | solution.py:218
  38.4 1.2 %collective-permute-start.14 = (f32[2,16,1024]{2,1,0:T(8,128)S(1)}, f32[2,16,1024]{2,1,0:T(8,128)S(1)}, u32[]{:S(2)}, u32[]{:S(2)}) collective-permute-start(f32[2,16,1024]{2,1,0:T(8,128)S(1)} %get-tuple-element.49), channel_id=1, source_target_pairs={{8,16},{16,8},{24,32},{32,24},{40,48},{48,40},{56,64},{64,56},{72,... | collective-permute-start | bytes 393224 | tf_op jit(solution)/shard_map/ppermute | solution.py:31
  39.6 4.1 %collective-permute-start.15 = (f32[2,16,1024]{2,1,0:T(8,128)S(1)}, f32[2,16,1024]{2,1,0:T(8,128)S(1)}, u32[]{:S(2)}, u32[]{:S(2)}) collective-permute-start(f32[2,16,1024]{2,1,0:T(8,128)S(1)} %get-tuple-element.50), channel_id=1, source_target_pairs={{0,8},{8,0},{1,9},{9,1},{2,10},{10,2},{3,11},{11,3},{4,12},{12,4},... | collective-permute-start | bytes 393224 | tf_op jit(solution)/shard_map/ppermute | solution.py:23
  43.7 1.1 %collective-permute-start.16 = (bf16[216,128]{1,0:T(8,128)(2,1)S(1)}, bf16[216,128]{1,0:T(8,128)(2,1)S(1)}, u32[]{:S(2)}, u32[]{:S(2)}) collective-permute-start(bf16[216,128]{1,0:T(8,128)(2,1)S(1)} %add_convert_fusion), channel_id=1, source_target_pairs={{0,48},{16,32},{32,16},{48,0},{1,49},{17,33},{33,17},{49,1},{2,50}... | collective-permute-start | bytes 165896 | tf_op jit(solution)/shard_map/ppermute | solution.py:23
  44.8 1.5 %output_planes.1 = (bf16[4,16,1024]{2,1,0:T(8,128)(2,1)S(1)}, f32[2,16,1024]{2,1,0:T(8,128)S(1)}) custom-call(bf16[6,16,1024]{2,1,0:T(8,128)(2,1)S(1)} %copy-done, bf16[13,16,1024]{2,1,0:T(8,128)(2,1)S(1)} %collective-permute-done.refs_1_.refs_9_, bf16[7,16,1024]{2,1,0:T(8,128)(2,1)S(1)} %collective-permute-done.3.refs_2_, ...), custom_call_target="tpu_custom_call" | custom-call | flops 679477248 | bytes 1048576 | tf_op jit(solution)/shard_map/output_planes/pallas_call | solution.py:218
  46.3 2.2 %collective-permute-done.16 = bf16[216,128]{1,0:T(8,128)(2,1)S(1)} collective-permute-done((bf16[216,128]{1,0:T(8,128)(2,1)S(1)}, bf16[216,128]{1,0:T(8,128)(2,1)S(1)}, u32[]{:S(2)}, u32[]{:S(2)}) %collective-permute-start.16) | collective-permute-done | bytes 55328 | tf_op jit(solution)/shard_map/ppermute | solution.py:23
  48.6 2.2 %grad_input_planes.1 = (bf16[6,16,1024]{2,1,0:T(8,128)(2,1)}, bf16[6,16,1024]{2,1,0:T(8,128)(2,1)}) custom-call(bf16[6,16,1024]{2,1,0:T(8,128)(2,1)S(1)} %copy-done.2, bf16[13,16,1024]{2,1,0:T(8,128)(2,1)S(1)} %collective-permute-done.refs_1_.refs_9_, bf16[6,16,1024]{2,1,0:T(8,128)(2,1)S(1)} %collective-permute-done.4.refs_10_.refs_2_, ...), custom_call_target="tpu_custom_call" | custom-call | flops 679477248 | bytes 1048576 | tf_op jit(solution)/shard_map/grad_input_planes/pallas_call | solution.py:218
  50.8 2.9 %collective-permute-done.17 = f32[216,128]{1,0:T(8,128)S(1)} collective-permute-done((f32[216,128]{1,0:T(8,128)S(1)}, f32[216,128]{1,0:T(8,128)S(1)}, u32[]{:S(2)}, u32[]{:S(2)}) %collective-permute-start.17) | collective-permute-done | bytes 110624 | tf_op jit(solution)/shard_map/ppermute | solution.py:23
  53.7 2.0 %collective-permute-start.18 = (f32[216,128]{1,0:T(8,128)S(1)}, f32[216,128]{1,0:T(8,128)S(1)}, u32[]{:S(2)}, u32[]{:S(2)}) collective-permute-start(f32[216,128]{1,0:T(8,128)S(1)} %add.15.mine), channel_id=1, source_target_pairs={{0,8},{8,0},{1,9},{9,1},{2,10},{10,2},{3,11},{11,3},{4,12},{12,4},... | collective-permute-start | bytes 331784 | tf_op jit(solution)/shard_map/ppermute | solution.py:23
  (40 shorter events, 7.3 us)
Async XLA Ops:
  2.9 12.9 %collective-permute-start.5 = (bf16[14,16,1024]{2,1,0:T(8,128)(2,1)}, bf16[14,16,1024]{2,1,0:T(8,128)(2,1)S(1)}, u32[]{:S(2)}, u32[]{:S(2)}) collective-permute-start(bf16[14,16,1024]{2,1,0:T(8,128)(2,1)} %get-tuple-element.35), channel_id=1, source_target_pairs={{0,4},{4,0},{1,5},{5,1},{2,6},{6,2},{3,7},{7,3},{8,12},{12,8},{9,1... | collective-permute-start | bytes 1376264 | tf_op jit(solution)/shard_map/ppermute | solution.py:23
  5.4 12.0 %collective-permute-start = (bf16[13,16,1024]{2,1,0:T(8,128)(2,1)}, bf16[13,16,1024]{2,1,0:T(8,128)(2,1)S(1)}, u32[]{:S(2)}, u32[]{:S(2)}) collective-permute-start(bf16[13,16,1024]{2,1,0:T(8,128)(2,1)} %get-tuple-element.30), channel_id=1, source_target_pairs={{0,1},{1,0},{2,3},{3,2},{4,5},{5,4},{6,7},{7,6},{8,9},{9,8},{10,11... | collective-permute-start | bytes 1277960 | tf_op jit(solution)/shard_map/ppermute | solution.py:23
  6.7 12.7 %collective-permute-start.1 = (bf16[13,16,1024]{2,1,0:T(8,128)(2,1)}, bf16[13,16,1024]{2,1,0:T(8,128)(2,1)S(1)}, u32[]{:S(2)}, u32[]{:S(2)}) collective-permute-start(bf16[13,16,1024]{2,1,0:T(8,128)(2,1)} %get-tuple-element.31), channel_id=1, source_target_pairs={{0,3},{1,2},{2,1},{3,0},{4,7},{5,6},{6,5},{7,4},{8,11},{9,10},{10,... | collective-permute-start | bytes 1277960 | tf_op jit(solution)/shard_map/ppermute | solution.py:23
  8.6 5.9 %collective-permute-start.2 = (bf16[1,16,1024]{2,1,0:T(8,128)(2,1)}, bf16[1,16,1024]{2,1,0:T(8,128)(2,1)S(1)}, u32[]{:S(2)}, u32[]{:S(2)}) collective-permute-start(bf16[1,16,1024]{2,1,0:T(8,128)(2,1)} %get-tuple-element.32), channel_id=1, source_target_pairs={{8,16},{16,8},{24,32},{32,24},{40,48},{48,40},{56,64},{64,56},{72,... | collective-permute-start | bytes 98312 | tf_op jit(solution)/shard_map/ppermute | solution.py:31
  11.2 18.4 %copy-start = (bf16[6,16,1024]{2,1,0:T(8,128)(2,1)S(1)}, bf16[6,16,1024]{2,1,0:T(8,128)(2,1)}, u32[]{:S(2)}) copy-start(bf16[6,16,1024]{2,1,0:T(8,128)(2,1)} %refs_0_.6) | copy-start | bytes 589828
  11.2 4.4 %collective-permute-start.6 = (bf16[1,16,1024]{2,1,0:T(8,128)(2,1)}, bf16[1,16,1024]{2,1,0:T(8,128)(2,1)S(1)}, u32[]{:S(2)}, u32[]{:S(2)}) collective-permute-start(bf16[1,16,1024]{2,1,0:T(8,128)(2,1)} %get-tuple-element.36), channel_id=1, source_target_pairs={{0,8},{8,0},{1,9},{9,1},{2,10},{10,2},{3,11},{11,3},{4,12},{12,4},... | collective-permute-start | bytes 98312 | tf_op jit(solution)/shard_map/ppermute | solution.py:23
  15.8 10.6 %collective-permute-start.7 = (bf16[14,16,1024]{2,1,0:T(8,128)(2,1)S(1)}, bf16[14,16,1024]{2,1,0:T(8,128)(2,1)S(1)}, u32[]{:S(2)}, u32[]{:S(2)}) collective-permute-start(bf16[14,16,1024]{2,1,0:T(8,128)(2,1)S(1)} %collective-permute-done.5.refs_4_.refs_12_), channel_id=1, source_target_pairs={{0,1},{1,0},{2,3},{3,2},{4,5},{5,4},{6,7},{7,6},{8,9},{9,8},{10,11... | collective-permute-start | bytes 1376264 | tf_op jit(solution)/shard_map/ppermute | solution.py:23
  17.4 6.8 %collective-permute-start.3 = (bf16[7,16,1024]{2,1,0:T(8,128)(2,1)S(1)}, bf16[7,16,1024]{2,1,0:T(8,128)(2,1)S(1)}, u32[]{:S(2)}, u32[]{:S(2)}) collective-permute-start(bf16[7,16,1024]{2,1,0:T(8,128)(2,1)S(1)} %slice.21), channel_id=1, source_target_pairs={{0,3},{1,2},{2,1},{3,0},{4,7},{5,6},{6,5},{7,4},{8,11},{9,10},{10,... | collective-permute-start | bytes 688136 | tf_op jit(solution)/shard_map/ppermute | solution.py:23
  19.4 10.2 %collective-permute-start.11 = (bf16[7,16,1024]{2,1,0:T(8,128)(2,1)S(1)}, bf16[7,16,1024]{2,1,0:T(8,128)(2,1)S(1)}, u32[]{:S(2)}, u32[]{:S(2)}) collective-permute-start(bf16[7,16,1024]{2,1,0:T(8,128)(2,1)S(1)} %slice.24), channel_id=1, source_target_pairs={{0,4},{4,0},{1,5},{5,1},{2,6},{6,2},{3,7},{7,3},{8,12},{12,8},{9,1... | collective-permute-start | bytes 688136 | tf_op jit(solution)/shard_map/ppermute | solution.py:23
  20.8 0.9 %copy-start.1 = (bf16[6,16,1024]{2,1,0:T(8,128)(2,1)S(1)}, bf16[6,16,1024]{2,1,0:T(8,128)(2,1)}, u32[]{:S(2)}) copy-start(bf16[6,16,1024]{2,1,0:T(8,128)(2,1)} %refs_0_.7) | copy-start | bytes 589828
  24.2 5.5 %collective-permute-start.10 = (bf16[6,16,1024]{2,1,0:T(8,128)(2,1)S(1)}, bf16[6,16,1024]{2,1,0:T(8,128)(2,1)S(1)}, u32[]{:S(2)}, u32[]{:S(2)}) collective-permute-start(bf16[6,16,1024]{2,1,0:T(8,128)(2,1)S(1)} %slice.23), channel_id=1, source_target_pairs={{0,4},{4,0},{1,5},{5,1},{2,6},{6,2},{3,7},{7,3},{8,12},{12,8},{9,1... | collective-permute-start | bytes 589832 | tf_op jit(solution)/shard_map/ppermute | solution.py:23
  24.6 10.6 %collective-permute-start.4 = (bf16[6,16,1024]{2,1,0:T(8,128)(2,1)S(1)}, bf16[6,16,1024]{2,1,0:T(8,128)(2,1)S(1)}, u32[]{:S(2)}, u32[]{:S(2)}) collective-permute-start(bf16[6,16,1024]{2,1,0:T(8,128)(2,1)S(1)} %slice.20), channel_id=1, source_target_pairs={{0,1},{1,0},{2,3},{3,2},{4,5},{5,4},{6,7},{7,6},{8,9},{9,8},{10,11... | collective-permute-start | bytes 589832 | tf_op jit(solution)/shard_map/ppermute | solution.py:23
  25.3 9.8 %collective-permute-start.9 = (bf16[6,16,1024]{2,1,0:T(8,128)(2,1)S(1)}, bf16[6,16,1024]{2,1,0:T(8,128)(2,1)S(1)}, u32[]{:S(2)}, u32[]{:S(2)}) collective-permute-start(bf16[6,16,1024]{2,1,0:T(8,128)(2,1)S(1)} %slice.20), channel_id=1, source_target_pairs={{0,4},{4,0},{1,5},{5,1},{2,6},{6,2},{3,7},{7,3},{8,12},{12,8},{9,1... | collective-permute-start | bytes 589832 | tf_op jit(solution)/shard_map/ppermute | solution.py:23
  26.4 10.7 %copy-start.2 = (bf16[6,16,1024]{2,1,0:T(8,128)(2,1)S(1)}, bf16[6,16,1024]{2,1,0:T(8,128)(2,1)}, u32[]{:S(2)}) copy-start(bf16[6,16,1024]{2,1,0:T(8,128)(2,1)} %refs_0_.7) | copy-start | bytes 589828
  26.4 10.7 %copy-start.3 = (bf16[3,3,3,128,16]{3,4,2,1,0:T(8,128)(2,1)S(1)}, bf16[3,3,3,128,16]{3,4,2,1,0:T(8,128)(2,1)}, u32[]{:S(2)}) copy-start(bf16[3,3,3,128,16]{3,4,2,1,0:T(8,128)(2,1)} %param.5) | copy-start | bytes 331780
  26.5 10.6 %copy-start.4 = (bf16[16,512]{1,0:T(8,128)(2,1)S(1)}, bf16[16,512]{1,0:T(8,128)(2,1)}, u32[]{:S(2)}) copy-start(bf16[16,512]{1,0:T(8,128)(2,1)} %get-tuple-element.42.refs_17_) | copy-start | bytes 49156
  26.5 10.6 %collective-permute-start.8 = (bf16[7,16,1024]{2,1,0:T(8,128)(2,1)S(1)}, bf16[7,16,1024]{2,1,0:T(8,128)(2,1)S(1)}, u32[]{:S(2)}, u32[]{:S(2)}) collective-permute-start(bf16[7,16,1024]{2,1,0:T(8,128)(2,1)S(1)} %slice.22), channel_id=1, source_target_pairs={{0,3},{1,2},{2,1},{3,0},{4,7},{5,6},{6,5},{7,4},{8,11},{9,10},{10,... | collective-permute-start | bytes 688136 | tf_op jit(solution)/shard_map/ppermute | solution.py:23
  30.9 5.2 %collective-permute-start.12 = (f32[216,128]{1,0:T(8,128)S(1)}, f32[216,128]{1,0:T(8,128)S(1)}, u32[]{:S(2)}, u32[]{:S(2)}) collective-permute-start(f32[216,128]{1,0:T(8,128)S(1)} %get-tuple-element.45), channel_id=1, source_target_pairs={{0,8},{8,0},{1,9},{9,1},{2,10},{10,2},{3,11},{11,3},{4,12},{12,4},... | collective-permute-start | bytes 331784 | tf_op jit(solution)/shard_map/ppermute | solution.py:23
  36.1 7.6 %collective-permute-start.13 = (f32[216,128]{1,0:T(8,128)S(1)}, f32[216,128]{1,0:T(8,128)S(1)}, u32[]{:S(2)}, u32[]{:S(2)}) collective-permute-start(f32[216,128]{1,0:T(8,128)S(1)} %add.12), channel_id=1, source_target_pairs={{0,16},{16,0},{32,48},{48,32},{1,17},{17,1},{33,49},{49,33},{2,18}... | collective-permute-start | bytes 331784 | tf_op jit(solution)/shard_map/ppermute | solution.py:23
  38.4 7.9 %collective-permute-start.14 = (f32[2,16,1024]{2,1,0:T(8,128)S(1)}, f32[2,16,1024]{2,1,0:T(8,128)S(1)}, u32[]{:S(2)}, u32[]{:S(2)}) collective-permute-start(f32[2,16,1024]{2,1,0:T(8,128)S(1)} %get-tuple-element.49), channel_id=1, source_target_pairs={{8,16},{16,8},{24,32},{32,24},{40,48},{48,40},{56,64},{64,56},{72,... | collective-permute-start | bytes 393224 | tf_op jit(solution)/shard_map/ppermute | solution.py:31
  39.6 6.7 %collective-permute-start.15 = (f32[2,16,1024]{2,1,0:T(8,128)S(1)}, f32[2,16,1024]{2,1,0:T(8,128)S(1)}, u32[]{:S(2)}, u32[]{:S(2)}) collective-permute-start(f32[2,16,1024]{2,1,0:T(8,128)S(1)} %get-tuple-element.50), channel_id=1, source_target_pairs={{0,8},{8,0},{1,9},{9,1},{2,10},{10,2},{3,11},{11,3},{4,12},{12,4},... | collective-permute-start | bytes 393224 | tf_op jit(solution)/shard_map/ppermute | solution.py:23
  43.7 4.8 %collective-permute-start.16 = (bf16[216,128]{1,0:T(8,128)(2,1)S(1)}, bf16[216,128]{1,0:T(8,128)(2,1)S(1)}, u32[]{:S(2)}, u32[]{:S(2)}) collective-permute-start(bf16[216,128]{1,0:T(8,128)(2,1)S(1)} %add_convert_fusion), channel_id=1, source_target_pairs={{0,48},{16,32},{32,16},{48,0},{1,49},{17,33},{33,17},{49,1},{2,50}... | collective-permute-start | bytes 165896 | tf_op jit(solution)/shard_map/ppermute | solution.py:23
  48.5 5.2 %collective-permute-start.17 = (f32[216,128]{1,0:T(8,128)S(1)}, f32[216,128]{1,0:T(8,128)S(1)}, u32[]{:S(2)}, u32[]{:S(2)}) collective-permute-start(f32[216,128]{1,0:T(8,128)S(1)} %convert_add_fusion), channel_id=1, source_target_pairs={{0,64},{64,0},{1,65},{65,1},{2,66},{66,2},{3,67},{67,3},{4,68},{68... | collective-permute-start | bytes 331784 | tf_op jit(solution)/shard_map/ppermute | solution.py:23
  53.7 3.0 %collective-permute-start.18 = (f32[216,128]{1,0:T(8,128)S(1)}, f32[216,128]{1,0:T(8,128)S(1)}, u32[]{:S(2)}, u32[]{:S(2)}) collective-permute-start(f32[216,128]{1,0:T(8,128)S(1)} %add.15.mine), channel_id=1, source_target_pairs={{0,8},{8,0},{1,9},{9,1},{2,10},{10,2},{3,11},{11,3},{4,12},{12,4},... | collective-permute-start | bytes 331784 | tf_op jit(solution)/shard_map/ppermute | solution.py:23
